TPU v7x, 128 devices: a whole 4x4x4 slice. The times are simulated.
128 devices in a mesh: dp: 16 (over z, x), tensor: 8 (over y, core).
Axes of the slice: x: 4, y: 4, z: 4, core: 2. Of those that a mesh axis runs over, the one named last changes fastest.
Arguments:
- inputs: bfloat16 [16, 512, 1536], P('dp'), may hold values from -6 to 6
- norm_weight: float32 [1536], replicated, may hold values from 0.5 to 1.5
- gate_proj: bfloat16 [1536, 3072], P(None, 'tensor'), may hold values from -0.15625 to 0.15625
- inner_proj: bfloat16 [1536, 3072], P(None, 'tensor'), may hold values from -0.15625 to 0.15625
- state_proj: bfloat16 [1536, 256], replicated, may hold values from -0.15625 to 0.15625
- step_proj: bfloat16 [1536, 48], P(None, 'tensor'), may hold values from -0.15625 to 0.15625
- inner_conv: float32 [4, 3072], P(None, 'tensor'), may hold values from -3 to 3
- inner_conv_bias: float32 [3072], P('tensor'), may hold values from -1.5 to 1.5
- state_conv: float32 [4, 256], replicated, may hold values from -3 to 3
- state_conv_bias: float32 [256], replicated, may hold values from -1.5 to 1.5
- step_bias: float32 [48], P('tensor'), may hold values from -6.9 to -2.25
- decay_log: float32 [48], P('tensor'), may hold values from 0 to 2.77
- skip_weight: float32 [48], P('tensor'), may hold values from 0.5 to 1.5
- gated_norm_weight: float32 [3072], P('tensor'), may hold values from 0.5 to 1.5
- out_proj: bfloat16 [3072, 1536], P('tensor'), may hold values from -0.109375 to 0.109375
- segments: int32 [16, 512], P('dp'), may hold values from 0 to 2, never falling along the last dimension, each value on 1 to 256 neighbouring positions
- cotangent: bfloat16 [16, 512, 1536], P('dp'), may hold values from -6 to 6
Outputs:
- outputs: bfloat16 [16, 512, 1536], P('dp')
- input_grad: float32 [16, 512, 1536], P('dp')
- norm_weight_grad: float32 [1536], replicated
- gate_proj_grad: float32 [1536, 3072], P(None, 'tensor')
- inner_proj_grad: float32 [1536, 3072], P(None, 'tensor')
- state_proj_grad: float32 [1536, 256], replicated
- step_proj_grad: float32 [1536, 48], P(None, 'tensor')
- inner_conv_grad: float32 [4, 3072], P(None, 'tensor')
- inner_conv_bias_grad: float32 [3072], P('tensor')
- state_conv_grad: float32 [4, 256], replicated
- state_conv_bias_grad: float32 [256], replicated
- step_bias_grad: float32 [48], P('tensor')
- decay_log_grad: float32 [48], P('tensor')
- skip_weight_grad: float32 [48], P('tensor')
- gated_norm_weight_grad: float32 [3072], P('tensor')
- out_proj_grad: float32 [3072, 1536], P('tensor')
Inputs may be any that keep to these rules, and one draw needn't show every extreme that they name: `segments`: within a sequence document numbers never fall, each document is a run of 1 to 256 tokens, and one has exactly 256.
All inputs are finite; a program needn't handle non-finite values.
Results may differ from a plain program's by a relative error of at most 0.0081.
Values may be sent and summed in bfloat16 or wider, within the bound.
No kernel may reach another device: no remote copies, remote signals or barrier semaphores. Data moves between devices by JAX's collectives and lax.ppermute only.
A program may use at most 128 MiB of HBM per device.

v0:
```python
import jax
import jax.numpy as jnp
from jax import lax
from jax.sharding import PartitionSpec as P

KERNEL = 4
GROUP = 256
INNER = 3072


epsilon = 1e-05
precise = lax.Precision.HIGHEST


def masked_conv(values, weights, bias, segs):
    length = values.shape[0]
    total = bias[None, :] + weights[0][None, :] * values
    for offset in range(1, KERNEL):
        earlier = jnp.concatenate(
            [jnp.zeros((offset, values.shape[1]), jnp.float32), values[: length - offset]], axis=0
        )
        earlier_seg = jnp.concatenate(
            [jnp.full((offset,), -1, jnp.int32), segs[: length - offset]], axis=0
        )
        same = (earlier_seg == segs).astype(jnp.float32)
        total = total + weights[offset][None, :] * earlier * same[:, None]
    return jax.nn.silu(total)


def group_body(carry, pieces, rate):
    state, previous = carry
    head_in, b_block, c_block, step_block, seg_block = pieces
    block = seg_block.shape[0]
    logs = jnp.cumsum(step_block * rate[None, :], axis=0).T
    row_ids = lax.broadcasted_iota(jnp.int32, (block, block), 0)
    col_ids = lax.broadcasted_iota(jnp.int32, (block, block), 1)
    linked = (seg_block[:, None] == seg_block[None, :]) & (row_ids >= col_ids)
    spread = jnp.where(linked[None, :, :], logs[:, :, None] - logs[:, None, :], 0.0)
    decay = jnp.exp(spread) * linked[None, :, :].astype(jnp.float32)
    scores = jnp.dot(c_block, b_block.T, precision=precise, preferred_element_type=jnp.float32)
    inflow = jnp.transpose(head_in * step_block[:, :, None], (1, 0, 2))
    within = jnp.einsum("hij,hjp->hip", scores[None, :, :] * decay, inflow, precision=precise)
    carried = (seg_block == previous).astype(jnp.float32)
    entering = (
        jnp.einsum("in,hpn->hip", c_block, state, precision=precise)
        * (jnp.exp(logs) * carried[None, :])[:, :, None]
    )
    final_seg = seg_block[block - 1]
    keeping = (seg_block == final_seg).astype(jnp.float32)
    tail = jnp.exp(logs[:, block - 1 :] - logs) * keeping[None, :]
    survive = jnp.exp(logs[:, block - 1]) * (final_seg == previous).astype(jnp.float32)
    new_state = state * survive[:, None, None] + jnp.einsum(
        "hjp,jn->hpn", inflow * tail[:, :, None], b_block, precision=precise
    )
    return ((new_state, final_seg), jnp.transpose(within + entering, (1, 0, 2)))


def state_space(heads_in, bmat, cmat, step, rate, segs):
    length, heads, headdim = heads_in.shape
    blocks = length // GROUP
    pieces = (
        heads_in.reshape(blocks, GROUP, heads, headdim),
        bmat.reshape(blocks, GROUP, -1),
        cmat.reshape(blocks, GROUP, -1),
        step.reshape(blocks, GROUP, heads),
        segs.reshape(blocks, GROUP),
    )

    def advance(carry, piece):
        return group_body(carry, piece, rate)

    start = (jnp.zeros((heads, headdim, bmat.shape[1]), jnp.float32), jnp.array(-1, jnp.int32))
    _, mixed = lax.scan(advance, start, pieces)
    return mixed.reshape(length, heads, headdim)


def contract_rows(left, right):
    return lax.dot_general(
        left, right, (((0,), (0,)), ((), ())), preferred_element_type=jnp.float32
    )


def contract_cols(left, right):
    return lax.dot_general(
        left, right, (((1,), (1,)), ((), ())), preferred_element_type=jnp.float32
    )


def norm_back(values, scale, grad, weight):
    weighted = grad * weight[None, :]
    gain_grad = jnp.sum(grad * values * scale, axis=0)
    result = scale * weighted - values * scale**3 * jnp.mean(
        weighted * values, axis=1, keepdims=True
    )
    return (result, gain_grad)


def per_device(
    inputs,
    norm_weight,
    gate_proj,
    inner_proj,
    state_proj,
    step_proj,
    inner_conv,
    inner_conv_bias,
    state_conv,
    state_conv_bias,
    step_bias,
    decay_log,
    skip_weight,
    gated_norm_weight,
    out_proj,
    segments,
    cotangent,
):
    values = inputs[0].astype(jnp.float32)
    segs = segments[0]
    grad_out = cotangent[0]
    grad_wide = grad_out.astype(jnp.float32)
    length = values.shape[0]
    in_scale = lax.rsqrt(jnp.mean(values * values, axis=1, keepdims=True) + epsilon)
    normed = (values * in_scale * norm_weight[None, :]).astype(jnp.bfloat16)
    gate = jnp.dot(normed, gate_proj, preferred_element_type=jnp.float32)
    inner = jnp.dot(normed, inner_proj, preferred_element_type=jnp.float32)
    states_in = jnp.dot(normed, state_proj, preferred_element_type=jnp.float32)
    step_raw = jnp.dot(normed, step_proj, preferred_element_type=jnp.float32)

    def state_branch(states_in, weights, bias):
        return masked_conv(states_in, weights, bias, segs)

    conv_states, state_pull = jax.vjp(state_branch, states_in, state_conv, state_conv_bias)

    def mixer(gate, inner, conv_states, step_raw, weights, bias, step_bias, decay_log, skip_weight):
        conv_inner = masked_conv(inner, weights, bias, segs)
        heads = decay_log.shape[0]
        half = conv_states.shape[1] // 2
        heads_in = conv_inner.reshape(length, heads, -1)
        step = jax.nn.softplus(step_raw + step_bias[None, :])
        mixed = state_space(
            heads_in, conv_states[:, :half], conv_states[:, half:], step, -jnp.exp(decay_log), segs
        )
        mixed = mixed + skip_weight[None, :, None] * heads_in
        return mixed.reshape(length, -1) * jax.nn.silu(gate)

    gated, mixer_pull = jax.vjp(
        mixer,
        gate,
        inner,
        conv_states,
        step_raw,
        inner_conv,
        inner_conv_bias,
        step_bias,
        decay_log,
        skip_weight,
    )
    squares = lax.psum(jnp.sum(gated * gated, axis=1), "tensor")
    out_scale = lax.rsqrt(squares / INNER + epsilon)[:, None]
    normed_out = (gated * out_scale * gated_norm_weight[None, :]).astype(jnp.bfloat16)
    summed = lax.psum(jnp.dot(normed_out, out_proj, preferred_element_type=jnp.float32), "tensor")
    outputs = (values + summed).astype(jnp.bfloat16)
    out_proj_grad = contract_rows(normed_out, grad_out)
    d_normed_out = contract_cols(grad_out, out_proj)
    weighted = d_normed_out * gated_norm_weight[None, :]
    gated_norm_grad = jnp.sum(d_normed_out * gated * out_scale, axis=0)
    dots = lax.psum(jnp.sum(weighted * gated, axis=1), "tensor")
    d_gated = out_scale * weighted - gated * out_scale**3 * (dots / INNER)[:, None]
    grads = mixer_pull(d_gated)
    state_total = lax.psum(grads[2], "tensor")
    d_states, state_conv_grad, state_conv_bias_grad = state_pull(state_total)
    gate_low = grads[0].astype(jnp.bfloat16)
    inner_low = grads[1].astype(jnp.bfloat16)
    step_low = grads[3].astype(jnp.bfloat16)
    states_low = d_states.astype(jnp.bfloat16)
    gate_proj_grad = contract_rows(normed, gate_low)
    inner_proj_grad = contract_rows(normed, inner_low)
    state_proj_grad = contract_rows(normed, states_low)
    step_proj_grad = contract_rows(normed, step_low)
    total = contract_cols(gate_low, gate_proj)
    total = total + contract_cols(inner_low, inner_proj)
    whole = lax.psum(total + contract_cols(step_low, step_proj), "tensor") + contract_cols(
        states_low, state_proj
    )
    input_grad, norm_grad = norm_back(values, in_scale, whole, norm_weight)
    input_grad = input_grad + grad_wide
    (
        norm_grad,
        gate_proj_grad,
        inner_proj_grad,
        state_proj_grad,
        step_proj_grad,
        inner_conv_grad,
        inner_bias_grad,
        state_conv_grad,
        state_conv_bias_grad,
        step_bias_grad,
        decay_grad,
        skip_grad,
        gated_norm_grad,
        out_proj_grad,
    ) = lax.psum(
        (
            norm_grad,
            gate_proj_grad,
            inner_proj_grad,
            state_proj_grad,
            step_proj_grad,
            grads[4],
            grads[5],
            state_conv_grad,
            state_conv_bias_grad,
            grads[6],
            grads[7],
            grads[8],
            gated_norm_grad,
            out_proj_grad,
        ),
        "dp",
    )
    return (
        outputs[None],
        input_grad[None],
        norm_grad,
        gate_proj_grad,
        inner_proj_grad,
        state_proj_grad,
        step_proj_grad,
        inner_conv_grad,
        inner_bias_grad,
        state_conv_grad,
        state_conv_bias_grad,
        step_bias_grad,
        decay_grad,
        skip_grad,
        gated_norm_grad,
        out_proj_grad,
    )


def solution(mesh):
    placed = (
        P("dp", None, None),
        P(),
        P(None, "tensor"),
        P(None, "tensor"),
        P(),
        P(None, "tensor"),
        P(None, "tensor"),
        P("tensor"),
        P(),
        P(),
        P("tensor"),
        P("tensor"),
        P("tensor"),
        P("tensor"),
        P("tensor", None),
        P("dp", None),
        P("dp", None, None),
    )
    return jax.shard_map(
        per_device,
        mesh=mesh,
        in_specs=placed,
        out_specs=(
            P("dp", None, None),
            P("dp", None, None),
            P(),
            P(None, "tensor"),
            P(None, "tensor"),
            P(),
            P(None, "tensor"),
            P(None, "tensor"),
            P("tensor"),
            P(),
            P(),
            P("tensor"),
            P("tensor"),
            P("tensor"),
            P("tensor"),
            P("tensor", None),
        ),
        check_vma=False,
    )
```

profile of v0, /device:TPU:1, one launch (start us, length us, event | category | flops | bytes accessed | tf_op | source)
XLA Modules:
  0.0 520.9 jit_solution(7215137746628319738)
XLA Ops:
  26.8 74.9 %while.85 = (s32[]{:T(128)}, f32[6,64,128]{2,1,0:T(8,128)S(1)}, s32[]{:T(128)}, f32[2,256,6,64]{1,0,3,2:T(2,128)}, pred[2,6,256,256]{3,2,1,0:T(32,128)(4,1)}, /*...) while((s32[]{:T(128)}, f32[6,64,128]{2,1,0:T(8,128)S(1)}, ...), condition=%wide.region_4.5_spmd.clone.clone, body=%wide.region_1.4_spmd.clone.clone.sunk | while | flops 709458432 | bytes 16738683 | solution.py:73
  38.7 3.2 fusion.273
  43.1 9.0 %dynamic_update_slice.271 = f32[2,256,6,64]{1,0,3,2:T(2,128)} dynamic-update-slice(f32[2,256,6,64]{1,0,3,2:T(2,128)} %get-tuple-element.2272, f32[1,256,6,64]{1,0,3,2:T(1,128)} %copy.235, s32[]{:T(128)} %get-tuple-element.2269, s32[]{:T(128)} %constant.196.clone.1..sunk.1, s32[]{:T(128)} %constant.196.clone.1..sunk.1, s32[]{:T(128)} %constant.196.clone.1..sunk.1) | dynamic-update-slice | bytes 786436 | tf_op jit(solution)/shard_map/jvp()/while/body/jit(dynamic_update_index_in_dim)/dynamic_update_slice | solution.py:73
  76.2 3.2 fusion.273
  80.6 9.0 %dynamic_update_slice.271 = f32[2,256,6,64]{1,0,3,2:T(2,128)} dynamic-update-slice(f32[2,256,6,64]{1,0,3,2:T(2,128)} %get-tuple-element.2272, f32[1,256,6,64]{1,0,3,2:T(1,128)} %copy.235, s32[]{:T(128)} %get-tuple-element.2269, s32[]{:T(128)} %constant.196.clone.1..sunk.1, s32[]{:T(128)} %constant.196.clone.1..sunk.1, s32[]{:T(128)} %constant.196.clone.1..sunk.1) | dynamic-update-slice | bytes 786436 | tf_op jit(solution)/shard_map/jvp()/while/body/jit(dynamic_update_index_in_dim)/dynamic_update_slice | solution.py:73
  106.2 3.8 multiply_reduce_fusion.7
  110.0 13.4 %psum.133 = f32[512]{0:T(512)S(1)} all-reduce(f32[512]{0:T(512)S(1)} %get-tuple-element.1706), channel_id=1, replica_groups=mesh['dp'=16,'tensor'=8] {'tensor'}, use_global_device_ids=true, to_apply=%region_6.7 | all-reduce | flops 512 | bytes 4096 | tf_op jit(solution)/shard_map/psum | solution.py:158
  123.5 4.3 fusion.164
  130.3 14.8 %psum.135 = f32[512]{0:T(512)S(1)} all-reduce(f32[512]{0:T(512)S(1)} %get-tuple-element.1525), channel_id=1, replica_groups=mesh['dp'=16,'tensor'=8] {'tensor'}, use_global_device_ids=true, to_apply=%region_9.10 | all-reduce | flops 512 | bytes 4096 | tf_op jit(solution)/shard_map/psum | solution.py:167
  145.2 4.4 multiply_reduce_fusion.1
  157.6 90.8 %while.84 = (s32[]{:T(128)}, f32[6]{0:T(128)}, f32[6,64,128]{2,1,0:T(8,128)S(1)}, f32[2,256,6,64]{1,0,3,2:T(2,128)}, f32[2,256,128]{2,1,0:T(8,128)}, /*index=5*/...) while((s32[]{:T(128)}, f32[6]{0:T(128)}, ...), condition=%wide.region_22.23_spmd.clone, body=%wide.region_10.22_spmd.clone.sunk | while | flops 1414123008 | bytes 31595924 | solution.py:73
  160.3 4.8 fusion.254
  174.5 7.6 %reduce-window.46 = f32[6,2,128]{2,1,0:T(2,128)S(1)} reduce-window(f32[6,2,128]{2,1,0:T(2,128)S(1)} %reshape.961, f32[]{:T(128)} %constant.197.clone.1..sunk), window={size=1x1x128 pad=0_0x0_0x0_127}, to_apply=%region_17.17 | reduce-window | flops 195072 | bytes 12292 | tf_op jit(solution)/shard_map/reduce-window.18
  186.4 9.0 %dynamic_update_slice.256 = f32[2,256,6,64]{1,0,3,2:T(2,128)} dynamic-update-slice(f32[2,256,6,64]{1,0,3,2:T(2,128)} %get-tuple-element.2379, f32[1,256,6,64]{1,0,3,2:T(1,128)} %copy.229, s32[]{:T(128)S(6)} %sub.235, s32[]{:T(128)} %constant.196.clone.1..sunk, s32[]{:T(128)} %constant.196.clone.1..sunk, s32[]{:T(128)} %constant.196.clone.1..sunk) | dynamic-update-slice | bytes 786436 | tf_op jit(solution)/shard_map/transpose(jvp())/while/body/jit(dynamic_update_index_in_dim)/dynamic_update_slice | solution.py:73
  205.7 4.8 fusion.254
  219.9 7.6 %reduce-window.46 = f32[6,2,128]{2,1,0:T(2,128)S(1)} reduce-window(f32[6,2,128]{2,1,0:T(2,128)S(1)} %reshape.961, f32[]{:T(128)} %constant.197.clone.1..sunk), window={size=1x1x128 pad=0_0x0_0x0_127}, to_apply=%region_17.17 | reduce-window | flops 195072 | bytes 12292 | tf_op jit(solution)/shard_map/reduce-window.18
  231.8 9.0 %dynamic_update_slice.256 = f32[2,256,6,64]{1,0,3,2:T(2,128)} dynamic-update-slice(f32[2,256,6,64]{1,0,3,2:T(2,128)} %get-tuple-element.2379, f32[1,256,6,64]{1,0,3,2:T(1,128)} %copy.229, s32[]{:T(128)S(6)} %sub.235, s32[]{:T(128)} %constant.196.clone.1..sunk, s32[]{:T(128)} %constant.196.clone.1..sunk, s32[]{:T(128)} %constant.196.clone.1..sunk) | dynamic-update-slice | bytes 786436 | tf_op jit(solution)/shard_map/transpose(jvp())/while/body/jit(dynamic_update_index_in_dim)/dynamic_update_slice | solution.py:73
  264.0 3.4 fusion.183
  272.2 80.7 %all-reduce.34.cloned.1.call-done = (f32[512,1536]{1,0:T(8,128)}, f32[512,1536]{1,0:T(8,128)}, f32[512,256]{1,0:T(8,128)}) async-done(((f32[512,1536]{1,0:T(8,128)}, f32[512,1536]{1,0:T(8,128)}, f32[512,256]{1,0:T(8,128)}), (f32[512,1536]{1,0:T(8,128)}, f32[512,1536]{1,0:T(8,128)}, f32[512,256]{1,0:T(8,128)})) %all-reduce.34.cloned.1.call-update) | async-done | bytes 6815760 | tf_op jit(solution)/shard_map/psum | solution.py:161
  360.7 5.1 fusion.137
  365.8 64.6 %all-reduce.26 = (f32[1536]{0:T(1024)}, f32[1536,6]{0,1:T(8,128)}, f32[4,384]{1,0:T(4,128)}, f32[384]{0:T(512)}, f32[4,256]{1,0:T(4,128)}, /*index=5*/f32[256]{0...) all-reduce(f32[1536]{0:T(1024)S(1)} %get-tuple-element.1522, ...), channel_id=1, replica_groups=mesh['dp'=16,'tensor'=8] {'dp'}, use_global_device_ids=true, to_apply=%region_27.28 | all-reduce | flops 14354 | bytes 114832 | tf_op jit(solution)/shard_map/psum | solution.py:202
  430.3 6.6 %fusion.134 = (f32[1,512,1536]{2,1,0:T(8,128)}, bf16[1,512,1536]{2,1,0:T(8,128)(2,1)}) fusion(f32[512,1536]{1,0:T(8,128)} %get-tuple-element.1765, bf16[1,512,1536]{2,1,0:T(8,128)(2,1)} %param.37, bf16[1,512,1536]{2,1,0:T(8,128)(2,1)S(1)} %copy-done.11, f32[512]{0:T(512)S(1)} %broadcast_multiply_fusion.7, f32[512]{0:T(512)S(1)} %copy-done.67, ...), kind=kLoop, calls=%fused_computation.194 | loop fusion | flops 7864320 | bytes 14168064 | tf_op jit(solution)/shard_map/broadcast_in_dim | solution.py:223
  436.9 67.9 %all-reduce.32.cloned.1.call-done = (f32[1536,384]{1,0:T(8,128)}, f32[1536,384]{1,0:T(8,128)}, f32[1536,256]{1,0:T(8,128)}, f32[384,1536]{1,0:T(8,128)}) async-done(((f32[1536,384]{1,0:T(8,128)}, f32[1536,384]{1,0:T(8,128)}, f32[1536,256]{1,0:T(8,128)}, f32[384,1536]{1,0:T(8,128)}), (f32[1536,384]{1,0:T(8,128)}, f32[1536,384]{1,0:T(8,128)}, f32[1536,256]{1,0:T(8,128)}, ...) | async-done | bytes 8650768 | tf_op jit(solution)/shard_map/psum | solution.py:202
  504.8 3.4 copy.372
  (421 shorter events, 163.3 us)
Async XLA Ops:
  7.2 99.0 %copy-start = (bf16[1536,384]{1,0:T(8,128)(2,1)S(1)}, bf16[1536,384]{1,0:T(8,128)(2,1)}, u32[]{:S(2)}) copy-start(bf16[1536,384]{1,0:T(8,128)(2,1)} %param.23) | copy-start | bytes 3538948
  7.2 345.7 %all-reduce.34.cloned.1.call-start = ((), (), s32[]{:S(2)}) async-start(), calls=%async_computation.1 | async-start | bytes 13631488 | tf_op jit(solution)/shard_map/psum | solution.py:161
  19.3 4.6 copy-start.75
  19.3 5.8 %copy-start.35 = (bf16[1536,6]{0,1:T(8,128)(2,1)S(1)}, bf16[1536,6]{0,1:T(8,128)(2,1)}, u32[]{:S(2)}) copy-start(bf16[1536,6]{0,1:T(8,128)(2,1)} %param.26) | copy-start | bytes 55300
  19.3 5.8 %copy-start.73 = (f32[6]{0:T(128)S(1)}, f32[6]{0:T(128)}, u32[]{:S(2)}) copy-start(f32[6]{0:T(128)} %param.31) | copy-start | bytes 76
  31.0 4.8 copy-start.7
  68.4 4.9 copy-start.7
  106.2 39.0 %copy-start.45 = (f32[384]{0:T(512)}, f32[384]{0:T(512)S(1)}, u32[]{:S(2)}) copy-start(f32[384]{0:T(512)S(1)} %mul.1077) | copy-start | bytes 4612
  106.2 17.3 %copy-start.34 = (f32[384]{0:T(512)S(1)}, f32[384]{0:T(512)}, u32[]{:S(2)}) copy-start(f32[384]{0:T(512)} %param.34) | copy-start | bytes 4612
  185.2 14.3 %copy-start.55 = (f32[6]{0:T(128)S(1)}, f32[6]{0:T(128)}, u32[]{:S(2)}) copy-start(f32[6]{0:T(128)} %get-tuple-element.2377) | copy-start | bytes 76 | tf_op jit(solution)/shard_map/transpose(jvp())/while
  185.3 15.1 %copy-start.38 = (f32[2,256,6]{1,2,0:T(8,128)}, f32[2,256,6]{1,2,0:T(8,128)S(1)}, u32[]{:S(2)}) copy-start(f32[2,256,6]{1,2,0:T(8,128)S(1)} %fusion.267) | copy-start | bytes 36868 | tf_op jit(solution)/shard_map/transpose(jvp())/while
  195.4 4.9 copy-start.1
  195.4 4.9 copy-start.6
  195.4 5.0 copy-start.30
  230.5 14.3 %copy-start.55 = (f32[6]{0:T(128)S(1)}, f32[6]{0:T(128)}, u32[]{:S(2)}) copy-start(f32[6]{0:T(128)} %get-tuple-element.2377) | copy-start | bytes 76 | tf_op jit(solution)/shard_map/transpose(jvp())/while
  230.6 15.1 %copy-start.38 = (f32[2,256,6]{1,2,0:T(8,128)}, f32[2,256,6]{1,2,0:T(8,128)S(1)}, u32[]{:S(2)}) copy-start(f32[2,256,6]{1,2,0:T(8,128)S(1)} %fusion.267) | copy-start | bytes 36868 | tf_op jit(solution)/shard_map/transpose(jvp())/while
  240.8 4.9 copy-start.1
  240.8 4.9 copy-start.6
  240.8 4.9 copy-start.30
  264.0 240.8 %all-reduce.32.cloned.1.call-start = ((), (), s32[]{:S(2)}) async-start(), calls=%async_computation | async-start | bytes 17301504 | tf_op jit(solution)/shard_map/psum | solution.py:202
  269.9 83.0 %copy-start.5 = (f32[512,256]{1,0:T(8,128)S(1)}, f32[512,256]{1,0:T(8,128)}, u32[]{:S(2)}) copy-start(f32[512,256]{1,0:T(8,128)} %copy-done.4) | copy-start | bytes 1572868
  360.7 5.1 copy-start.71
  360.7 69.6 %copy-start.11 = (bf16[1,512,1536]{2,1,0:T(8,128)(2,1)S(1)}, bf16[1,512,1536]{2,1,0:T(8,128)(2,1)}, u32[]{:S(2)}) copy-start(bf16[1,512,1536]{2,1,0:T(8,128)(2,1)} %param.21) | copy-start | bytes 4718596
  360.7 69.6 %copy-start.67 = (f32[512]{0:T(512)S(1)}, f32[512]{0:T(512)}, u32[]{:S(2)}) copy-start(f32[512]{0:T(512)} %get-tuple-element.1754) | copy-start | bytes 6148
  (68 other events, 136.3 us)
Sparse Core Ops, SparseCore 0:
  264.1 88.7 all-reduce.33
  358.6 146.2 all-reduce.31
where the time goes:
time: 525 us; the launch traced here: 521 us
  waiting for transfers between devices  149 us (28%)
  local copies, waits for them, and re-layouts  112 us (21%)
  blocking collectives  92.8 us (18%)
  matrix products  81.9 us (16%)
  other arithmetic  67.7 us (13%)
  between operations  14.9 us (3%)
    psum x1, waiting for transfers between devices, per_device(): lax.psum(jnp.dot(normed_out, out_proj, preferred_element_type=jnp.float32...  80.7 us
    psum x1, waiting for transfers between devices, per_device(): lax.psum((norm_grad, gate_proj_grad, inner_proj_grad, state_proj_grad, st...  67.9 us
    psum x1, blocking collectives, per_device(): lax.psum((norm_grad, gate_proj_grad, inner_proj_grad, state_proj_grad, st...  64.6 us
    dynamic_update_slice x18, local copies, waits for them, and re-layouts, state_space(): _, mixed = lax.scan(advance, start, pieces)  50.5 us
    unnamed x136, local copies, waits for them, and re-layouts  22.7 us
    dot_general x6, matrix products, group_body(): jnp.einsum('hij,hjp->hip', scores[None, :, :] * decay, inflow, precision=...  21.5 us
    another operation x29, other arithmetic  19.2 us
    dynamic_update_slice x20, other arithmetic, state_space(): _, mixed = lax.scan(advance, start, pieces)  17.4 us
  transfers between devices with their start and end apart: 2, of which 2 were waited for; matrix products, arithmetic and copies ran while one was open for 4% of the time, Pallas kernels for 0%

commit v1 on v0

v1 whole, which is shorter than its diff:
```python
import functools

import jax
import jax.numpy as jnp
from jax import lax
from jax.experimental import pallas as pl
from jax.experimental.pallas import tpu as pltpu
from jax.sharding import Mesh, PartitionSpec as P

KERNEL = 4
INNER = 3072
EPS = 1e-05
T = 512
GROUP = 256
D = 1536
C = 384
NH = 6
HD = 64
N = 128
BF = jnp.bfloat16
F32 = jnp.float32
EXACT = lax.Precision.HIGHEST
VM = pl.BlockSpec(memory_space=pltpu.VMEM)


def dot(a, b, precision=None):
    return jnp.dot(a, b, preferred_element_type=F32, precision=precision)


def dot_nt(a, b):
    return lax.dot_general(a, b, (((1,), (1,)), ((), ())), preferred_element_type=F32)


def dot_tn(a, b):
    return lax.dot_general(a, b, (((0,), (0,)), ((), ())), preferred_element_type=F32)


def sigmoid(v):
    return 1.0 / (1.0 + jnp.exp(-v))


def softplus(v):
    return jnp.maximum(v, 0.0) + jnp.log1p(jnp.exp(-jnp.abs(v)))


def lane_ids(rows, cols):
    return lax.broadcasted_iota(jnp.int32, (rows, cols), 1)


def row_ids(rows, cols):
    return lax.broadcasted_iota(jnp.int32, (rows, cols), 0)


def conv_masks(seg):
    lanes = lane_ids(1, T)
    out = []
    for k in range(1, KERNEL):
        same = (pltpu.roll(seg, k, 1) == seg) & (lanes >= k)
        out.append(same.astype(F32))
    return out


def conv_forward(v, cols, bias, masks):
    total = bias + cols[0] * v
    for k in range(1, KERNEL):
        total = total + cols[k] * (pltpu.roll(v, k, 1) * masks[k - 1])
    return total


def conv_backward(d_pre, v, cols, masks):
    d_v = cols[0] * d_pre
    taps = [jnp.sum(d_pre * v, axis=1, keepdims=True)]
    for k in range(1, KERNEL):
        back = pltpu.roll(d_pre * masks[k - 1], T - k, 1)
        d_v = d_v + cols[k] * back
        taps.append(jnp.sum(back * v, axis=1, keepdims=True))
    return d_v, taps, jnp.sum(d_pre, axis=1, keepdims=True)


def scan_logs(step, rate, rows_ref, seg):
    upper = (row_ids(GROUP, GROUP) <= lane_ids(GROUP, GROUP)).astype(F32)
    a = step * rate
    logs = jnp.concatenate(
        [dot(a[:, :GROUP], upper, EXACT), dot(a[:, GROUP:], upper, EXACT)], axis=1
    )
    rows_ref[...] = jnp.zeros_like(rows_ref)
    rows_ref[0:8, :] = logs
    rows_ref[8:9, :] = seg.astype(F32)
    return logs, rows_ref[...].T


def link_mask(cols, segf, c):
    sl = slice(c * GROUP, (c + 1) * GROUP)
    same = cols[sl, 8:9] == segf[:, sl]
    later = lane_ids(GROUP, GROUP) >= row_ids(GROUP, GROUP)
    return jnp.where(same & later, 0.0, -1e30)


def state_rows(logs, segf):
    final = segf[:, GROUP - 1 : GROUP]
    tail = jnp.exp(logs[:, GROUP - 1 : GROUP] - logs[:, :GROUP]) * (
        segf[:, :GROUP] == final
    ).astype(F32)
    entry = jnp.exp(logs[:, GROUP:]) * (segf[:, GROUP:] == final).astype(F32)
    return tail, entry


def per_head(rows, width):
    return jnp.concatenate(
        [jnp.broadcast_to(rows[h : h + 1, :], (HD, width)) for h in range(NH)], axis=0
    )


def fwd_kernel(
    x_ref, cot_ref, nw_ref, gp_ref, ip_ref, sp_ref, tp_ref, ic_ref, icb_ref, sc_ref, scb_ref,
    tb_ref, dl_ref, sk_ref, gnw_ref, op_ref, seg_ref,
    normed_ref, gate_ref, inner_ref, pre_ref, mixed_ref, dno_ref, states_ref, spre_ref,
    raw_ref, cols_ref, scols_ref, head_ref, sums_ref,
    tpad, rows_scr, par_scr, u_scr,
):
    def norm_block(r, _):
        sl = pl.ds(r * 32, 32)
        v = x_ref[sl, :].astype(F32)
        scale = lax.rsqrt(jnp.mean(v * v, axis=1, keepdims=True) + EPS)
        normed_ref[sl, :] = (v * scale * nw_ref[...]).astype(BF)
        return 0

    lax.fori_loop(0, T // 32, norm_block, 0)
    par_scr[...] = jnp.zeros_like(par_scr)
    par_scr[0:4, 0:C] = ic_ref[...]
    par_scr[4:5, 0:C] = icb_ref[...]
    par_scr[5:6, 0:C] = gnw_ref[...]
    par_scr[0:4, C : C + 256] = sc_ref[...]
    par_scr[4:5, C : C + 256] = scb_ref[...]
    par_scr[8:9, 0:NH] = tb_ref[...]
    par_scr[9:10, 0:NH] = dl_ref[...]
    par_scr[10:11, 0:NH] = sk_ref[...]
    par = par_scr[...].T
    cols_ref[...] = par[0:C, 0:8]
    scols_ref[...] = par[C : C + 256, 0:8]
    head_ref[...] = par[0:8, :]
    tpad[...] = jnp.zeros_like(tpad)
    tpad[:, 0:NH] = tp_ref[...]
    normed = normed_ref[...]
    gate_ref[...] = dot(normed, gp_ref[...]).T
    inner_ref[...] = dot(normed, ip_ref[...]).T
    states_ref[...] = dot(normed, sp_ref[...]).T
    raw_ref[...] = dot(normed, tpad[...]).T[0:8, :]
    dno_ref[...] = dot_nt(op_ref[...], cot_ref[...])

    seg = seg_ref[...]
    segf = seg.astype(F32)
    masks = conv_masks(seg)
    head = head_ref[...]
    step = softplus(raw_ref[...] + head[:, 8:9])
    rate = -jnp.exp(head[:, 9:10])
    logs, lcols = scan_logs(step, rate, rows_scr, seg)

    sv = states_ref[...]
    spre = conv_forward(
        sv, [scols_ref[:, k : k + 1] for k in range(KERNEL)], scols_ref[:, 4:5], masks
    )
    spre_ref[...] = spre
    cs = spre * sigmoid(spre)
    b_tok = cs[0:N, :].T.astype(BF)
    c_low = cs[N:, :].astype(BF)
    for h in range(NH):
        hs = slice(h * HD, (h + 1) * HD)
        pre = conv_forward(
            inner_ref[hs, :], [cols_ref[hs, k : k + 1] for k in range(KERNEL)],
            cols_ref[hs, 4:5], masks,
        )
        pre_ref[hs, :] = pre
        u_scr[hs, :] = pre * sigmoid(pre)
    tail, entry = state_rows(logs, segf)
    weighted = u_scr[:, 0:GROUP] * per_head(step[:, 0:GROUP] * tail, GROUP)
    state = dot(weighted.astype(BF), b_tok[0:GROUP, :])
    entering = dot(state.astype(BF), c_low[:, GROUP:])
    for c in range(2):
        sl = slice(c * GROUP, (c + 1) * GROUP)
        neg = link_mask(lcols, segf, c)
        scores = dot(b_tok[sl, :], c_low[:, sl])
        for h in range(NH):
            hs = slice(h * HD, (h + 1) * HD)
            decay = jnp.exp((logs[h : h + 1, sl] - lcols[sl, h : h + 1]) + neg)
            m = (scores * decay).astype(BF)
            u = u_scr[hs, sl]
            y = dot((u * step[h : h + 1, sl]).astype(BF), m)
            if c == 1:
                y = y + entering[hs, :] * entry[h : h + 1, :]
            mixed_ref[hs, sl] = y + head[h : h + 1, 10:11] * u
    squares = jnp.zeros((1, T), F32)
    dots = jnp.zeros((1, T), F32)
    for h in range(NH):
        hs = slice(h * HD, (h + 1) * HD)
        g = gate_ref[hs, :]
        gated = mixed_ref[hs, :] * (g * sigmoid(g))
        squares = squares + jnp.sum(gated * gated, axis=0, keepdims=True)
        dots = dots + jnp.sum(dno_ref[hs, :] * cols_ref[hs, 5:6] * gated, axis=0, keepdims=True)
    sums_ref[0:1, :] = squares
    sums_ref[1:2, :] = dots


def sds(shape, dtype):
    return jax.ShapeDtypeStruct(shape, dtype)


def call(kernel, outs, args, scratch=(), smem=0, cost=(0, 0), name=None):
    specs = [pl.BlockSpec(memory_space=pltpu.SMEM)] * smem + [VM] * (len(args) - smem)
    return pl.pallas_call(
        kernel,
        out_shape=outs,
        in_specs=specs,
        out_specs=jax.tree.map(lambda _: VM, outs),
        scratch_shapes=list(scratch),
        compiler_params=pltpu.CompilerParams(vmem_limit_bytes=48 << 20),
        cost_estimate=pl.CostEstimate(flops=cost[0], bytes_accessed=cost[1], transcendentals=0),
        name=name,
    )(*args)


def forward(*args):
    outs = [
        sds((T, D), BF), sds((C, T), F32), sds((C, T), F32), sds((C, T), F32), sds((C, T), F32),
        sds((C, T), F32), sds((256, T), F32), sds((256, T), F32), sds((8, T), F32),
        sds((C, 8), F32), sds((256, 8), F32), sds((8, 128), F32), sds((2, T), F32),
    ]
    scratch = [
        pltpu.VMEM((D, 128), BF), pltpu.VMEM((128, T), F32), pltpu.VMEM((128, 640), F32),
        pltpu.VMEM((C, T), F32),
    ]
    return call(fwd_kernel, outs, args, scratch, 0, (6_000_000_000, 16_000_000), "forward")


def mid_kernel(
    sums_ref, gate_ref, mixed_ref, dno_ref, cols_ref, cot_ref, normed_ref,
    out_grad_ref, gate_grad_ref, no_ref, gate_low_ref, dy_ref, gain_ref,
    no_scr, low_scr,
):
    total = jnp.sum(sums_ref[...], axis=0)
    scale = lax.rsqrt(total[0:1, :] / INNER + EPS)
    slope = scale * scale * scale * (total[1:2, :] / INNER)
    for h in range(NH):
        hs = slice(h * HD, (h + 1) * HD)
        g = gate_ref[hs, :]
        s = sigmoid(g)
        silu = g * s
        mixed = mixed_ref[hs, :]
        gated = mixed * silu
        gain = cols_ref[hs, 5:6]
        normal = gated * scale
        no_scr[hs, :] = (normal * gain).astype(BF)
        dno = dno_ref[hs, :]
        gain_ref[hs, :] = jnp.broadcast_to(jnp.sum(dno * normal, axis=1, keepdims=True), (HD, 8))
        d_gated = scale * (dno * gain) - gated * slope
        low_scr[hs, :] = (d_gated * mixed * (s * (1.0 + g * (1.0 - s)))).astype(BF)
        dy_ref[hs, :] = d_gated * silu
    out_grad_ref[...] = dot(no_scr[...], cot_ref[...]).astype(out_grad_ref.dtype)
    gate_grad_ref[...] = dot(low_scr[...], normed_ref[...]).astype(gate_grad_ref.dtype)
    no_ref[...] = no_scr[...].T
    gate_low_ref[...] = low_scr[...].T


def middle(*args):
    outs = [
        sds((C, D), F32), sds((C, D), BF), sds((T, C), BF), sds((T, C), BF), sds((C, T), F32),
        sds((C, 8), F32),
    ]
    scratch = [pltpu.VMEM((C, T), BF), pltpu.VMEM((C, T), BF)]
    return call(mid_kernel, outs, args, scratch, 0, (3_000_000_000, 12_000_000), "middle")


def bwd_kernel(
    idx_ref, inner_ref, pre_ref, dy_ref, spre_ref, raw_ref, cols_ref, head_ref, seg_ref, normed_ref,
    inner_grad_ref, step_grad_ref, inner_low_ref, step_low_ref, give_ref, keep_ref, small_ref,
    heads_ref,
    rows_scr, u_scr, di_scr, low_scr,
):
    seg = seg_ref[...]
    segf = seg.astype(F32)
    masks = conv_masks(seg)
    head = head_ref[...]
    raw = raw_ref[...] + head[:, 8:9]
    step = softplus(raw)
    rate = -jnp.exp(head[:, 9:10])
    logs, lcols = scan_logs(step, rate, rows_scr, seg)
    spre = spre_ref[...]
    cs = spre * sigmoid(spre)
    b_low = cs[0:N, :].astype(BF)
    c_low = cs[N:, :].astype(BF)
    b_tok = cs[0:N, :].T.astype(BF)
    c_tok = cs[N:, :].T.astype(BF)
    for h in range(NH):
        hs = slice(h * HD, (h + 1) * HD)
        pre = pre_ref[hs, :]
        u_scr[hs, :] = pre * sigmoid(pre)
    tail, entry = state_rows(logs, segf)
    first, second = slice(0, GROUP), slice(GROUP, T)
    weighted = (u_scr[:, first] * per_head(step[:, first] * tail, GROUP)).astype(BF)
    state = dot(weighted, b_tok[first, :]).astype(BF)
    d_entering = (dy_ref[:, second] * per_head(entry, GROUP)).astype(BF)
    d_state = dot(d_entering, c_tok[second, :]).astype(BF)
    entering = dot(state, c_low[:, second])
    into = dot(d_state, b_low[:, first])
    d_c_second = dot_tn(state, d_entering)
    d_b_first = dot_tn(d_state, weighted)
    tri = (row_ids(GROUP, GROUP) >= lane_ids(GROUP, GROUP)).astype(BF)
    before = (row_ids(GROUP, GROUP) < lane_ids(GROUP, GROUP)).astype(F32)
    upto = (row_ids(GROUP, GROUP) < lane_ids(GROUP, GROUP)).astype(F32)
    since = (row_ids(GROUP, GROUP) >= lane_ids(GROUP, GROUP)).astype(F32)
    out_step = []
    out_skip = []
    da_rows = [[None, None] for _ in range(NH)]
    for c in range(2):
        sl = slice(c * GROUP, (c + 1) * GROUP)
        neg = link_mask(lcols, segf, c)
        scores = dot(b_tok[sl, :], c_low[:, sl])
        d_scores = jnp.zeros((GROUP, GROUP), F32)
        for h in range(NH):
            hs = slice(h * HD, (h + 1) * HD)
            decay = jnp.exp((logs[h : h + 1, sl] - lcols[sl, h : h + 1]) + neg)
            m = scores * decay
            dy = dy_ref[hs, sl].astype(BF)
            inflow = (u_scr[hs, sl] * step[h : h + 1, sl]).astype(BF)
            g = dot_tn(inflow, dy)
            d_scores = d_scores + g * decay
            w = dot((g * m).astype(BF), tri)
            da = jnp.sum(w * before, axis=0, keepdims=True)
            da_rows[h][c] = da
            di = dot_nt(dy, m.astype(BF))
            if c == 0:
                di = di + into[hs, :] * tail[h : h + 1, :]
            di_scr[hs, sl] = di
        ds = d_scores.astype(BF)
        d_b = dot_nt(c_low[:, sl], ds)
        d_c = dot(b_low[:, sl], ds)
        if c == 0:
            d_b = d_b + d_b_first
        else:
            d_c = d_c + d_c_second
        give_ref[:, sl] = jnp.where(idx_ref[0] == 0, d_c, d_b).astype(BF)
        keep_ref[:, sl] = jnp.where(idx_ref[0] == 0, d_b, d_c).astype(BF)
    zero = jnp.zeros((1, GROUP), F32)
    q_rows, e_rows = [], []
    for h in range(NH):
        hs = slice(h * HD, (h + 1) * HD)
        q = u_scr[hs, first] * step[h : h + 1, first] * into[hs, :]
        q_rows.append(jnp.sum(q, axis=0, keepdims=True))
        e = dy_ref[hs, second] * entering[hs, :]
        e_rows.append(jnp.sum(e, axis=0, keepdims=True))
    q8 = jnp.concatenate(q_rows + [zero, zero], axis=0) * tail
    e8 = jnp.concatenate(e_rows + [zero, zero], axis=0) * entry
    da0 = jnp.concatenate([da_rows[h][0] for h in range(NH)] + [zero, zero], axis=0)
    da1 = jnp.concatenate([da_rows[h][1] for h in range(NH)] + [zero, zero], axis=0)
    da = jnp.concatenate([da0 + dot(q8, upto, EXACT), da1 + dot(e8, since, EXACT)], axis=1)
    d_steps = []
    for h in range(NH):
        hs = slice(h * HD, (h + 1) * HD)
        pre = pre_ref[hs, :]
        s = sigmoid(pre)
        u = u_scr[hs, :]
        di = di_scr[hs, :]
        dy = dy_ref[hs, :]
        d_steps.append(jnp.sum(di * u, axis=0, keepdims=True))
        out_skip.append(jnp.sum(dy * u, axis=0, keepdims=True))
        d_u = di * step[h : h + 1, :] + head[h : h + 1, 10:11] * dy
        d_pre = d_u * (s * (1.0 + pre * (1.0 - s)))
        d_v, taps, bias = conv_backward(
            d_pre, inner_ref[hs, :], [cols_ref[hs, k : k + 1] for k in range(KERNEL)], masks
        )
        low_scr[hs, :] = d_v.astype(BF)
        for k in range(KERNEL):
            small_ref[hs, k : k + 1] = taps[k]
        small_ref[hs, 4:5] = bias
    zero = jnp.zeros((2, T), F32)
    d_step = jnp.concatenate(d_steps + [zero], axis=0) + da * rate
    skips = jnp.concatenate(out_skip + [zero], axis=0)
    d_raw = d_step * sigmoid(raw)
    heads_ref[...] = jnp.zeros_like(heads_ref)
    heads_ref[:, 0:1] = jnp.sum(d_raw, axis=1, keepdims=True)
    heads_ref[:, 1:2] = jnp.sum(da * step, axis=1, keepdims=True) * rate
    heads_ref[:, 2:3] = jnp.sum(skips, axis=1, keepdims=True)
    rows_scr[...] = jnp.zeros_like(rows_scr)
    rows_scr[0:8, :] = d_raw
    step_low_ref[...] = rows_scr[...].T.astype(BF)
    step_grad_ref[...] = dot(d_raw.astype(BF), normed_ref[...])
    inner_grad_ref[...] = dot(low_scr[...], normed_ref[...]).astype(inner_grad_ref.dtype)
    inner_low_ref[...] = low_scr[...].T


def backward(*args):
    outs = [
        sds((C, D), BF), sds((8, D), F32), sds((T, C), BF), sds((T, 128), BF), sds((128, T), BF),
        sds((128, T), BF), sds((C, 8), F32), sds((8, 128), F32),
    ]
    scratch = [
        pltpu.VMEM((128, T), F32), pltpu.VMEM((C, T), F32), pltpu.VMEM((C, T), F32),
        pltpu.VMEM((C, T), BF),
    ]
    return call(bwd_kernel, outs, args, scratch, 1, (6_000_000_000, 10_000_000), "backward")


def tail_kernel(
    idx_ref, p0_ref, p1_ref, p2_ref, p3_ref, states_ref, spre_ref, scols_ref, seg_ref, normed_ref,
    gate_low_ref, inner_low_ref, step_low_ref, gp_ref, ip_ref, tp_ref, sp_ref, step_grad_ref,
    small_ref, heads_ref, gain_ref,
    give_ref, keep_ref, pack_ref,
    tpad, low_scr, tok_scr, pad_scr,
):
    core = idx_ref[0]
    own = pl.ds(pl.multiple_of(core * 128 + idx_ref[1] * 32, 32), 32)
    masks = conv_masks(seg_ref[...])
    d_cs = (p0_ref[...] + p1_ref[...].astype(F32)) + (
        p2_ref[...].astype(F32) + p3_ref[...].astype(F32)
    )
    pre = spre_ref[own, :]
    s = sigmoid(pre)
    d_pre = d_cs * (s * (1.0 + pre * (1.0 - s)))
    cols = scols_ref[own, :]
    d_v, taps, bias = conv_backward(
        d_pre, states_ref[own, :], [cols[:, k : k + 1] for k in range(KERNEL)], masks
    )
    low_scr[...] = jnp.zeros_like(low_scr)
    low_scr[own, :] = d_v
    tok_scr[...] = low_scr[...].T.astype(BF)
    pack_ref[0:32, :] = dot(d_v.astype(BF), normed_ref[...]).astype(pack_ref.dtype)
    pad_scr[...] = jnp.zeros_like(pad_scr)
    pad_scr[0:C, 0:8] = small_ref[...]
    pad_scr[0:C, 5:6] = gain_ref[:, 0:1]
    for k in range(KERNEL):
        pad_scr[C : C + 32, k : k + 1] = taps[k]
    pad_scr[C : C + 32, 4:5] = bias
    rows = pad_scr[...].T[0:8, :]
    pack_ref[32:40, :] = step_grad_ref[...].astype(pack_ref.dtype)
    pack_ref[40:48, 0:512] = rows.astype(pack_ref.dtype)
    pack_ref[40:48, 512:640] = heads_ref[...].astype(pack_ref.dtype)
    pack_ref[40:48, 640:] = jnp.zeros((8, D - 640), pack_ref.dtype)
    tpad[...] = jnp.zeros_like(tpad)
    tpad[:, 0:NH] = tp_ref[...]
    for ref, half in ((give_ref, 1 - core), (keep_ref, core)):
        tok = pl.ds(pl.multiple_of(half * GROUP, GROUP), GROUP)
        total = dot_nt(gate_low_ref[tok, :], gp_ref[...])
        total = total + dot_nt(inner_low_ref[tok, :], ip_ref[...])
        total = total + dot_nt(tok_scr[tok, :], sp_ref[...])
        total = total + dot_nt(step_low_ref[tok, :], tpad[...])
        ref[...] = total.astype(BF)


def tail(*args):
    outs = [sds((GROUP, D), BF), sds((GROUP, D), BF), sds((48, D), BF)]
    scratch = [
        pltpu.VMEM((D, 128), BF), pltpu.VMEM((256, T), F32), pltpu.VMEM((T, 256), BF),
        pltpu.VMEM((512, 128), F32),
    ]
    return call(tail_kernel, outs, args, scratch, 1, (3_500_000_000, 10_000_000), "tail")


def product_kernel(idx_ref, no_ref, op_ref, give_ref, keep_ref):
    core = idx_ref[0]
    for ref, half in ((give_ref, 1 - core), (keep_ref, core)):
        tok = pl.ds(pl.multiple_of(half * GROUP, GROUP), GROUP)
        ref[...] = dot(no_ref[tok, :], op_ref[...]).astype(BF)


def product(*args):
    outs = [sds((GROUP, D), BF), sds((GROUP, D), BF)]
    return call(product_kernel, outs, args, (), 1, (1_500_000_000, 4_000_000), "product")


def fold_kernel(idx_ref, keep_ref, got_ref, own_ref, *send_refs):
    rows = own_ref.shape[0]
    for k in range(4):
        sl = pl.ds(pl.multiple_of(lax.rem(idx_ref[1] + k, 4) * rows, rows), rows)
        v = keep_ref[sl, :].astype(F32) + got_ref[sl, :].astype(F32)
        if k == 0:
            own_ref[...] = v
        else:
            send_refs[k - 1][...] = v.astype(BF)


def scatter(idx, give, keep):
    got = lax.ppermute(give, "core", [(0, 1), (1, 0)])
    rows, width = keep.shape[0] // 4, keep.shape[1]
    outs = [sds((rows, width), F32)] + [sds((rows, width), BF)] * 3
    own, *sends = call(fold_kernel, outs, (idx, keep, got), (), 1, (2_000_000, 2_000_000), "fold")
    return [own] + [turn(send, "y", k + 1) for k, send in enumerate(sends)]


def turn(v, axis, by):
    return lax.ppermute(v, axis, [(i, (i + by) % 4) for i in range(4)])


def join_kernel(idx_ref, *refs):
    out_ref = refs[4]
    rows = refs[0].shape[0]
    for k in range(4):
        slot = lax.rem(idx_ref[1] + 4 - k, 4)
        out_ref[pl.ds(pl.multiple_of(slot * rows, rows), rows), :] = refs[k][...]


def finish_kernel(idx_ref, mine_ref, other_ref, out_ref):
    rows = mine_ref.shape[0]
    core = idx_ref[0]
    out_ref[pl.ds(pl.multiple_of(core * rows, rows), rows), :] = mine_ref[...].astype(out_ref.dtype)
    out_ref[pl.ds(pl.multiple_of((1 - core) * rows, rows), rows), :] = other_ref[...].astype(
        out_ref.dtype
    )


def gather(idx, chunk, dtype):
    rows, width = chunk.shape
    pieces = [chunk] + [turn(chunk, "y", k) for k in range(1, 4)]
    half = call(join_kernel, sds((4 * rows, width), BF), (idx, *pieces), (), 1, (0, 2_000_000), "join")
    other = lax.ppermute(half, "core", [(0, 1), (1, 0)])
    return call(
        finish_kernel, sds((8 * rows, width), dtype), (idx, half, other), (), 1, (0, 4_000_000), "finish"
    )


def input_kernel(p0, p1, p2, p3, x_ref, cot_ref, nw_ref, ig_ref, norm_ref):
    d_normed = (p0[...] + p1[...].astype(F32)) + (p2[...].astype(F32) + p3[...].astype(F32))
    v = x_ref[...].astype(F32)
    scale = lax.rsqrt(jnp.mean(v * v, axis=1, keepdims=True) + EPS)
    weighted = d_normed * nw_ref[...]
    grad = scale * weighted - v * (
        scale * scale * scale * jnp.mean(weighted * v, axis=1, keepdims=True)
    )
    ig_ref[...] = (cot_ref[...].astype(F32) + grad).astype(BF)
    norm_ref[...] = jnp.broadcast_to(
        jnp.sum(d_normed * v * scale, axis=0, keepdims=True), norm_ref.shape
    ).astype(BF)


def output_kernel(p0, p1, p2, p3, x_ref, out_ref):
    total = (p0[...] + p1[...].astype(F32)) + (p2[...].astype(F32) + p3[...].astype(F32))
    out_ref[...] = (x_ref[...].astype(F32) + total).astype(BF)


def order_kernel(idx_ref, *refs, place):
    out_ref, scr = refs[4], refs[5]
    for k in range(4):
        scr[lax.rem(idx_ref[place] + 4 - k, 4)] = refs[k][...].astype(F32)
    out_ref[...] = ((scr[0] + scr[1]) + (scr[2] + scr[3])).astype(out_ref.dtype)


def ring_sum(idx, v, axis, place, dtype):
    pieces = [v] + [turn(v, axis, k) for k in range(1, 4)]
    return call(
        functools.partial(order_kernel, place=place), sds(v.shape, dtype), (idx, *pieces),
        [pltpu.VMEM((4,) + v.shape, F32)], 1, (0, 1_000_000), "ring",
    )


def per_device(
    inputs, norm_weight, gate_proj, inner_proj, state_proj, step_proj, inner_conv,
    inner_conv_bias, state_conv, state_conv_bias, step_bias, decay_log, skip_weight,
    gated_norm_weight, out_proj, segments, cotangent,
):
    x, cot = inputs[0], cotangent[0]
    core, y = lax.axis_index("core"), lax.axis_index("y")
    idx = jnp.stack([core, y, lax.axis_index("x"), lax.axis_index("z")]).astype(jnp.int32)
    row = lambda v: v.reshape(1, -1)
    nw = row(norm_weight)
    (normed, gate, inner, pre, mixed, dno, states, spre, raw, cols, scols, head, sums) = forward(
        x, cot, nw, gate_proj, inner_proj, state_proj, step_proj, inner_conv,
        row(inner_conv_bias), state_conv, row(state_conv_bias), row(step_bias), row(decay_log),
        row(skip_weight), row(gated_norm_weight), out_proj, segments,
    )
    tensor, dp = ("y", "core"), ("z", "x")
    sums = lax.all_to_all(jnp.broadcast_to(sums[None], (8, 2, T)), tensor, 0, 0, tiled=True)
    out_grad, gate_grad, no, gate_low, dy, gain = middle(
        sums, gate, mixed, dno, cols, cot, normed
    )
    out_grad = lax.psum(out_grad, dp)

    def dp_scatter(v):
        parts = lax.all_to_all(v.reshape(16, C // 16, D), dp, 0, 0, tiled=True)
        return jnp.sum(parts.astype(F32), axis=0).astype(BF)

    gate_part = dp_scatter(gate_grad)
    inner_grad, step_grad, inner_low, step_low, give, keep, small, heads = backward(
        idx, inner, pre, dy, spre, raw, cols, head, segments, normed
    )
    inner_part = dp_scatter(inner_grad)
    pieces = scatter(idx, give, keep)
    give, keep, pack = tail(
        idx, *pieces, states, spre, scols, segments, normed, gate_low, inner_low, step_low,
        gate_proj, inner_proj, step_proj, state_proj, step_grad, small, heads, gain,
    )
    pieces = scatter(idx, give, keep)
    start = core * GROUP + y * 64
    x_part = lax.dynamic_slice_in_dim(x, start, 64)
    cot_part = lax.dynamic_slice_in_dim(cot, start, 64)
    ig_part, norm_part = call(
        input_kernel, [sds((64, D), BF), sds((8, D), BF)], (*pieces, x_part, cot_part, nw), (), 0,
        (2_000_000, 1_000_000), "input_part",
    )
    pieces = scatter(idx, *product(idx, no, out_proj))
    out_part = call(
        output_kernel, sds((64, D), BF), (*pieces, x_part), (), 0, (1_000_000, 1_000_000), "out_part"
    )
    outputs = gather(idx, out_part, BF)
    input_grad = gather(idx, ig_part, F32)
    pack = jnp.concatenate([pack, norm_part], axis=0)
    pack = ring_sum(idx, ring_sum(idx, pack, "x", 2, BF), "z", 3, F32)
    ends = jnp.concatenate([pack[0:32], pack[40:48], pack[48:56]], axis=0).astype(BF)
    ends = gather(idx, ends, F32).reshape(8, 48, D)
    own = jnp.stack([gate_part, inner_part])
    whole = lax.all_to_all(
        jnp.broadcast_to(own[None], (16, 2, C // 16, D)), dp, 0, 0, tiled=True
    )
    gate_grad = whole[:, 0].reshape(C, D).T.astype(F32)
    inner_grad = whole[:, 1].reshape(C, D).T.astype(F32)
    state_grad = ends[:, 0:32].reshape(256, D).T
    state_small = ends[:, 32:40, C : C + 32].transpose(1, 0, 2).reshape(8, 256)
    norm_grad = jnp.sum(ends[:, 40], axis=0)
    return (
        outputs[None], input_grad[None], norm_grad, gate_grad, inner_grad, state_grad,
        pack[32 : 32 + NH].T, pack[40:44, 0:C], pack[44, 0:C], state_small[0:4], state_small[4],
        pack[40 : 40 + NH, 512], pack[40 : 40 + NH, 513], pack[40 : 40 + NH, 514], pack[45, 0:C],
        out_grad,
    )


def solution(mesh):
    small = Mesh(mesh.devices.reshape(4, 4, 4, 2), ("z", "x", "y", "core"))
    dp, tp = ("z", "x"), ("y", "core")
    placed = (
        P(dp, None, None), P(), P(None, tp), P(None, tp), P(), P(None, tp), P(None, tp), P(tp),
        P(), P(), P(tp), P(tp), P(tp), P(tp), P(tp, None), P(dp, None), P(dp, None, None),
    )
    out = (
        P(dp, None, None), P(dp, None, None), P(), P(None, tp), P(None, tp), P(), P(None, tp),
        P(None, tp), P(tp), P(), P(), P(tp), P(tp), P(tp), P(tp), P(tp, None),
    )
    return jax.shard_map(per_device, mesh=small, in_specs=placed, out_specs=out, check_vma=False)
```

time: 525 us -> 283 us (0.54)
  blocking collectives: 92.8 us -> 10.5 us
  matrix products: 81.9 us -> 0 us
  local copies, waits for them, and re-layouts: 112 us -> 45 us
  other arithmetic: 67.7 us -> 6.49 us
  starting transfers between devices: 0.08 us -> 53.8 us
  Pallas kernels: 0 us -> 42.9 us
  waiting for transfers between devices: 149 us -> 108 us
    psum x3 -> x0, blocking collectives: 92.8 us -> none  [the longest x1 64.6 us: per_device(): lax.psum((norm_grad, gate_proj_grad, inner_proj_grad, state_proj_grad, st...]
    psum x2 -> x1, waiting for transfers between devices: 149 us -> 61.3 us  [per_device(): out_grad = lax.psum(out_grad, dp)]
    dot_general x39 -> x0, matrix products: 81.9 us -> none  [the longest x6 21.5 us: group_body(): jnp.einsum('hij,hjp->hip', scores[None, :, :] * decay, inflow, precision=...]
    dynamic_update_slice x18 -> x0, local copies, waits for them, and re-layouts: 50.5 us -> none  [state_space(): _, mixed = lax.scan(advance, start, pieces)]
    ppermute x0 -> x30, waiting for transfers between devices: none -> 45.2 us  [the longest x24 44.2 us: turn(): return lax.ppermute(v, axis, [(i, (i + by) % 4) for i in range(4)])]
    pallas_call x0 -> x18, Pallas kernels: none -> 42.9 us  [call(): pl.pallas_call(kernel, out_shape=outs, in_specs=specs, out_specs=jax.tree...]
    ppermute x0 -> x30, starting transfers between devices: none -> 33.4 us  [the longest x24 26.9 us: turn(): return lax.ppermute(v, axis, [(i, (i + by) % 4) for i in range(4)])]
    all_to_all x0 -> x3, starting transfers between devices: none -> 20.4 us  [the longest x2 13.3 us: dp_scatter(): parts = lax.all_to_all(v.reshape(16, C // 16, D), dp, 0, 0, tiled=True)]
  transfers between devices with their start and end apart: 2 -> 34, of which waited for: 2 -> 15; matrix products, arithmetic and copies ran while one was open for 4% -> 9% of each run, Pallas kernels for 0% -> 10%
where the time goes in v1:
time: 283 us; the launch traced here: 281 us
  waiting for transfers between devices  108 us (38%)
  starting transfers between devices  53.8 us (19%)
  local copies, waits for them, and re-layouts  45 us (16%)
  Pallas kernels  42.9 us (15%)
  between operations  14.6 us (5%)
  blocking collectives  10.5 us (4%)
  other arithmetic  6.49 us (2%)
    psum x1, waiting for transfers between devices, per_device(): out_grad = lax.psum(out_grad, dp)  61.3 us
    ppermute x24, waiting for transfers between devices, turn(): return lax.ppermute(v, axis, [(i, (i + by) % 4) for i in range(4)])  44.2 us
    pallas_call x18, Pallas kernels, call(): pl.pallas_call(kernel, out_shape=outs, in_specs=specs, out_specs=jax.tree...  42.9 us
    unnamed x96, local copies, waits for them, and re-layouts  32.3 us
    ppermute x24, starting transfers between devices, turn(): return lax.ppermute(v, axis, [(i, (i + by) % 4) for i in range(4)])  26.9 us
    all_to_all x2, starting transfers between devices, dp_scatter(): parts = lax.all_to_all(v.reshape(16, C // 16, D), dp, 0, 0, tiled=True)  13.3 us
    all_to_all x1, blocking collectives, per_device(): lax.all_to_all(jnp.broadcast_to(sums[None], (8, 2, T)), tensor, 0, 0, til...  10.5 us
    all_to_all x1, starting transfers between devices, per_device(): lax.all_to_all(jnp.broadcast_to(own[None], (16, 2, C // 16, D)), dp, 0, 0...  7.06 us
  transfers between devices with their start and end apart: 34, of which 15 were waited for; matrix products, arithmetic and copies ran while one was open for 9% of the time, Pallas kernels for 10%

profile of v1, /device:TPU:1, one launch (start us, length us, event | category | flops | bytes accessed | tf_op | source)
XLA Modules:
  0.0 281.3 jit_solution(2243597873594385681)
XLA Ops:
  15.0 10.2 %forward.1 = (bf16[512,1536]{1,0:T(8,128)(2,1)}, f32[384,512]{1,0:T(8,128)S(1)}, f32[384,512]{1,0:T(8,128)S(1)}, f32[384,512]{1,0:T(8,128)S(1)}, f32[384,512]{1,...) custom-call(bf16[512,1536]{1,0:T(8,128)(2,1)} %bitcast.54, ...), custom_call_target="tpu_custom_call" | custom-call | flops 6000000000 | bytes 16000000 | tf_op jit(solution)/shard_map/forward/pallas_call | solution.py:210
  28.1 10.5 %all_to_all.20.sums_ref = f32[8,2,512]{2,1,0:T(2,128)S(1)} all-to-all(f32[8,2,512]{2,1,0:T(2,128)S(1)} %broadcast_in_dim.8), channel_id=1, replica_groups=mesh['z'=4,'x'=4,'y'=4,'core'=2] {'y','core'}, dimensions={0} | all-to-all | bytes 65536 | tf_op jit(solution)/shard_map/all_to_all | solution.py:570
  38.6 5.0 %middle.1 = (f32[384,1536]{1,0:T(8,128)}, bf16[384,1536]{1,0:T(8,128)(2,1)}, bf16[512,384]{1,0:T(8,128)(2,1)S(1)}, bf16[512,384]{1,0:T(8,128)(2,1)S(1)}, f32[384,512]{1,0:T(8,128)S(1)}, /*index=5*/f32[384,8]{1,0:T(8,128)S(1)}) custom-call(f32[8,2,512]{2,1,0:T(2,128)S(1)} %all_to_all.20.sums_ref, f32[384,512]{1,0:T(8,128)S(1)} %get-tuple-element.63.gate_ref, ...), custom_call_target="tpu_custom_call" | custom-call | flops 3000000000 | bytes 12000000 | tf_op jit(solution)/shard_map/middle/pallas_call | solution.py:210
  45.1 7.8 %all-to-all-start.1 = ((bf16[16,24,1536]{2,1,0:T(8,128)(2,1)}), bf16[16,24,1536]{2,1,0:T(8,128)(2,1)}, u32[]{:S(2)}, u32[]{:S(2)}) async-start(bf16[16,24,1536]{2,1,0:T(8,128)(2,1)} %bitcast.15), calls=%async_computation.1 | async-start | bytes 2359296 | tf_op jit(solution)/shard_map/all_to_all | solution.py:577
  54.2 7.6 %backward.1 = (bf16[384,1536]{1,0:T(8,128)(2,1)}, f32[8,1536]{1,0:T(8,128)S(1)}, bf16[512,384]{1,0:T(8,128)(2,1)S(1)}, bf16[512,128]{1,0:T(8,128)(2,1)S(1)}, bf1...) custom-call(s32[4]{0:T(128)S(1)} %pad_add_fusion.idx_ref, ...), custom_call_target="tpu_custom_call" | custom-call | flops 6000000000 | bytes 10000000 | tf_op jit(solution)/shard_map/backward/pallas_call | solution.py:210
  70.3 5.5 %all-to-all-start.2 = ((bf16[16,24,1536]{2,1,0:T(8,128)(2,1)}), bf16[16,24,1536]{2,1,0:T(8,128)(2,1)}, u32[]{:S(2)}, u32[]{:S(2)}) async-start(bf16[16,24,1536]{2,1,0:T(8,128)(2,1)} %bitcast.17), calls=%async_computation.2 | async-start | bytes 2359296 | tf_op jit(solution)/shard_map/all_to_all | solution.py:577
  81.7 6.0 %tail.1 = (bf16[256,1536]{1,0:T(8,128)(2,1)}, bf16[256,1536]{1,0:T(8,128)(2,1)S(1)}, bf16[48,1536]{1,0:T(8,128)(2,1)S(1)}) custom-call(s32[4]{0:T(128)S(1)} %pad_add_fusion.idx_ref, f32[32,512]{1,0:T(8,128)S(1)} %get-tuple-element.83.p0_ref, bf16[32,512]{1,0:T(8,128)(2,1)S(1)} %collective-permute-done.9.p1_ref, ...), custom_call_target="tpu_custom_call" | custom-call | flops 3500000000 | bytes 10000000 | tf_op jit(solution)/shard_map/tail/pallas_call | solution.py:210
  91.3 2.2 product.1
  106.2 7.1 %all-to-all-start.3 = ((bf16[16,2,24,1536]{3,2,1,0:T(8,128)(2,1)}), bf16[16,2,24,1536]{3,2,1,0:T(8,128)(2,1)}, u32[]{:S(2)}, u32[]{:S(2)}) async-start(bf16[16,2,24,1536]{3,2,1,0:T(8,128)(2,1)} %broadcast_in_dim.21), calls=%async_computation.3 | async-start | bytes 4718592 | tf_op jit(solution)/shard_map/all_to_all | solution.py:609
  117.6 2.6 collective-permute-start.22
  125.7 3.6 %collective-permute-start.6 = (bf16[64,1536]{1,0:T(8,128)(2,1)S(1)}, bf16[64,1536]{1,0:T(8,128)(2,1)S(1)}, u32[]{:S(2)}, u32[]{:S(2)}) collective-permute-start(bf16[64,1536]{1,0:T(8,128)(2,1)S(1)} %out_part.1.refs_0_), channel_id=1, source_target_pairs={{0,6},{2,0},{4,2},{6,4},{1,7},{3,1},{5,3},{7,5},{8,14},{10,8},{12,... | collective-permute-start | bytes 589832 | tf_op jit(solution)/shard_map/ppermute | solution.py:490
  129.3 16.8 %collective-permute-done.22.refs_3_ = bf16[56,1536]{1,0:T(8,128)(2,1)S(1)} collective-permute-done((bf16[56,1536]{1,0:T(8,128)(2,1)S(1)}, bf16[56,1536]{1,0:T(8,128)(2,1)S(1)}, u32[]{:S(2)}, u32[]{:S(2)}) %collective-permute-start.22) | collective-permute-done | bytes 172064 | tf_op jit(solution)/shard_map/ppermute | solution.py:490
  148.3 3.7 %collective-permute-done.20.refs_1_ = bf16[56,1536]{1,0:T(8,128)(2,1)S(1)} collective-permute-done((bf16[56,1536]{1,0:T(8,128)(2,1)S(1)}, bf16[56,1536]{1,0:T(8,128)(2,1)S(1)}, u32[]{:S(2)}, u32[]{:S(2)}) %collective-permute-start.20) | collective-permute-done | bytes 172064 | tf_op jit(solution)/shard_map/ppermute | solution.py:490
  158.2 3.0 %collective-permute-done.24.refs_2_ = bf16[56,1536]{1,0:T(8,128)(2,1)S(1)} collective-permute-done((bf16[56,1536]{1,0:T(8,128)(2,1)S(1)}, bf16[56,1536]{1,0:T(8,128)(2,1)S(1)}, u32[]{:S(2)}, u32[]{:S(2)}) %collective-permute-start.24) | collective-permute-done | bytes 172064 | tf_op jit(solution)/shard_map/ppermute | solution.py:490
  161.2 5.2 %collective-permute-done.23.refs_1_ = bf16[56,1536]{1,0:T(8,128)(2,1)S(1)} collective-permute-done((bf16[56,1536]{1,0:T(8,128)(2,1)S(1)}, bf16[56,1536]{1,0:T(8,128)(2,1)S(1)}, u32[]{:S(2)}, u32[]{:S(2)}) %collective-permute-start.23) | collective-permute-done | bytes 172064 | tf_op jit(solution)/shard_map/ppermute | solution.py:490
  168.9 2.7 collective-permute-start.28
  173.9 2.3 collective-permute-start.7
  176.2 3.6 %collective-permute-done.16.refs_1_ = bf16[64,1536]{1,0:T(8,128)(2,1)S(1)} collective-permute-done((bf16[64,1536]{1,0:T(8,128)(2,1)S(1)}, bf16[64,1536]{1,0:T(8,128)(2,1)S(1)}, u32[]{:S(2)}, u32[]{:S(2)}) %collective-permute-start.16) | collective-permute-done | bytes 196640 | tf_op jit(solution)/shard_map/ppermute | solution.py:490
  181.4 3.9 %collective-permute-done.26.refs_1_ = bf16[48,1536]{1,0:T(8,128)(2,1)} collective-permute-done((bf16[48,1536]{1,0:T(8,128)(2,1)}, bf16[48,1536]{1,0:T(8,128)(2,1)}, u32[]{:S(2)}, u32[]{:S(2)}) %collective-permute-start.26) | collective-permute-done | bytes 147488 | tf_op jit(solution)/shard_map/ppermute | solution.py:490
  191.4 2.4 finish.4
  195.9 3.0 %copy.55 = f32[1536,256]{1,0:T(8,128)} copy(f32[1536,256]{0,1:T(8,128)} %bitcast.49) | data formatting | bytes 3145728
  205.0 3.0 %copy.54 = f32[1536,384]{1,0:T(8,128)} copy(f32[1536,384]{0,1:T(8,128)} %get-tuple-element.163) | data formatting | bytes 4718592
  209.9 61.3 %all-reduce.2.cloned.1.call-done = f32[384,1536]{1,0:T(8,128)} async-done(((f32[384,1536]{1,0:T(8,128)}), f32[384,1536]{1,0:T(8,128)}) %all-reduce.2.cloned.1.call-update) | async-done | bytes 2359312 | tf_op jit(solution)/shard_map/psum | solution.py:574
  271.2 3.2 %copy.60 = f32[384,1536]{1,0:T(8,128)} copy(f32[384,1536]{1,0:T(8,128)} %all-reduce.2.cloned.1.call-done) | data formatting | bytes 4718592
  (190 shorter events, 84.4 us)
Async XLA Ops:
  45.1 25.2 %all-to-all-start.1 = ((bf16[16,24,1536]{2,1,0:T(8,128)(2,1)}), bf16[16,24,1536]{2,1,0:T(8,128)(2,1)}, u32[]{:S(2)}, u32[]{:S(2)}) async-start(bf16[16,24,1536]{2,1,0:T(8,128)(2,1)} %bitcast.15), calls=%async_computation.1 | async-start | bytes 2359296 | tf_op jit(solution)/shard_map/all_to_all | solution.py:577
  65.9 10.0 %collective-permute-start.9 = (bf16[32,512]{1,0:T(8,128)(2,1)S(1)}, bf16[32,512]{1,0:T(8,128)(2,1)S(1)}, u32[]{:S(2)}, u32[]{:S(2)}) collective-permute-start(bf16[32,512]{1,0:T(8,128)(2,1)S(1)} %get-tuple-element.84), channel_id=1, source_target_pairs={{0,2},{2,4},{4,6},{6,0},{1,3},{3,5},{5,7},{7,1},{8,10},{10,12},{12... | collective-permute-start | bytes 98312 | tf_op jit(solution)/shard_map/ppermute | solution.py:490
  70.3 32.8 %all-to-all-start.2 = ((bf16[16,24,1536]{2,1,0:T(8,128)(2,1)}), bf16[16,24,1536]{2,1,0:T(8,128)(2,1)}, u32[]{:S(2)}, u32[]{:S(2)}) async-start(bf16[16,24,1536]{2,1,0:T(8,128)(2,1)} %bitcast.17), calls=%async_computation.2 | async-start | bytes 2359296 | tf_op jit(solution)/shard_map/all_to_all | solution.py:577
  93.6 19.8 %collective-permute-start = (bf16[256,1536]{1,0:T(8,128)(2,1)}, bf16[256,1536]{1,0:T(8,128)(2,1)S(1)}, u32[]{:S(2)}, u32[]{:S(2)}) collective-permute-start(bf16[256,1536]{1,0:T(8,128)(2,1)} %get-tuple-element.70), channel_id=1, source_target_pairs={{0,1},{1,0},{2,3},{3,2},{4,5},{5,4},{6,7},{7,6},{8,9},{9,8},{10,11... | collective-permute-start | bytes 2359304 | tf_op jit(solution)/shard_map/ppermute | solution.py:482
  97.6 17.8 %collective-permute-start.13 = (bf16[64,1536]{1,0:T(8,128)(2,1)}, bf16[64,1536]{1,0:T(8,128)(2,1)S(1)}, u32[]{:S(2)}, u32[]{:S(2)}) collective-permute-start(bf16[64,1536]{1,0:T(8,128)(2,1)} %get-tuple-element.99), channel_id=1, source_target_pairs={{0,2},{2,4},{4,6},{6,0},{1,3},{3,5},{5,7},{7,1},{8,10},{10,12},{12... | collective-permute-start | bytes 589832 | tf_op jit(solution)/shard_map/ppermute | solution.py:490
  98.1 19.1 %collective-permute-start.14 = (bf16[64,1536]{1,0:T(8,128)(2,1)}, bf16[64,1536]{1,0:T(8,128)(2,1)S(1)}, u32[]{:S(2)}, u32[]{:S(2)}) collective-permute-start(bf16[64,1536]{1,0:T(8,128)(2,1)} %get-tuple-element.100), channel_id=1, source_target_pairs={{0,4},{2,6},{4,0},{6,2},{1,5},{3,7},{5,1},{7,3},{8,12},{10,14},{12... | collective-permute-start | bytes 589832 | tf_op jit(solution)/shard_map/ppermute | solution.py:490
  99.7 17.5 %collective-permute-start.15 = (bf16[64,1536]{1,0:T(8,128)(2,1)}, bf16[64,1536]{1,0:T(8,128)(2,1)S(1)}, u32[]{:S(2)}, u32[]{:S(2)}) collective-permute-start(bf16[64,1536]{1,0:T(8,128)(2,1)} %get-tuple-element.101), channel_id=1, source_target_pairs={{0,6},{2,0},{4,2},{6,4},{1,7},{3,1},{5,3},{7,5},{8,14},{10,8},{12,... | collective-permute-start | bytes 589832 | tf_op jit(solution)/shard_map/ppermute | solution.py:490
  106.2 94.7 %all-to-all-start.3 = ((bf16[16,2,24,1536]{3,2,1,0:T(8,128)(2,1)}), bf16[16,2,24,1536]{3,2,1,0:T(8,128)(2,1)}, u32[]{:S(2)}, u32[]{:S(2)}) async-start(bf16[16,2,24,1536]{3,2,1,0:T(8,128)(2,1)} %broadcast_in_dim.21), calls=%async_computation.3 | async-start | bytes 4718592 | tf_op jit(solution)/shard_map/all_to_all | solution.py:609
  113.3 157.9 %all-reduce.2.cloned.1.call-start = ((), (), s32[]{:S(2)}) async-start(), calls=%async_computation.4 | async-start | bytes 4718592 | tf_op jit(solution)/shard_map/psum | solution.py:574
  114.2 10.1 %collective-permute-start.2 = (bf16[64,1536]{1,0:T(8,128)(2,1)S(1)}, bf16[64,1536]{1,0:T(8,128)(2,1)S(1)}, u32[]{:S(2)}, u32[]{:S(2)}) collective-permute-start(bf16[64,1536]{1,0:T(8,128)(2,1)S(1)} %get-tuple-element.73), channel_id=1, source_target_pairs={{0,4},{2,6},{4,0},{6,2},{1,5},{3,7},{5,1},{7,3},{8,12},{10,14},{12... | collective-permute-start | bytes 589832 | tf_op jit(solution)/shard_map/ppermute | solution.py:490
  115.4 10.2 %collective-permute-start.3 = (bf16[64,1536]{1,0:T(8,128)(2,1)S(1)}, bf16[64,1536]{1,0:T(8,128)(2,1)S(1)}, u32[]{:S(2)}, u32[]{:S(2)}) collective-permute-start(bf16[64,1536]{1,0:T(8,128)(2,1)S(1)} %get-tuple-element.74), channel_id=1, source_target_pairs={{0,6},{2,0},{4,2},{6,4},{1,7},{3,1},{5,3},{7,5},{8,14},{10,8},{12,... | collective-permute-start | bytes 589832 | tf_op jit(solution)/shard_map/ppermute | solution.py:490
  117.6 28.5 %collective-permute-start.22 = (bf16[56,1536]{1,0:T(8,128)(2,1)S(1)}, bf16[56,1536]{1,0:T(8,128)(2,1)S(1)}, u32[]{:S(2)}, u32[]{:S(2)}) collective-permute-start(bf16[56,1536]{1,0:T(8,128)(2,1)S(1)} %constant_dynamic-update-slice_fusion.refs_0_), channel_id=1, source_target_pairs={{0,24},{8,0},{16,8},{24,16},{1,25},{9,1},{17,9},{25,17},{2,26},{10... | collective-permute-start | bytes 516104 | tf_op jit(solution)/shard_map/ppermute | solution.py:490
  120.2 28.1 %collective-permute-start.21 = (bf16[56,1536]{1,0:T(8,128)(2,1)S(1)}, bf16[56,1536]{1,0:T(8,128)(2,1)S(1)}, u32[]{:S(2)}, u32[]{:S(2)}) collective-permute-start(bf16[56,1536]{1,0:T(8,128)(2,1)S(1)} %constant_dynamic-update-slice_fusion.refs_0_), channel_id=1, source_target_pairs={{0,16},{8,24},{16,0},{24,8},{1,17},{9,25},{17,1},{25,9},{2,18},{10... | collective-permute-start | bytes 516104 | tf_op jit(solution)/shard_map/ppermute | solution.py:490
  122.7 29.4 %collective-permute-start.20 = (bf16[56,1536]{1,0:T(8,128)(2,1)S(1)}, bf16[56,1536]{1,0:T(8,128)(2,1)S(1)}, u32[]{:S(2)}, u32[]{:S(2)}) collective-permute-start(bf16[56,1536]{1,0:T(8,128)(2,1)S(1)} %constant_dynamic-update-slice_fusion.refs_0_), channel_id=1, source_target_pairs={{0,8},{8,16},{16,24},{24,0},{1,9},{9,17},{17,25},{25,1},{2,10},{10... | collective-permute-start | bytes 516104 | tf_op jit(solution)/shard_map/ppermute | solution.py:490
  125.7 42.4 %collective-permute-start.6 = (bf16[64,1536]{1,0:T(8,128)(2,1)S(1)}, bf16[64,1536]{1,0:T(8,128)(2,1)S(1)}, u32[]{:S(2)}, u32[]{:S(2)}) collective-permute-start(bf16[64,1536]{1,0:T(8,128)(2,1)S(1)} %out_part.1.refs_0_), channel_id=1, source_target_pairs={{0,6},{2,0},{4,2},{6,4},{1,7},{3,1},{5,3},{7,5},{8,14},{10,8},{12,... | collective-permute-start | bytes 589832 | tf_op jit(solution)/shard_map/ppermute | solution.py:490
  155.5 10.9 %collective-permute-start.23 = (bf16[56,1536]{1,0:T(8,128)(2,1)S(1)}, bf16[56,1536]{1,0:T(8,128)(2,1)S(1)}, u32[]{:S(2)}, u32[]{:S(2)}) collective-permute-start(bf16[56,1536]{1,0:T(8,128)(2,1)S(1)} %ring.2.refs_0_), channel_id=1, source_target_pairs={{0,32},{32,64},{64,96},{96,0},{1,33},{33,65},{65,97},{97,1},{2,34}... | collective-permute-start | bytes 516104 | tf_op jit(solution)/shard_map/ppermute | solution.py:490
  155.9 13.0 %collective-permute-start.5 = (bf16[64,1536]{1,0:T(8,128)(2,1)S(1)}, bf16[64,1536]{1,0:T(8,128)(2,1)S(1)}, u32[]{:S(2)}, u32[]{:S(2)}) collective-permute-start(bf16[64,1536]{1,0:T(8,128)(2,1)S(1)} %out_part.1.refs_0_), channel_id=1, source_target_pairs={{0,4},{2,6},{4,0},{6,2},{1,5},{3,7},{5,1},{7,3},{8,12},{10,14},{12... | collective-permute-start | bytes 589832 | tf_op jit(solution)/shard_map/ppermute | solution.py:490
  158.2 13.3 %collective-permute-start.4 = (bf16[64,1536]{1,0:T(8,128)(2,1)S(1)}, bf16[64,1536]{1,0:T(8,128)(2,1)S(1)}, u32[]{:S(2)}, u32[]{:S(2)}) collective-permute-start(bf16[64,1536]{1,0:T(8,128)(2,1)S(1)} %out_part.1.refs_0_), channel_id=1, source_target_pairs={{0,2},{2,4},{4,6},{6,0},{1,3},{3,5},{5,7},{7,1},{8,10},{10,12},{12... | collective-permute-start | bytes 589832 | tf_op jit(solution)/shard_map/ppermute | solution.py:490
  161.2 11.2 %collective-permute-start.18 = (bf16[64,1536]{1,0:T(8,128)(2,1)S(1)}, bf16[64,1536]{1,0:T(8,128)(2,1)S(1)}, u32[]{:S(2)}, u32[]{:S(2)}) collective-permute-start(bf16[64,1536]{1,0:T(8,128)(2,1)S(1)} %get-tuple-element.102.refs_0_), channel_id=1, source_target_pairs={{0,6},{2,0},{4,2},{6,4},{1,7},{3,1},{5,3},{7,5},{8,14},{10,8},{12,... | collective-permute-start | bytes 589832 | tf_op jit(solution)/shard_map/ppermute | solution.py:490
  168.1 11.6 %collective-permute-start.16 = (bf16[64,1536]{1,0:T(8,128)(2,1)S(1)}, bf16[64,1536]{1,0:T(8,128)(2,1)S(1)}, u32[]{:S(2)}, u32[]{:S(2)}) collective-permute-start(bf16[64,1536]{1,0:T(8,128)(2,1)S(1)} %get-tuple-element.102.refs_0_), channel_id=1, source_target_pairs={{0,2},{2,4},{4,6},{6,0},{1,3},{3,5},{5,7},{7,1},{8,10},{10,12},{12... | collective-permute-start | bytes 589832 | tf_op jit(solution)/shard_map/ppermute | solution.py:490
  168.9 12.3 %collective-permute-start.28 = (bf16[48,1536]{1,0:T(8,128)(2,1)}, bf16[48,1536]{1,0:T(8,128)(2,1)}, u32[]{:S(2)}, u32[]{:S(2)}) collective-permute-start(bf16[48,1536]{1,0:T(8,128)(2,1)} %pad_maximum_fusion.refs_0_), channel_id=1, source_target_pairs={{0,6},{2,0},{4,2},{6,4},{1,7},{3,1},{5,3},{7,5},{8,14},{10,8},{12,... | collective-permute-start | bytes 442376 | tf_op jit(solution)/shard_map/ppermute | solution.py:490
  172.4 13.0 %collective-permute-start.26 = (bf16[48,1536]{1,0:T(8,128)(2,1)}, bf16[48,1536]{1,0:T(8,128)(2,1)}, u32[]{:S(2)}, u32[]{:S(2)}) collective-permute-start(bf16[48,1536]{1,0:T(8,128)(2,1)} %pad_maximum_fusion.refs_0_), channel_id=1, source_target_pairs={{0,2},{2,4},{4,6},{6,0},{1,3},{3,5},{5,7},{7,1},{8,10},{10,12},{12... | collective-permute-start | bytes 442376 | tf_op jit(solution)/shard_map/ppermute | solution.py:490
  173.9 15.8 %collective-permute-start.7 = (bf16[256,1536]{1,0:T(8,128)(2,1)S(1)}, bf16[256,1536]{1,0:T(8,128)(2,1)S(1)}, u32[]{:S(2)}, u32[]{:S(2)}) collective-permute-start(bf16[256,1536]{1,0:T(8,128)(2,1)S(1)} %join.3.mine_ref), channel_id=1, source_target_pairs={{0,1},{1,0},{2,3},{3,2},{4,5},{5,4},{6,7},{7,6},{8,9},{9,8},{10,11... | collective-permute-start | bytes 2359304 | tf_op jit(solution)/shard_map/ppermute | solution.py:514
  180.3 11.1 %collective-permute-start.19 = (bf16[256,1536]{1,0:T(8,128)(2,1)S(1)}, bf16[256,1536]{1,0:T(8,128)(2,1)S(1)}, u32[]{:S(2)}, u32[]{:S(2)}) collective-permute-start(bf16[256,1536]{1,0:T(8,128)(2,1)S(1)} %join.4.mine_ref), channel_id=1, source_target_pairs={{0,1},{1,0},{2,3},{3,2},{4,5},{5,4},{6,7},{7,6},{8,9},{9,8},{10,11... | collective-permute-start | bytes 2359304 | tf_op jit(solution)/shard_map/ppermute | solution.py:514
  (55 other events, 283.7 us)
Sparse Core Ops, SparseCore 0:
  181.3 89.9 all-reduce.1

commit v2 on v1

v2 whole, which is shorter than its diff:
```python
import functools

import jax
import jax.numpy as jnp
from jax import lax
from jax.experimental import pallas as pl
from jax.experimental.pallas import tpu as pltpu
from jax.sharding import Mesh, PartitionSpec as P

KERNEL = 4
INNER = 3072
EPS = 1e-05
T = 512
GROUP = 256
D = 1536
C = 384
NH = 6
HD = 64
N = 128
BF = jnp.bfloat16
F32 = jnp.float32
EXACT = lax.Precision.HIGHEST


def dot(a, b, precision=None):
    return jnp.dot(a, b, preferred_element_type=F32, precision=precision)


def dot_nt(a, b):
    return lax.dot_general(a, b, (((1,), (1,)), ((), ())), preferred_element_type=F32)


def dot_tn(a, b):
    return lax.dot_general(a, b, (((0,), (0,)), ((), ())), preferred_element_type=F32)


def sigmoid(v):
    return 1.0 / (1.0 + jnp.exp(-v))


def softplus(v):
    return jnp.maximum(v, 0.0) + jnp.log1p(jnp.exp(-jnp.abs(v)))


def lane_ids(rows, cols):
    return lax.broadcasted_iota(jnp.int32, (rows, cols), 1)


def row_ids(rows, cols):
    return lax.broadcasted_iota(jnp.int32, (rows, cols), 0)


def conv_masks(seg):
    lanes = lane_ids(1, T)
    out = []
    for k in range(1, KERNEL):
        same = (pltpu.roll(seg, k, 1) == seg) & (lanes >= k)
        out.append(same.astype(F32))
    return out


def conv_forward(v, cols, bias, masks):
    total = bias + cols[0] * v
    for k in range(1, KERNEL):
        total = total + cols[k] * (pltpu.roll(v, k, 1) * masks[k - 1])
    return total


def conv_backward(d_pre, v, cols, masks):
    d_v = cols[0] * d_pre
    taps = [jnp.sum(d_pre * v, axis=1, keepdims=True)]
    for k in range(1, KERNEL):
        back = pltpu.roll(d_pre * masks[k - 1], T - k, 1)
        d_v = d_v + cols[k] * back
        taps.append(jnp.sum(back * v, axis=1, keepdims=True))
    return d_v, taps, jnp.sum(d_pre, axis=1, keepdims=True)


def scan_logs(step, rate, rows_ref, segf):
    upper = (row_ids(GROUP, GROUP) <= lane_ids(GROUP, GROUP)).astype(F32)
    a = step * rate
    logs = jnp.concatenate(
        [dot(a[:, :GROUP], upper, EXACT), dot(a[:, GROUP:], upper, EXACT)], axis=1
    )
    rows_ref[...] = jnp.zeros_like(rows_ref)
    rows_ref[0:8, :] = logs
    rows_ref[8:9, :] = segf
    return logs, rows_ref[...].T


def link_mask(cols, segf, c):
    sl = slice(c * GROUP, (c + 1) * GROUP)
    same = cols[sl, 8:9] == segf[:, sl]
    later = lane_ids(GROUP, GROUP) >= row_ids(GROUP, GROUP)
    return jnp.where(same & later, 0.0, -1e30)


def state_rows(logs, segf):
    final = segf[:, GROUP - 1 : GROUP]
    tail = jnp.exp(logs[:, GROUP - 1 : GROUP] - logs[:, :GROUP]) * (
        segf[:, :GROUP] == final
    ).astype(F32)
    entry = jnp.exp(logs[:, GROUP:]) * (segf[:, GROUP:] == final).astype(F32)
    return tail, entry


def per_head(rows, width):
    return jnp.concatenate(
        [jnp.broadcast_to(rows[h : h + 1, :], (HD, width)) for h in range(NH)], axis=0
    )


class Source:
    def __init__(self, hbm, vmem, sem):
        self.copy, self.ref = pltpu.make_async_copy(hbm, vmem, sem), vmem
        self.copy.start()
        self.waits = True

    def __call__(self):
        if self.waits:
            self.copy.wait()
            self.waits = False
        return self.ref


class Target:
    def __init__(self, hbm, vmem, sem):
        self.copy, self.ref = pltpu.make_async_copy(vmem, hbm, sem), vmem
        self.sent = False

    def put(self):
        self.copy.start()
        self.sent = True


def sds(shape, dtype):
    return jax.ShapeDtypeStruct(shape, dtype)


class Here:
    def __init__(self, ref):
        self.ref = ref

    def __call__(self):
        return self.ref

    def put(self):
        pass


NEAR, FAR, FREE = pltpu.VMEM, pltpu.HBM, pl.ANY


def pinned(v, where):
    return v if where is FREE else pltpu.with_memory_space_constraint(v, where)


def call(
    body, outs, args, scratch=(), name=None, near=(), free=(), near_out=(), free_out=(), us=0.0,
    vmem=40,
):
    n, m = len(args) - 1, len(outs)
    where = [NEAR if k in near else FREE if k in free else FAR for k in range(n)]
    where_out = [NEAR if k in near_out else FREE if k in free_out else FAR for k in range(m)]
    far = [k for k in range(n) if k not in near]
    far_out = [k for k in range(m) if k not in near_out]

    def kernel(idx_ref, *refs):
        ins, results, rest = refs[:n], refs[n : n + m], refs[n + m :]
        buffers, rest = rest[: len(far)], rest[len(far) :]
        out_buffers, rest = rest[: len(far_out)], rest[len(far_out) :]
        in_sems, out_sems, *own = rest
        sources, targets = [Here(ref) for ref in ins], [Here(ref) for ref in results]
        for j, k in enumerate(far):
            sources[k] = Source(ins[k], buffers[j], in_sems.at[j])
        for j, k in enumerate(far_out):
            targets[k] = Target(results[k], out_buffers[j], out_sems.at[j])
        body(idx_ref, sources, targets, *own)
        for source in sources:
            source()
        for k in far_out:
            if not targets[k].sent:
                targets[k].put()
        for k in far_out:
            targets[k].copy.wait()

    buffers = [pltpu.VMEM(args[1 + k].shape, args[1 + k].dtype) for k in far]
    buffers += [pltpu.VMEM(outs[k].shape, outs[k].dtype) for k in far_out]
    sems = [pltpu.SemaphoreType.DMA((max(len(v), 1),)) for v in (far, far_out)]
    return launch(kernel, outs, args, [*buffers, *sems, *scratch], name, where, where_out, us, vmem)


def launch(kernel, outs, args, scratch, name, where, where_out, us=0.0, vmem=40):
    return pl.pallas_call(
        kernel,
        out_shape=[v if w is FREE else w(v.shape, v.dtype) for v, w in zip(outs, where_out)],
        in_specs=[pl.BlockSpec(memory_space=pltpu.SMEM)]
        + [pl.BlockSpec(memory_space=w) for w in where],
        out_specs=[pl.BlockSpec(memory_space=w) for w in where_out],
        scratch_shapes=scratch,
        compiler_params=pltpu.CompilerParams(vmem_limit_bytes=vmem << 20),
        cost_estimate=pl.CostEstimate(
            flops=int(us * 1e9) + 1000, bytes_accessed=1000, transcendentals=0
        ),
        name=name,
    )(args[0], *[pinned(v, w) for v, w in zip(args[1:], where)])


SPREAD_US, WIDEN_US, REDUCE_US, INPUT_US = 0.0, 20.0, 0.0, 20.0


def fwd_kernel(idx_ref, sources, targets, rows_scr, par_scr, u_scr, inner_scr):
    (
        x_in, nw_in, ic_in, icb_in, sc_in, scb_in, tb_in, dl_in, sk_in, gnw_in, seg_in, tp_in,
        ip_in, sp_in, gp_in, op_in, cot_in,
    ) = sources
    (
        normed_ref, gate_ref, inner_ref, pre_ref, mixed_ref, dno_ref, states_ref, spre_ref,
        raw_ref, cols_ref, scols_ref, head_ref, sums_ref, x_part_ref, cot_part_ref,
    ) = [target.ref for target in targets]
    par_scr[...] = jnp.zeros_like(par_scr)
    nw_ref, x_ref = nw_in(), x_in()

    def norm_block(r, _):
        sl = pl.ds(r * 64, 64)
        v = x_ref[sl, :].astype(F32)
        scale = lax.rsqrt(jnp.mean(v * v, axis=1, keepdims=True) + EPS)
        normed_ref[sl, :] = (v * scale * nw_ref[...].reshape(1, D)).astype(BF)
        return 0

    lax.fori_loop(0, T // 64, norm_block, 0)
    own = pl.ds(pl.multiple_of(idx_ref[0] * GROUP + idx_ref[1] * 64, 64), 64)
    x_part_ref[...] = x_ref[own, :]
    targets[0].put()
    targets[13].put()
    par_scr[0:4, 0:C] = ic_in()[...]
    par_scr[4:5, 0:C] = icb_in()[...].reshape(1, C)
    par_scr[5:6, 0:C] = gnw_in()[...].reshape(1, C)
    par_scr[0:4, C : C + 256] = sc_in()[...]
    par_scr[4:5, C : C + 256] = scb_in()[...].reshape(1, 256)
    par_scr[8:9, 0:NH] = tb_in()[...].reshape(1, NH)
    par_scr[9:10, 0:NH] = dl_in()[...].reshape(1, NH)
    par_scr[10:11, 0:NH] = sk_in()[...].reshape(1, NH)
    par = par_scr[...].T
    cols_ref[...] = par[0:C, 0:8]
    scols_ref[...] = par[C : C + 256, 0:8]
    head_ref[...] = par[0:8, :]
    normed = normed_ref[...]
    raw_ref[0:8, :] = jnp.concatenate(
        [dot_nt(tp_in()[...], normed), jnp.zeros((8 - NH, T), F32)], axis=0
    )
    segf = seg_in()[...].astype(F32)
    raw_ref[8:16, :] = jnp.broadcast_to(segf, (8, T))
    inner_scr[...] = dot(normed, ip_in()[...]).T
    inner_ref[...] = inner_scr[...].astype(BF)
    states = dot(normed, sp_in()[...]).T
    states_ref[...] = states.astype(BF)
    gate_ref[...] = dot(normed, gp_in()[...]).T
    for k in (1, 2, 6, 8, 9, 10, 11):
        targets[k].put()
    cot_ref = cot_in()
    dno_ref[...] = dot_nt(op_in()[...], cot_ref[...])
    cot_part_ref[...] = cot_ref[own, :]
    targets[5].put()
    targets[14].put()

    masks = conv_masks(segf)
    head = head_ref[...]
    step = softplus(raw_ref[0:8, :] + head[:, 8:9])
    rate = -jnp.exp(head[:, 9:10])
    logs, lcols = scan_logs(step, rate, rows_scr, segf)

    spre = conv_forward(
        states, [scols_ref[:, k : k + 1] for k in range(KERNEL)], scols_ref[:, 4:5], masks
    )
    spre_ref[...] = spre
    targets[7].put()
    cs = spre * sigmoid(spre)
    b_tok = cs[0:N, :].T.astype(BF)
    c_low = cs[N:, :].astype(BF)
    for h in range(NH):
        hs = slice(h * HD, (h + 1) * HD)
        pre = conv_forward(
            inner_scr[hs, :], [cols_ref[hs, k : k + 1] for k in range(KERNEL)],
            cols_ref[hs, 4:5], masks,
        )
        pre_ref[hs, :] = pre
        u_scr[hs, :] = pre * sigmoid(pre)
    targets[3].put()
    tail, entry = state_rows(logs, segf)
    weighted = u_scr[:, 0:GROUP] * per_head(step[:, 0:GROUP] * tail, GROUP)
    state = dot(weighted.astype(BF), b_tok[0:GROUP, :])
    entering = dot(state.astype(BF), c_low[:, GROUP:])
    for c in range(2):
        sl = slice(c * GROUP, (c + 1) * GROUP)
        neg = link_mask(lcols, segf, c)
        scores = dot(b_tok[sl, :], c_low[:, sl])
        for h in range(NH):
            hs = slice(h * HD, (h + 1) * HD)
            decay = jnp.exp((logs[h : h + 1, sl] - lcols[sl, h : h + 1]) + neg)
            m = (scores * decay).astype(BF)
            u = u_scr[hs, sl]
            y = dot((u * step[h : h + 1, sl]).astype(BF), m)
            if c == 1:
                y = y + entering[hs, :] * entry[h : h + 1, :]
            mixed_ref[hs, sl] = y + head[h : h + 1, 10:11] * u
    targets[4].put()
    squares = jnp.zeros((1, T), F32)
    dots = jnp.zeros((1, T), F32)
    for h in range(NH):
        hs = slice(h * HD, (h + 1) * HD)
        g = gate_ref[hs, :]
        gated = mixed_ref[hs, :] * (g * sigmoid(g))
        squares = squares + jnp.sum(gated * gated, axis=0, keepdims=True)
        dots = dots + jnp.sum(dno_ref[hs, :] * cols_ref[hs, 5:6] * gated, axis=0, keepdims=True)
    sums_ref[...] = jnp.broadcast_to(
        jnp.concatenate([squares, dots], axis=0)[None], sums_ref.shape
    )


def forward(*args):
    outs = [
        sds((T, D), BF), sds((C, T), F32), sds((C, T), BF), sds((C, T), F32), sds((C, T), F32),
        sds((C, T), F32), sds((256, T), BF), sds((256, T), F32), sds((16, T), F32),
        sds((C, 8), F32), sds((256, 8), F32), sds((8, 128), F32), sds((8, 2, T), F32),
        sds((64, D), BF), sds((64, D), BF),
    ]
    scratch = [
        pltpu.VMEM((128, T), F32), pltpu.VMEM((128, 640), F32), pltpu.VMEM((C, T), F32),
        pltpu.VMEM((C, T), F32),
    ]
    return call(fwd_kernel, outs, args, scratch, "forward", near_out=(1, 4, 5))


def mid_kernel(idx_ref, sources, targets, no_scr, low_scr):
    sums_in, gate_in, mixed_in, dno_in, cols_in, cot_in, normed_in = sources
    grads_ref, no_ref, gate_low_ref, dy_ref, gain_ref = [t.ref for t in targets]
    total = jnp.sum(sums_in()[...], axis=0)
    scale = lax.rsqrt(total[0:1, :] / INNER + EPS)
    slope = scale * scale * scale * (total[1:2, :] / INNER)
    gate_ref, mixed_ref, dno_ref, cols_ref = gate_in(), mixed_in(), dno_in(), cols_in()
    for h in range(NH):
        hs = slice(h * HD, (h + 1) * HD)
        g = gate_ref[hs, :]
        s = sigmoid(g)
        silu = g * s
        mixed = mixed_ref[hs, :]
        gated = mixed * silu
        gain = cols_ref[hs, 5:6]
        normal = gated * scale
        no_scr[hs, :] = (normal * gain).astype(BF)
        dno = dno_ref[hs, :]
        gain_ref[hs, :] = jnp.broadcast_to(jnp.sum(dno * normal, axis=1, keepdims=True), (HD, 8))
        d_gated = scale * (dno * gain) - gated * slope
        low_scr[hs, :] = (d_gated * mixed * (s * (1.0 + g * (1.0 - s)))).astype(BF)
        dy_ref[hs, :] = (d_gated * silu).astype(BF)
    targets[3].put()
    out_grad = dot(no_scr[...], cot_in()[...]).astype(BF)
    for k in range(16):
        rows, columns = slice(k % 4 * 96, (k % 4 + 1) * 96), slice(k // 4 * C, (k // 4 + 1) * C)
        grads_ref[k, 96:192, :] = out_grad[rows, columns]
    gate_grad = dot(low_scr[...], normed_in()[...]).T.astype(BF)
    for k in range(16):
        grads_ref[k, 0:96, :] = gate_grad[k * 96 : (k + 1) * 96, :]
    targets[0].put()
    no_ref[...] = no_scr[...].T
    gate_low_ref[...] = low_scr[...].T


def middle(*args):
    outs = [
        sds((16, 192, C), BF), sds((T, C), BF), sds((T, C), BF), sds((C, T), BF), sds((C, 8), F32),
    ]
    scratch = [pltpu.VMEM((C, T), BF), pltpu.VMEM((C, T), BF)]
    return call(mid_kernel, outs, args, scratch, "middle", near=(1, 2, 3), free=(0,))


def bwd_kernel(
    idx_ref, sources, targets, rows_scr, u_scr, di_scr, low_scr, cs_scr, slow_scr, tpad, pad_scr,
    grad_scr, tok_scr, low_tok, step_tok, give_scr,
):
    (
        raw_in, head_in, spre_in, pre_in, dy_in, cols_in, inner_in, normed_in, scols_in,
        states_in, gate_low_in, sp_in, tp_in, gp_in, ip_in, no_in, op_in,
    ) = sources
    inner_grad_ref, keep_ref, extra_ref, *gives = [t.ref for t in targets]
    core = idx_ref[0]
    raw_ref, head_ref, spre_ref = raw_in(), head_in(), spre_in()
    segf = raw_ref[8:9, :]
    masks = conv_masks(segf)
    head = head_ref[...]
    raw = raw_ref[0:8, :] + head[:, 8:9]
    step = softplus(raw)
    rate = -jnp.exp(head[:, 9:10])
    logs, lcols = scan_logs(step, rate, rows_scr, segf)
    spre = spre_ref[...]
    cs = spre * sigmoid(spre)
    b_low = cs[0:N, :].astype(BF)
    c_low = cs[N:, :].astype(BF)
    b_tok = cs[0:N, :].T.astype(BF)
    c_tok = cs[N:, :].T.astype(BF)
    pre_ref, dy_ref = pre_in(), dy_in()
    for h in range(NH):
        hs = slice(h * HD, (h + 1) * HD)
        pre = pre_ref[hs, :]
        u_scr[hs, :] = pre * sigmoid(pre)
    tail, entry = state_rows(logs, segf)
    first, second = slice(0, GROUP), slice(GROUP, T)
    weighted = (u_scr[:, first] * per_head(step[:, first] * tail, GROUP)).astype(BF)
    state = dot(weighted, b_tok[first, :]).astype(BF)
    d_entering = (dy_ref[:, second] * per_head(entry, GROUP)).astype(BF)
    d_state = dot(d_entering, c_tok[second, :]).astype(BF)
    entering = dot(state, c_low[:, second])
    into = dot(d_state, b_low[:, first])
    d_c_second = dot_tn(state, d_entering)
    d_b_first = dot_tn(d_state, weighted)
    tri = (row_ids(GROUP, GROUP) >= lane_ids(GROUP, GROUP)).astype(BF)
    before = (row_ids(GROUP, GROUP) < lane_ids(GROUP, GROUP)).astype(F32)
    upto = (row_ids(GROUP, GROUP) < lane_ids(GROUP, GROUP)).astype(F32)
    since = (row_ids(GROUP, GROUP) >= lane_ids(GROUP, GROUP)).astype(F32)
    out_step = []
    out_skip = []
    da_rows = [[None, None] for _ in range(NH)]
    for c in range(2):
        sl = slice(c * GROUP, (c + 1) * GROUP)
        neg = link_mask(lcols, segf, c)
        scores = dot(b_tok[sl, :], c_low[:, sl])
        d_scores = jnp.zeros((GROUP, GROUP), F32)
        for h in range(NH):
            hs = slice(h * HD, (h + 1) * HD)
            decay = jnp.exp((logs[h : h + 1, sl] - lcols[sl, h : h + 1]) + neg)
            m = scores * decay
            dy = dy_ref[hs, sl]
            inflow = (u_scr[hs, sl] * step[h : h + 1, sl]).astype(BF)
            g = dot_tn(inflow, dy)
            d_scores = d_scores + g * decay
            w = dot((g * m).astype(BF), tri)
            da = jnp.sum(w * before, axis=0, keepdims=True)
            da_rows[h][c] = da
            di = dot_nt(dy, m.astype(BF))
            if c == 0:
                di = di + into[hs, :] * tail[h : h + 1, :]
            di_scr[hs, sl] = di
        ds = d_scores.astype(BF)
        d_b = dot_nt(c_low[:, sl], ds)
        d_c = dot(b_low[:, sl], ds)
        if c == 0:
            d_b = d_b + d_b_first
        else:
            d_c = d_c + d_c_second
        cs_scr[0:N, sl] = d_b
        cs_scr[N:, sl] = d_c
    cols_ref, inner_ref, normed_ref = cols_in(), inner_in(), normed_in()
    zero = jnp.zeros((1, GROUP), F32)
    q_rows, e_rows = [], []
    for h in range(NH):
        hs = slice(h * HD, (h + 1) * HD)
        q = u_scr[hs, first] * step[h : h + 1, first] * into[hs, :]
        q_rows.append(jnp.sum(q, axis=0, keepdims=True))
        e = dy_ref[hs, second] * entering[hs, :]
        e_rows.append(jnp.sum(e, axis=0, keepdims=True))
    q8 = jnp.concatenate(q_rows + [zero, zero], axis=0) * tail
    e8 = jnp.concatenate(e_rows + [zero, zero], axis=0) * entry
    da0 = jnp.concatenate([da_rows[h][0] for h in range(NH)] + [zero, zero], axis=0)
    da1 = jnp.concatenate([da_rows[h][1] for h in range(NH)] + [zero, zero], axis=0)
    da = jnp.concatenate([da0 + dot(q8, upto, EXACT), da1 + dot(e8, since, EXACT)], axis=1)
    d_steps = []
    pad_scr[...] = jnp.zeros_like(pad_scr)
    for h in range(NH):
        hs = slice(h * HD, (h + 1) * HD)
        pre = pre_ref[hs, :]
        s = sigmoid(pre)
        u = u_scr[hs, :]
        di = di_scr[hs, :]
        dy = dy_ref[hs, :].astype(F32)
        d_steps.append(jnp.sum(di * u, axis=0, keepdims=True))
        out_skip.append(jnp.sum(dy * u, axis=0, keepdims=True))
        d_u = di * step[h : h + 1, :] + head[h : h + 1, 10:11] * dy
        d_pre = d_u * (s * (1.0 + pre * (1.0 - s)))
        d_v, taps, bias = conv_backward(
            d_pre, inner_ref[hs, :].astype(F32),
            [cols_ref[hs, k : k + 1] for k in range(KERNEL)], masks,
        )
        low_scr[hs, :] = d_v.astype(BF)
        for k in range(KERNEL):
            pad_scr[hs, k : k + 1] = taps[k]
        pad_scr[hs, 4:5] = bias
    zero = jnp.zeros((2, T), F32)
    d_step = jnp.concatenate(d_steps + [zero], axis=0) + da * rate
    skips = jnp.concatenate(out_skip + [zero], axis=0)
    d_raw = d_step * sigmoid(raw)
    inner_grad_ref[...] = dot(low_scr[...], normed_ref[...]).T.astype(BF)
    targets[0].put()
    rows_scr[...] = jnp.zeros_like(rows_scr)
    rows_scr[0:8, :] = d_raw
    step_tok[...] = rows_scr[...].T.astype(BF)
    extra_ref[0:8, :] = dot(d_raw.astype(BF), normed_ref[...])
    scols_ref, states_ref = scols_in(), states_in()
    for part in range(4):
        rs = slice(part * 64, (part + 1) * 64)
        ps = slice(C + part * 64, C + (part + 1) * 64)
        pre = spre_ref[rs, :]
        s = sigmoid(pre)
        d_pre = cs_scr[rs, :] * (s * (1.0 + pre * (1.0 - s)))
        d_v, taps, bias = conv_backward(
            d_pre, states_ref[rs, :].astype(F32),
            [scols_ref[rs, k : k + 1] for k in range(KERNEL)], masks,
        )
        slow_scr[rs, :] = d_v.astype(BF)
        for k in range(KERNEL):
            pad_scr[ps, k : k + 1] = taps[k]
        pad_scr[ps, 4:5] = bias
    rows = pad_scr[...].T[0:8, :]
    columns = [
        jnp.sum(d_raw, axis=1, keepdims=True), jnp.sum(da * step, axis=1, keepdims=True) * rate,
        jnp.sum(skips, axis=1, keepdims=True), jnp.zeros((8, 125), F32),
    ]
    extra_ref[8:16, :] = jnp.concatenate(
        [rows[:, 0:C], *columns, jnp.zeros((8, D - C - 128), F32)], axis=1
    )
    targets[2].put()
    taps = jnp.concatenate(
        [
            jnp.concatenate([rows[:, C:], jnp.zeros((8, D - 256), F32)], axis=1),
            jnp.zeros((8, D), F32),
        ],
        axis=0,
    ).astype(BF)
    tok_scr[...] = slow_scr[...].T
    low_tok[...] = low_scr[...].T
    grad_scr[...] = dot(slow_scr[...], normed_ref[...]).astype(BF)
    tpad[...] = jnp.zeros_like(tpad)
    tpad[0:NH, :] = tp_in()[...]
    gate_low_ref, no_ref = gate_low_in(), no_in()
    gp_ref, ip_ref, sp_ref, op_ref = gp_in(), ip_in(), sp_in(), op_in()
    for give, half in ((True, 1 - core), (False, core)):
        tok = pl.ds(pl.multiple_of(half * GROUP, GROUP), GROUP)
        total = dot_nt(gate_low_ref[tok, :], gp_ref[...])
        total = total + dot_nt(low_tok[tok, :], ip_ref[...])
        total = total + dot_nt(tok_scr[tok, :], sp_ref[...])
        total = (total + dot(step_tok[tok, :], tpad[...])).astype(BF)
        out = dot(no_ref[tok, :], op_ref[...]).astype(BF)
        for k in range(4):
            slot = lax.rem(k + 4 - idx_ref[1], 4)
            rows = pl.ds(pl.multiple_of(half * 128 + k * 32, 32), 32)
            ref = give_scr if give else keep_ref
            ref[slot, 0:64, :] = total[k * 64 : (k + 1) * 64, :]
            ref[slot, 64:96, :] = grad_scr[rows, :]
            ref[slot, 96:112, :] = taps
            ref[slot, 112:176, :] = out[k * 64 : (k + 1) * 64, :]
        if give:
            for k in range(4):
                gives[k][...] = give_scr[k]


def backward(*args):
    outs = [sds((D, C), BF), sds((4, 176, D), BF), sds((16, D), F32), *[sds((176, D), BF)] * 4]
    scratch = [
        pltpu.VMEM((128, T), F32), pltpu.VMEM((C, T), F32), pltpu.VMEM((C, T), F32),
        pltpu.VMEM((C, T), BF), pltpu.VMEM((256, T), F32), pltpu.VMEM((256, T), BF),
        pltpu.VMEM((128, D), BF), pltpu.VMEM((C + 256, 128), F32), pltpu.VMEM((256, D), BF),
        pltpu.VMEM((T, 256), BF), pltpu.VMEM((T, C), BF), pltpu.VMEM((T, 128), BF),
        pltpu.VMEM((4, 176, D), BF),
    ]
    return call(bwd_kernel, outs, args, scratch, "backward", near_out=(1, 3, 4, 5, 6))


def fold_kernel(idx_ref, keep, g0, g1, g2, g3, own_hbm, s1, s2, s3, own, sem):
    for k in (0, 1, 2, 3):
        total = keep[k].astype(F32) + (g0, g1, g2, g3)[k][...].astype(F32)
        if k == 0:
            own[...] = total
            store = pltpu.make_async_copy(own, own_hbm, sem)
            store.start()
        else:
            (s1, s2, s3)[k - 1][...] = total.astype(BF)
    store.wait()


def swap(v):
    return lax.ppermute(v, "core", [(0, 1), (1, 0)])


def turn(v, axis, by):
    return lax.ppermute(v, axis, [(i, (i + by) % 4) for i in range(4)])


def scatter(idx, gives, keep):
    _, rows, width = keep.shape
    outs = [sds((rows, width), F32)] + [sds((rows, width), BF)] * 3
    scratch = [pltpu.VMEM((rows, width), F32), pltpu.SemaphoreType.DMA(())]
    own, *sends = launch(
        fold_kernel, outs, (idx, keep, *map(swap, gives)), scratch, "fold", [NEAR] * 5,
        [FAR, NEAR, NEAR, NEAR], vmem=16,
    )
    return [own] + [turn(send, "y", k + 1) for k, send in enumerate(sends)]


def gather(chunk, *earlier):
    pieces = [chunk] + [turn(chunk, "y", k) for k in range(1, 4)]
    return pieces + [swap(after(piece, *earlier)) for piece in pieces]


def place_of(idx_ref, k):
    half = idx_ref[0] if k < 4 else 1 - idx_ref[0]
    return half, half * 4 + lax.rem(idx_ref[1] + 4 - k % 4, 4)


def finish_kernel(idx_ref, *refs):
    pieces, out_hbm, grad_hbm = refs[:8], refs[8], refs[9]
    buf, grad, in_sems, out_sems = refs[10:]
    loads = [pltpu.make_async_copy(pieces[k], buf.at[k], in_sems.at[k]) for k in range(8)]
    for load in loads:
        load.start()
    stores = []
    for k in range(8):
        _, place = place_of(idx_ref, k)
        rows = pl.ds(pl.multiple_of(place * 64, 64), 64)
        loads[k].wait()
        stores.append(
            pltpu.make_async_copy(buf.at[k, 64:128], out_hbm.at[rows], out_sems.at[0, k])
        )
        stores[-1].start()
        grad[k] = buf[k, 0:64, :].astype(F32)
        stores.append(pltpu.make_async_copy(grad.at[k], grad_hbm.at[rows], out_sems.at[1, k]))
        stores[-1].start()
    for store in stores:
        store.wait()


def ends_kernel(idx_ref, sources, targets, state_scr, small_scr):
    (
        state_ref, norm_ref, sconv_ref, sbias_ref, step_ref, taps_ref, bias_ref, tb_ref, dl_ref,
        sk_ref, gnw_ref,
    ) = [t.ref for t in targets]
    for k in range(8):
        _, place = place_of(idx_ref, k)
        piece = sources[k]()
        for j in range(4):
            columns = slice(j * C, (j + 1) * C)
            for half in range(2):
                rows = pl.ds(pl.multiple_of(place * 32 + half * 16, 16), 16)
                state_scr[rows, columns] = piece[j * 4 + half].astype(F32)
            small_scr[place, :, columns] = piece[j * 4 + 2].astype(F32)
    for row in range(12):
        sl = slice(row * 128, (row + 1) * 128)
        state_ref[sl, :] = state_scr[:, sl].T
    targets[0].put()
    sconv_ref[...] = small_scr[0, 0:4, 0:256]
    sbias_ref[...] = small_scr[0, 4:5, 0:256].reshape(256)
    norm = small_scr[0, 8:9, :]
    for k in range(1, 8):
        norm = norm + small_scr[k, 8:9, :]
    norm_ref[...] = norm.reshape(D)
    own = sources[0]()
    for j in range(4):
        step_ref[:, j * C : (j + 1) * C] = own[j * 4 + 3][0:NH, :].astype(F32)
    smalls = jnp.concatenate([own[3], own[7]], axis=1)[8:16, :].astype(F32)
    taps_ref[...] = smalls[0:4, 0:C]
    bias_ref[...] = smalls[4:5, 0:C].reshape(C)
    gnw_ref[...] = smalls[5:6, 0:C].reshape(C)
    heads = jnp.concatenate([smalls[:, C : C + 128], jnp.zeros((120, 128), F32)], axis=0).T
    tb_ref[...] = heads[0:1, 0:NH].reshape(NH)
    dl_ref[...] = heads[1:2, 0:NH].reshape(NH)
    sk_ref[...] = heads[2:3, 0:NH].reshape(NH)


def input_kernel(idx_ref, sources, targets, pad_scr):
    x_ref, cot_ref, nw_ref, extra_ref, gain_ref = [source() for source in sources[:5]]
    chunk_ref, pack_ref = [t.ref for t in targets]
    p0, p1, p2, p3 = [source() for source in sources[5:]]
    total = (p0[...] + p1[...].astype(F32)) + (p2[...].astype(F32) + p3[...].astype(F32))
    d_normed = total[0:64, :]
    v = x_ref[...].astype(F32)
    scale = lax.rsqrt(jnp.mean(v * v, axis=1, keepdims=True) + EPS)
    weighted = d_normed * nw_ref[...].reshape(1, D)
    grad = scale * weighted - v * (
        scale * scale * scale * jnp.mean(weighted * v, axis=1, keepdims=True)
    )
    chunk_ref[0:64, :] = (cot_ref[...].astype(F32) + grad).astype(BF)
    chunk_ref[64:128, :] = (v + total[112:176, :]).astype(BF)
    targets[0].put()
    norm = jnp.broadcast_to(jnp.sum(d_normed * v * scale, axis=0, keepdims=True), (8, D))
    pad_scr[...] = jnp.zeros_like(pad_scr)
    pad_scr[:, 5:6] = gain_ref[:, 0:1]
    gain = jnp.concatenate([pad_scr[...].T[0:8, :], jnp.zeros((8, D - C), F32)], axis=1)
    rows = [
        total[64:80, :], total[80:96, :], jnp.concatenate([total[96:104, :], norm], axis=0),
        jnp.concatenate([extra_ref[0:8, :], extra_ref[8:16, :] + gain], axis=0),
    ]
    for k in range(16):
        pack_ref[k] = rows[k % 4][:, k // 4 * C : (k // 4 + 1) * C].astype(BF)


def share_kernel(idx_ref, sources, targets):
    total = total_of(sources[0]())
    for k in range(16):
        targets[0].ref[k] = total


def total_of(parts_ref):
    total = parts_ref[0].astype(F32)
    for k in range(1, 16):
        total = total + parts_ref[k].astype(F32)
    return total.astype(BF)


def reduce_kernel(idx_ref, sources, targets):
    targets[0].ref[...] = total_of(sources[0]())


def spread_kernel(idx_ref, parts_hbm, out_hbm, parts, own, sem, sems):
    load = pltpu.make_async_copy(parts_hbm, parts, sem)
    load.start()
    load.wait()
    own[...] = total_of(parts)
    stores = [pltpu.make_async_copy(own, out_hbm.at[k], sems.at[k]) for k in range(16)]
    for store in stores:
        store.start()
    for store in stores:
        store.wait()


def widen_kernel(idx_ref, hbm, wide_hbm, buf, wide, in_sems, out_sems):
    loads = [pltpu.make_async_copy(hbm.at[k], buf.at[k], in_sems.at[k]) for k in range(4)]
    for load in loads:
        load.start()
    stores = []
    for k in range(4):
        loads[k].wait()
        wide[k] = buf[k].astype(F32)
        stores.append(pltpu.make_async_copy(wide.at[k], wide_hbm.at[k], out_sems.at[k]))
        stores[-1].start()
    for store in stores:
        store.wait()


def widen_two_kernel(idx_ref, hbm, out_hbm, gate_hbm, buf, out, gate, in_sems, out_sems):
    loads = [pltpu.make_async_copy(hbm.at[k], buf.at[k], in_sems.at[k]) for k in range(4)]
    for load in loads:
        load.start()
    stores = []
    for k in range(4):
        loads[k].wait()
        for j in range(4):
            gate[k, j] = buf[k, j, 0:96, :].astype(F32)
            out[k, j * 96 : (j + 1) * 96, :] = buf[k, j, 96:192, :].astype(F32)
        columns = slice(k * C, (k + 1) * C)
        stores.append(pltpu.make_async_copy(gate.at[k], gate_hbm.at[k], out_sems.at[0, k]))
        stores.append(
            pltpu.make_async_copy(out.at[k], out_hbm.at[:, columns], out_sems.at[1, k])
        )
        stores[-2].start()
        stores[-1].start()
    for store in stores:
        store.wait()


def after(idx, *values):
    return lax.optimization_barrier((idx, *values))[0]


def per_device(
    inputs, norm_weight, gate_proj, inner_proj, state_proj, step_proj, inner_conv,
    inner_conv_bias, state_conv, state_conv_bias, step_bias, decay_log, skip_weight,
    gated_norm_weight, out_proj, segments, cotangent,
):
    x, cot, step_rows = inputs[0], cotangent[0], step_proj.T
    dma = pltpu.SemaphoreType.DMA
    idx = jnp.stack([lax.axis_index(a) for a in ("core", "y", "x", "z")]).astype(jnp.int32)
    (
        normed, gate, inner, pre, mixed, dno, states, spre, raw, cols, scols, head, sums, x_part,
        cot_part,
    ) = forward(
        idx, x, norm_weight, inner_conv, inner_conv_bias, state_conv, state_conv_bias, step_bias,
        decay_log, skip_weight, gated_norm_weight, segments, step_rows, inner_proj, state_proj,
        gate_proj, out_proj, cot,
    )
    sums = lax.all_to_all(sums, ("y", "core"), 0, 0, tiled=True)
    grads, no, gate_low, dy, gain = middle(idx, sums, gate, mixed, dno, cols, cot, normed)

    def dp_terms(v):
        return lax.all_to_all(v, ("x", "z"), 0, 0, tiled=True)

    first_terms = dp_terms(grads)
    inner_grad, keep, extra, *gives = backward(
        idx, raw, head, spre, pre, dy, cols, inner, normed, scols, states, gate_low, state_proj,
        step_rows, gate_proj, inner_proj, no, out_proj,
    )
    pieces = scatter(idx, gives, keep)
    (first,) = call(
        reduce_kernel, [sds((192, C), BF)], (after(idx, pieces[0]), first_terms), name="reduce",
        free=(0,), us=REDUCE_US,
    )
    inner_grad = after(inner_grad.reshape(16, D // 16, C), first)
    inner_terms = dp_terms(inner_grad)
    first = lax.all_gather(first, ("x", "z"))
    chunk, pack = call(
        input_kernel, [sds((128, D), BF), sds((16, 16, C), BF)],
        (idx, x_part, cot_part, norm_weight, extra, gain, *pieces),
        [pltpu.VMEM((C, 128), F32)], "input_part", free=(6, 7, 8), free_out=(0, 1),
        us=INPUT_US,
    )
    (spread,) = launch(
        spread_kernel, [sds((16, D // 16, C), BF)], (after(idx, chunk), inner_terms),
        [
            pltpu.VMEM((16, D // 16, C), BF), pltpu.VMEM((D // 16, C), BF), dma(()), dma((16,)),
        ],
        "spread", [FREE], [FAR], SPREAD_US,
    )
    (pack,) = call(
        share_kernel, [sds((16, 16, C), BF)], (idx, dp_terms(after(pack, spread))), name="share",
        free=(0,), free_out=(0,),
    )
    parts = gather(chunk, pack)
    outputs, input_grad = launch(
        finish_kernel, [sds((T, D), BF), sds((T, D), F32)], (idx, *parts),
        [
            pltpu.VMEM((8, 128, D), BF), pltpu.VMEM((8, 64, D), F32), dma((8,)), dma((2, 8)),
        ],
        "finish", [FREE] * 8, [FAR] * 2,
    )
    pack = dp_terms(pack)
    whole = dp_terms(after(spread, pack, input_grad))
    (
        state_grad, norm_grad, sconv, sbias, step_grad, taps, bias, tb, dl, sk, gnw,
    ) = call(
        ends_kernel,
        [
            sds((D, 256), F32), sds((D,), F32), sds((KERNEL, 256), F32), sds((256,), F32),
            sds((NH, D), F32), sds((KERNEL, C), F32), sds((C,), F32), sds((NH,), F32),
            sds((NH,), F32), sds((NH,), F32), sds((C,), F32),
        ],
        (idx, *gather(pack)), [pltpu.VMEM((256, D), F32), pltpu.VMEM((8, 16, D), F32)], "ends",
        free=range(8),
    )
    (inner_grad,) = launch(
        widen_kernel, [sds((4, 384, C), F32)], (idx, whole.reshape(4, 384, C)),
        [pltpu.VMEM((4, 384, C), BF), pltpu.VMEM((4, 384, C), F32), dma((4,)), dma((4,))],
        "widen", [FREE], [FAR], WIDEN_US,
    )
    out_grad, gate_grad = launch(
        widen_two_kernel, [sds((C, D), F32), sds((4, 4, 96, C), F32)],
        (idx, first.reshape(4, 4, 192, C)),
        [
            pltpu.VMEM((4, 4, 192, C), BF), pltpu.VMEM((4, C, C), F32),
            pltpu.VMEM((4, 4, 96, C), F32), dma((4,)), dma((2, 4)),
        ],
        "widen_two", [FAR], [FAR] * 2,
    )
    return (
        outputs[None], input_grad[None], norm_grad, gate_grad.reshape(D, C),
        inner_grad.reshape(D, C), state_grad, step_grad.T, taps, bias, sconv, sbias, tb, dl, sk,
        gnw, out_grad,
    )


def solution(mesh):
    small = Mesh(mesh.devices.reshape(4, 4, 4, 2), ("z", "x", "y", "core"))
    dp, tp = ("z", "x"), ("y", "core")
    placed = (
        P(dp, None, None), P(), P(None, tp), P(None, tp), P(), P(None, tp), P(None, tp), P(tp),
        P(), P(), P(tp), P(tp), P(tp), P(tp), P(tp, None), P(dp, None), P(dp, None, None),
    )
    out = (
        P(dp, None, None), P(dp, None, None), P(), P(None, tp), P(None, tp), P(), P(None, tp),
        P(None, tp), P(tp), P(), P(), P(tp), P(tp), P(tp), P(tp), P(tp, None),
    )
    return jax.shard_map(per_device, mesh=small, in_specs=placed, out_specs=out, check_vma=False)
```

time: 283 us -> 172 us (0.61)
  waiting for transfers between devices: 108 us -> 26 us
  local copies, waits for them, and re-layouts: 45 us -> 0 us
  Pallas kernels: 42.9 us -> 59.6 us
  blocking collectives: 10.5 us -> 26.1 us
  starting transfers between devices: 53.8 us -> 45.4 us
  other arithmetic: 6.49 us -> 0.08 us
    psum x1 -> x0, waiting for transfers between devices: 61.3 us -> none  [per_device(): out_grad = lax.psum(out_grad, dp)]
    unnamed x96 -> x0, local copies, waits for them, and re-layouts: 32.3 us -> none
    ppermute x24 -> x9, waiting for transfers between devices: 44.2 us -> 13.4 us  [turn(): return lax.ppermute(v, axis, [(i, (i + by) % 4) for i in range(4)])]
    pallas_call x18 -> x12, Pallas kernels: 42.9 us -> 59.6 us  [launch(): pl.pallas_call(kernel, out_shape=[v if w is FREE else w(v.shape, v.dtype)...]
    all_to_all x1 -> x2, blocking collectives: 10.5 us -> 26.1 us  [the longest x1 15.4 us: dp_terms(): return lax.all_to_all(v, ('x', 'z'), 0, 0, tiled=True)]
    ppermute x24 -> x9, starting transfers between devices: 26.9 us -> 11.8 us  [turn(): return lax.ppermute(v, axis, [(i, (i + by) % 4) for i in range(4)])]
    ppermute x6 -> x12, starting transfers between devices: 6.48 us -> 14 us  [swap(): return lax.ppermute(v, 'core', [(0, 1), (1, 0)])]
    all_to_all x3 -> x4, waiting for transfers between devices: 1.51 us -> 8.18 us  [dp_terms(): return lax.all_to_all(v, ('x', 'z'), 0, 0, tiled=True)]
  transfers between devices with their start and end apart: 34 -> 26, of which waited for: 15 -> 13; matrix products, arithmetic and copies ran while one was open for 9% -> 0% of each run, Pallas kernels for 10% -> 22%
where the time goes in v2:
time: 172 us; the launch traced here: 171 us
  Pallas kernels  59.6 us (35%)
  starting transfers between devices  45.4 us (26%)
  blocking collectives  26.1 us (15%)
  waiting for transfers between devices  26 us (15%)
  between operations  14.3 us (8%)
    pallas_call x12, Pallas kernels, launch(): pl.pallas_call(kernel, out_shape=[v if w is FREE else w(v.shape, v.dtype)...  59.6 us
    all_to_all x4, starting transfers between devices, dp_terms(): return lax.all_to_all(v, ('x', 'z'), 0, 0, tiled=True)  19.3 us
    all_to_all x1, blocking collectives, dp_terms(): return lax.all_to_all(v, ('x', 'z'), 0, 0, tiled=True)  15.4 us
    ppermute x12, starting transfers between devices, swap(): return lax.ppermute(v, 'core', [(0, 1), (1, 0)])  14 us
    ppermute x9, waiting for transfers between devices, turn(): return lax.ppermute(v, axis, [(i, (i + by) % 4) for i in range(4)])  13.4 us
    ppermute x9, starting transfers between devices, turn(): return lax.ppermute(v, axis, [(i, (i + by) % 4) for i in range(4)])  11.8 us
    all_to_all x1, blocking collectives, per_device(): sums = lax.all_to_all(sums, ('y', 'core'), 0, 0, tiled=True)  10.7 us
    all_to_all x4, waiting for transfers between devices, dp_terms(): return lax.all_to_all(v, ('x', 'z'), 0, 0, tiled=True)  8.18 us
  transfers between devices with their start and end apart: 26, of which 13 were waited for; matrix products, arithmetic and copies ran while one was open for 0% of the time, Pallas kernels for 22%

profile of v2, /device:TPU:1, one launch (start us, length us, event | category | flops | bytes accessed | tf_op | source)
XLA Modules:
  0.0 171.5 jit_solution(3280675890330587840)
XLA Ops:
  7.3 12.0 %forward.1 = (bf16[512,1536]{1,0:T(8,128)(2,1)}, f32[384,512]{1,0:T(8,128)S(1)}, bf16[384,512]{1,0:T(8,128)(2,1)}, f32[384,512]{1,0:T(8,128)}, f32[384,512]{1,0:...) custom-call(s32[4]{0:T(128)S(1)} %pad_add_fusion.idx_ref, ...), custom_call_target="tpu_custom_call" | custom-call | flops 1000 | bytes 1000 | tf_op jit(solution)/shard_map/forward/pallas_call | solution.py:194
  19.3 10.7 %all_to_all.30.refs_0_ = f32[8,2,512]{2,1,0:T(2,128)S(1)} all-to-all(f32[8,2,512]{2,1,0:T(2,128)} %get-tuple-element.79), channel_id=1, replica_groups=mesh['z'=4,'x'=4,'y'=4,'core'=2] {'y','core'}, dimensions={0} | all-to-all | bytes 65536 | tf_op jit(solution)/shard_map/all_to_all | solution.py:779
  30.0 5.7 %middle.1 = (bf16[16,192,384]{2,1,0:T(8,128)(2,1)}, bf16[512,384]{1,0:T(8,128)(2,1)}, bf16[512,384]{1,0:T(8,128)(2,1)}, bf16[384,512]{1,0:T(8,128)(2,1)}, f32[384,8]{1,0:T(8,128)}) custom-call(s32[4]{0:T(128)S(1)} %pad_add_fusion.idx_ref, f32[8,2,512]{2,1,0:T(2,128)S(1)} %all_to_all.30.refs_0_, f32[384,512]{1,0:T(8,128)S(1)} %get-tuple-element.80.refs_1_, ...), custom_call_target="tpu_custom_call" | custom-call | flops 1000 | bytes 1000 | tf_op jit(solution)/shard_map/middle/pallas_call | solution.py:194
  35.7 7.6 %all-to-all-start.1 = ((bf16[16,192,384]{2,1,0:T(8,128)(2,1)}), bf16[16,192,384]{2,1,0:T(8,128)(2,1)S(1)}, u32[]{:S(2)}, u32[]{:S(2)}) async-start(bf16[16,192,384]{2,1,0:T(8,128)(2,1)} %get-tuple-element.107), calls=%async_computation.1 | async-start | bytes 4718592 | tf_op jit(solution)/shard_map/all_to_all | solution.py:783
  43.5 14.7 %backward.1 = (bf16[1536,384]{1,0:T(8,128)(2,1)}, bf16[4,176,1536]{2,1,0:T(8,128)(2,1)S(1)}, f32[16,1536]{1,0:T(8,128)}, bf16[176,1536]{1,0:T(8,128)(2,1)S(1)}, ...) custom-call(s32[4]{0:T(128)S(1)} %pad_add_fusion.idx_ref, ...), custom_call_target="tpu_custom_call" | custom-call | flops 1000 | bytes 1000 | tf_op jit(solution)/shard_map/backward/pallas_call | solution.py:194
  63.2 2.8 %fold.1 = (f32[176,1536]{1,0:T(8,128)}, bf16[176,1536]{1,0:T(8,128)(2,1)}, bf16[176,1536]{1,0:T(8,128)(2,1)}, bf16[176,1536]{1,0:T(8,128)(2,1)}) custom-call(s32[4]{0:T(128)S(1)} %pad_add_fusion.idx_ref, bf16[4,176,1536]{2,1,0:T(8,128)(2,1)S(1)} %get-tuple-element.93.keep, bf16[176,1536]{1,0:T(8,128)(2,1)S(1)} %collective-permute-done.g0, ...), custom_call_target="tpu_custom_call" | custom-call | flops 1000 | bytes 1000 | tf_op jit(solution)/shard_map/fold/pallas_call | solution.py:194
  69.2 5.5 %all-to-all-done.1.refs_0_ = bf16[16,192,384]{2,1,0:T(8,128)(2,1)S(1)} async-done(((bf16[16,192,384]{2,1,0:T(8,128)(2,1)}), bf16[16,192,384]{2,1,0:T(8,128)(2,1)S(1)}, u32[]{:S(2)}, u32[]{:S(2)}) %all-to-all-start.1) | async-done | bytes 2359328 | tf_op jit(solution)/shard_map/all_to_all | solution.py:783
  76.5 3.7 %all-to-all-start.2 = ((bf16[16,96,384]{2,1,0:T(8,128)(2,1)}), bf16[16,96,384]{2,1,0:T(8,128)(2,1)S(1)}, u32[]{:S(2)}, u32[]{:S(2)}) async-start(bf16[16,96,384]{2,1,0:T(8,128)(2,1)} %bitcast.20), calls=%async_computation.2 | async-start | bytes 2359296 | tf_op jit(solution)/shard_map/all_to_all | solution.py:783
  81.8 10.5 %collective-permute-done.5.refs_7_ = bf16[176,1536]{1,0:T(8,128)(2,1)} collective-permute-done((bf16[176,1536]{1,0:T(8,128)(2,1)}, bf16[176,1536]{1,0:T(8,128)(2,1)}, u32[]{:S(2)}, u32[]{:S(2)}) %collective-permute-start.5) | collective-permute-done | bytes 540704 | tf_op jit(solution)/shard_map/ppermute | solution.py:585
  93.2 3.8 %input_part.1 = (bf16[128,1536]{1,0:T(8,128)(2,1)S(1)}, bf16[16,16,384]{2,1,0:T(8,128)(2,1)S(1)}) custom-call(s32[4]{0:T(128)S(1)} %pad_add_fusion.idx_ref, bf16[64,1536]{1,0:T(8,128)(2,1)} %get-tuple-element.73.refs_0_, bf16[64,1536]{1,0:T(8,128)(2,1)} %get-tuple-element.74.refs_1_, f32[1536]{0:T(1024)} %refs_2_.3, f32[16,1536]{1,0:T(8,128)} %get-tuple-element.91.refs_3_, ...), custom_call_target="tpu_custom_call" | custom-call | flops 20000000000 | bytes 1000 | tf_op jit(solution)/shard_map/input_part/pallas_call | solution.py:194
  98.3 3.2 %collective-permute-start.8 = (bf16[128,1536]{1,0:T(8,128)(2,1)S(1)}, bf16[128,1536]{1,0:T(8,128)(2,1)S(1)}, u32[]{:S(2)}, u32[]{:S(2)}) collective-permute-start(bf16[128,1536]{1,0:T(8,128)(2,1)S(1)} %get-tuple-element.110.refs_0_), channel_id=1, source_target_pairs={{0,4},{2,6},{4,0},{6,2},{1,5},{3,7},{5,1},{7,3},{8,12},{10,14},{12... | collective-permute-start | bytes 1179656 | tf_op jit(solution)/shard_map/ppermute | solution.py:585
  101.5 2.1 %spread.1 = bf16[16,96,384]{2,1,0:T(8,128)(2,1)} custom-call(s32[4]{0:T(128)S(1)} %pad_add_fusion.idx_ref, bf16[16,96,384]{2,1,0:T(8,128)(2,1)S(1)} %all-to-all-done.2.parts_hbm), custom_call_target="tpu_custom_call" | custom-call | flops 1000 | bytes 1000 | tf_op jit(solution)/shard_map/spread/pallas_call | solution.py:194
  103.6 15.4 %all_to_all.31.refs_0_ = bf16[16,16,384]{2,1,0:T(8,128)(2,1)S(1)} all-to-all(bf16[16,16,384]{2,1,0:T(8,128)(2,1)S(1)} %get-tuple-element.109), channel_id=1, replica_groups=mesh['z'=4,'x'=4,'y'=4,'core'=2] {'x','z'}, dimensions={0} | all-to-all | bytes 393216 | tf_op jit(solution)/shard_map/all_to_all | solution.py:783
  120.5 2.9 %collective-permute-start.10 = (bf16[128,1536]{1,0:T(8,128)(2,1)S(1)}, bf16[128,1536]{1,0:T(8,128)(2,1)S(1)}, u32[]{:S(2)}, u32[]{:S(2)}) collective-permute-start(bf16[128,1536]{1,0:T(8,128)(2,1)S(1)} %get-tuple-element.110.refs_0_), channel_id=1, source_target_pairs={{0,1},{1,0},{2,3},{3,2},{4,5},{5,4},{6,7},{7,6},{8,9},{9,8},{10,11... | collective-permute-start | bytes 1179656 | tf_op jit(solution)/shard_map/ppermute | solution.py:581
  124.0 4.0 %all-to-all-start.4 = ((bf16[16,16,384]{2,1,0:T(8,128)(2,1)}), bf16[16,16,384]{2,1,0:T(8,128)(2,1)S(1)}, u32[]{:S(2)}, u32[]{:S(2)}) async-start(bf16[16,16,384]{2,1,0:T(8,128)(2,1)} %share.1), calls=%async_computation.4 | async-start | bytes 393216 | tf_op jit(solution)/shard_map/all_to_all | solution.py:783
  128.0 4.4 %finish.1 = (bf16[512,1536]{1,0:T(8,128)(2,1)}, f32[512,1536]{1,0:T(8,128)}) custom-call(s32[4]{0:T(128)S(1)} %pad_add_fusion.idx_ref, bf16[128,1536]{1,0:T(8,128)(2,1)S(1)} %get-tuple-element.110.refs_0_, bf16[128,1536]{1,0:T(8,128)(2,1)S(1)} %collective-permute-done.7.refs_1_, bf16[128,1536]{1,0:T(8,128)(2,1)S(1)} %collective-permute-done.8.refs_2_, ...), custom_call_target="tpu_custom_call" | custom-call | flops 1000 | bytes 1000 | tf_op jit(solution)/shard_map/finish/pallas_call | solution.py:194
  132.4 2.6 %all-to-all-done.4.refs_0_ = bf16[16,16,384]{2,1,0:T(8,128)(2,1)S(1)} async-done(((bf16[16,16,384]{2,1,0:T(8,128)(2,1)}), bf16[16,16,384]{2,1,0:T(8,128)(2,1)S(1)}, u32[]{:S(2)}, u32[]{:S(2)}) %all-to-all-start.4) | async-done | bytes 196640 | tf_op jit(solution)/shard_map/all_to_all | solution.py:783
  135.0 4.0 %all-to-all-start.5 = ((bf16[16,96,384]{2,1,0:T(8,128)(2,1)}), bf16[16,96,384]{2,1,0:T(8,128)(2,1)S(1)}, u32[]{:S(2)}, u32[]{:S(2)}) async-start(bf16[16,96,384]{2,1,0:T(8,128)(2,1)} %spread.1), calls=%async_computation.5 | async-start | bytes 2359296 | tf_op jit(solution)/shard_map/all_to_all | solution.py:783
  141.2 2.2 %collective-permute-start.16 = (bf16[16,16,384]{2,1,0:T(8,128)(2,1)S(1)}, bf16[16,16,384]{2,1,0:T(8,128)(2,1)S(1)}, u32[]{:S(2)}, u32[]{:S(2)}) collective-permute-start(bf16[16,16,384]{2,1,0:T(8,128)(2,1)S(1)} %all-to-all-done.4.refs_0_), channel_id=1, source_target_pairs={{0,6},{2,0},{4,2},{6,4},{1,7},{3,1},{5,3},{7,5},{8,14},{10,8},{12,... | collective-permute-start | bytes 589832 | tf_op jit(solution)/shard_map/ppermute | solution.py:585
  143.3 2.0 %collective-permute-start.17 = (bf16[16,16,384]{2,1,0:T(8,128)(2,1)S(1)}, bf16[16,16,384]{2,1,0:T(8,128)(2,1)S(1)}, u32[]{:S(2)}, u32[]{:S(2)}) collective-permute-start(bf16[16,16,384]{2,1,0:T(8,128)(2,1)S(1)} %all-to-all-done.4.refs_0_), channel_id=1, source_target_pairs={{0,1},{1,0},{2,3},{3,2},{4,5},{5,4},{6,7},{7,6},{8,9},{9,8},{10,11... | collective-permute-start | bytes 589832 | tf_op jit(solution)/shard_map/ppermute | solution.py:581
  145.6 6.3 %collective-permute-start.18 = (bf16[16,16,384]{2,1,0:T(8,128)(2,1)S(1)}, bf16[16,16,384]{2,1,0:T(8,128)(2,1)S(1)}, u32[]{:S(2)}, u32[]{:S(2)}) collective-permute-start(bf16[16,16,384]{2,1,0:T(8,128)(2,1)S(1)} %collective-permute-done.14.refs_1_), channel_id=1, source_target_pairs={{0,1},{1,0},{2,3},{3,2},{4,5},{5,4},{6,7},{7,6},{8,9},{9,8},{10,11... | collective-permute-start | bytes 589832 | tf_op jit(solution)/shard_map/ppermute | solution.py:581
  153.6 4.7 %ends.1 = (f32[1536,256]{1,0:T(8,128)}, f32[1536]{0:T(1024)}, f32[4,256]{1,0:T(4,128)}, f32[256]{0:T(256)}, f32[6,1536]{1,0:T(8,128)}, /*index=5*/f32[4,384]{1,0...) custom-call(s32[4]{0:T(128)S(1)} %pad_add_fusion.idx_ref, ...), custom_call_target="tpu_custom_call" | custom-call | flops 1000 | bytes 1000 | tf_op jit(solution)/shard_map/ends/pallas_call | solution.py:194
  158.4 2.3 %widen.1 = f32[4,384,384]{2,1,0:T(8,128)} custom-call(s32[4]{0:T(128)S(1)} %pad_add_fusion.idx_ref, bf16[4,384,384]{2,1,0:T(8,128)(2,1)S(1)} %bitcast.15), custom_call_target="tpu_custom_call" | custom-call | flops 20000000000 | bytes 1000 | tf_op jit(solution)/shard_map/widen/pallas_call | solution.py:194
  160.7 3.9 %widen_two.1 = (f32[384,1536]{1,0:T(8,128)}, f32[4,4,96,384]{3,2,1,0:T(8,128)}) custom-call(s32[4]{0:T(128)S(1)} %pad_add_fusion.idx_ref, bf16[4,4,192,384]{3,2,1,0:T(8,128)(2,1)} %bitcast.18), custom_call_target="tpu_custom_call" | custom-call | flops 1000 | bytes 1000 | tf_op jit(solution)/shard_map/widen_two/pallas_call | solution.py:194
  (44 shorter events, 20.2 us)
Async XLA Ops:
  35.7 39.1 %all-to-all-start.1 = ((bf16[16,192,384]{2,1,0:T(8,128)(2,1)}), bf16[16,192,384]{2,1,0:T(8,128)(2,1)S(1)}, u32[]{:S(2)}, u32[]{:S(2)}) async-start(bf16[16,192,384]{2,1,0:T(8,128)(2,1)} %get-tuple-element.107), calls=%async_computation.1 | async-start | bytes 4718592 | tf_op jit(solution)/shard_map/all_to_all | solution.py:783
  43.3 117.4 %all-gather.3.cloned.1.call-start = ((), (), s32[]{:S(2)}) async-start(), calls=%async_computation.6 | async-start | bytes 2506752 | tf_op jit(solution)/shard_map/all_gather | solution.py:797
  58.3 2.6 %collective-permute-start = (bf16[176,1536]{1,0:T(8,128)(2,1)S(1)}, bf16[176,1536]{1,0:T(8,128)(2,1)S(1)}, u32[]{:S(2)}, u32[]{:S(2)}) collective-permute-start(bf16[176,1536]{1,0:T(8,128)(2,1)S(1)} %get-tuple-element.94), channel_id=1, source_target_pairs={{0,1},{1,0},{2,3},{3,2},{4,5},{5,4},{6,7},{7,6},{8,9},{9,8},{10,11... | collective-permute-start | bytes 1622024 | tf_op jit(solution)/shard_map/ppermute | solution.py:581
  59.3 2.3 %collective-permute-start.1 = (bf16[176,1536]{1,0:T(8,128)(2,1)S(1)}, bf16[176,1536]{1,0:T(8,128)(2,1)S(1)}, u32[]{:S(2)}, u32[]{:S(2)}) collective-permute-start(bf16[176,1536]{1,0:T(8,128)(2,1)S(1)} %get-tuple-element.95), channel_id=1, source_target_pairs={{0,1},{1,0},{2,3},{3,2},{4,5},{5,4},{6,7},{7,6},{8,9},{9,8},{10,11... | collective-permute-start | bytes 1622024 | tf_op jit(solution)/shard_map/ppermute | solution.py:581
  59.4 3.0 %collective-permute-start.2 = (bf16[176,1536]{1,0:T(8,128)(2,1)S(1)}, bf16[176,1536]{1,0:T(8,128)(2,1)S(1)}, u32[]{:S(2)}, u32[]{:S(2)}) collective-permute-start(bf16[176,1536]{1,0:T(8,128)(2,1)S(1)} %get-tuple-element.96), channel_id=1, source_target_pairs={{0,1},{1,0},{2,3},{3,2},{4,5},{5,4},{6,7},{7,6},{8,9},{9,8},{10,11... | collective-permute-start | bytes 1622024 | tf_op jit(solution)/shard_map/ppermute | solution.py:581
  59.8 3.4 %collective-permute-start.3 = (bf16[176,1536]{1,0:T(8,128)(2,1)S(1)}, bf16[176,1536]{1,0:T(8,128)(2,1)S(1)}, u32[]{:S(2)}, u32[]{:S(2)}) collective-permute-start(bf16[176,1536]{1,0:T(8,128)(2,1)S(1)} %get-tuple-element.97), channel_id=1, source_target_pairs={{0,1},{1,0},{2,3},{3,2},{4,5},{5,4},{6,7},{7,6},{8,9},{9,8},{10,11... | collective-permute-start | bytes 1622024 | tf_op jit(solution)/shard_map/ppermute | solution.py:581
  66.0 15.8 %collective-permute-start.4 = (bf16[176,1536]{1,0:T(8,128)(2,1)}, bf16[176,1536]{1,0:T(8,128)(2,1)S(1)}, u32[]{:S(2)}, u32[]{:S(2)}) collective-permute-start(bf16[176,1536]{1,0:T(8,128)(2,1)} %get-tuple-element.99), channel_id=1, source_target_pairs={{0,2},{2,4},{4,6},{6,0},{1,3},{3,5},{5,7},{7,1},{8,10},{10,12},{12... | collective-permute-start | bytes 1622024 | tf_op jit(solution)/shard_map/ppermute | solution.py:585
  66.6 25.7 %collective-permute-start.5 = (bf16[176,1536]{1,0:T(8,128)(2,1)}, bf16[176,1536]{1,0:T(8,128)(2,1)}, u32[]{:S(2)}, u32[]{:S(2)}) collective-permute-start(bf16[176,1536]{1,0:T(8,128)(2,1)} %get-tuple-element.100), channel_id=1, source_target_pairs={{0,4},{2,6},{4,0},{6,2},{1,5},{3,7},{5,1},{7,3},{8,12},{10,14},{12... | collective-permute-start | bytes 1622024 | tf_op jit(solution)/shard_map/ppermute | solution.py:585
  68.4 24.9 %collective-permute-start.6 = (bf16[176,1536]{1,0:T(8,128)(2,1)}, bf16[176,1536]{1,0:T(8,128)(2,1)}, u32[]{:S(2)}, u32[]{:S(2)}) collective-permute-start(bf16[176,1536]{1,0:T(8,128)(2,1)} %get-tuple-element.101), channel_id=1, source_target_pairs={{0,6},{2,0},{4,2},{6,4},{1,7},{3,1},{5,3},{7,5},{8,14},{10,8},{12,... | collective-permute-start | bytes 1622024 | tf_op jit(solution)/shard_map/ppermute | solution.py:585
  76.5 25.0 %all-to-all-start.2 = ((bf16[16,96,384]{2,1,0:T(8,128)(2,1)}), bf16[16,96,384]{2,1,0:T(8,128)(2,1)S(1)}, u32[]{:S(2)}, u32[]{:S(2)}) async-start(bf16[16,96,384]{2,1,0:T(8,128)(2,1)} %bitcast.20), calls=%async_computation.2 | async-start | bytes 2359296 | tf_op jit(solution)/shard_map/all_to_all | solution.py:783
  97.0 26.3 %collective-permute-start.7 = (bf16[128,1536]{1,0:T(8,128)(2,1)S(1)}, bf16[128,1536]{1,0:T(8,128)(2,1)S(1)}, u32[]{:S(2)}, u32[]{:S(2)}) collective-permute-start(bf16[128,1536]{1,0:T(8,128)(2,1)S(1)} %get-tuple-element.110.refs_0_), channel_id=1, source_target_pairs={{0,2},{2,4},{4,6},{6,0},{1,3},{3,5},{5,7},{7,1},{8,10},{10,12},{12... | collective-permute-start | bytes 1179656 | tf_op jit(solution)/shard_map/ppermute | solution.py:585
  98.3 25.2 %collective-permute-start.8 = (bf16[128,1536]{1,0:T(8,128)(2,1)S(1)}, bf16[128,1536]{1,0:T(8,128)(2,1)S(1)}, u32[]{:S(2)}, u32[]{:S(2)}) collective-permute-start(bf16[128,1536]{1,0:T(8,128)(2,1)S(1)} %get-tuple-element.110.refs_0_), channel_id=1, source_target_pairs={{0,4},{2,6},{4,0},{6,2},{1,5},{3,7},{5,1},{7,3},{8,12},{10,14},{12... | collective-permute-start | bytes 1179656 | tf_op jit(solution)/shard_map/ppermute | solution.py:585
  101.5 22.4 %collective-permute-start.9 = (bf16[128,1536]{1,0:T(8,128)(2,1)S(1)}, bf16[128,1536]{1,0:T(8,128)(2,1)S(1)}, u32[]{:S(2)}, u32[]{:S(2)}) collective-permute-start(bf16[128,1536]{1,0:T(8,128)(2,1)S(1)} %get-tuple-element.110.refs_0_), channel_id=1, source_target_pairs={{0,6},{2,0},{4,2},{6,4},{1,7},{3,1},{5,3},{7,5},{8,14},{10,8},{12,... | collective-permute-start | bytes 1179656 | tf_op jit(solution)/shard_map/ppermute | solution.py:585
  120.5 7.5 %collective-permute-start.10 = (bf16[128,1536]{1,0:T(8,128)(2,1)S(1)}, bf16[128,1536]{1,0:T(8,128)(2,1)S(1)}, u32[]{:S(2)}, u32[]{:S(2)}) collective-permute-start(bf16[128,1536]{1,0:T(8,128)(2,1)S(1)} %get-tuple-element.110.refs_0_), channel_id=1, source_target_pairs={{0,1},{1,0},{2,3},{3,2},{4,5},{5,4},{6,7},{7,6},{8,9},{9,8},{10,11... | collective-permute-start | bytes 1179656 | tf_op jit(solution)/shard_map/ppermute | solution.py:581
  123.4 4.6 %collective-permute-start.11 = (bf16[128,1536]{1,0:T(8,128)(2,1)S(1)}, bf16[128,1536]{1,0:T(8,128)(2,1)S(1)}, u32[]{:S(2)}, u32[]{:S(2)}) collective-permute-start(bf16[128,1536]{1,0:T(8,128)(2,1)S(1)} %collective-permute-done.7.refs_1_), channel_id=1, source_target_pairs={{0,1},{1,0},{2,3},{3,2},{4,5},{5,4},{6,7},{7,6},{8,9},{9,8},{10,11... | collective-permute-start | bytes 1179656 | tf_op jit(solution)/shard_map/ppermute | solution.py:581
  123.5 4.5 %collective-permute-start.12 = (bf16[128,1536]{1,0:T(8,128)(2,1)S(1)}, bf16[128,1536]{1,0:T(8,128)(2,1)S(1)}, u32[]{:S(2)}, u32[]{:S(2)}) collective-permute-start(bf16[128,1536]{1,0:T(8,128)(2,1)S(1)} %collective-permute-done.8.refs_2_), channel_id=1, source_target_pairs={{0,1},{1,0},{2,3},{3,2},{4,5},{5,4},{6,7},{7,6},{8,9},{9,8},{10,11... | collective-permute-start | bytes 1179656 | tf_op jit(solution)/shard_map/ppermute | solution.py:581
  123.9 4.1 %collective-permute-start.13 = (bf16[128,1536]{1,0:T(8,128)(2,1)S(1)}, bf16[128,1536]{1,0:T(8,128)(2,1)S(1)}, u32[]{:S(2)}, u32[]{:S(2)}) collective-permute-start(bf16[128,1536]{1,0:T(8,128)(2,1)S(1)} %collective-permute-done.9.refs_3_), channel_id=1, source_target_pairs={{0,1},{1,0},{2,3},{3,2},{4,5},{5,4},{6,7},{7,6},{8,9},{9,8},{10,11... | collective-permute-start | bytes 1179656 | tf_op jit(solution)/shard_map/ppermute | solution.py:581
  124.0 11.1 %all-to-all-start.4 = ((bf16[16,16,384]{2,1,0:T(8,128)(2,1)}), bf16[16,16,384]{2,1,0:T(8,128)(2,1)S(1)}, u32[]{:S(2)}, u32[]{:S(2)}) async-start(bf16[16,16,384]{2,1,0:T(8,128)(2,1)} %share.1), calls=%async_computation.4 | async-start | bytes 393216 | tf_op jit(solution)/shard_map/all_to_all | solution.py:783
  135.0 23.3 %all-to-all-start.5 = ((bf16[16,96,384]{2,1,0:T(8,128)(2,1)}), bf16[16,96,384]{2,1,0:T(8,128)(2,1)S(1)}, u32[]{:S(2)}, u32[]{:S(2)}) async-start(bf16[16,96,384]{2,1,0:T(8,128)(2,1)} %spread.1), calls=%async_computation.5 | async-start | bytes 2359296 | tf_op jit(solution)/shard_map/all_to_all | solution.py:783
  139.1 6.5 %collective-permute-start.14 = (bf16[16,16,384]{2,1,0:T(8,128)(2,1)S(1)}, bf16[16,16,384]{2,1,0:T(8,128)(2,1)S(1)}, u32[]{:S(2)}, u32[]{:S(2)}) collective-permute-start(bf16[16,16,384]{2,1,0:T(8,128)(2,1)S(1)} %all-to-all-done.4.refs_0_), channel_id=1, source_target_pairs={{0,2},{2,4},{4,6},{6,0},{1,3},{3,5},{5,7},{7,1},{8,10},{10,12},{12... | collective-permute-start | bytes 589832 | tf_op jit(solution)/shard_map/ppermute | solution.py:585
  140.8 11.1 %collective-permute-start.15 = (bf16[16,16,384]{2,1,0:T(8,128)(2,1)S(1)}, bf16[16,16,384]{2,1,0:T(8,128)(2,1)S(1)}, u32[]{:S(2)}, u32[]{:S(2)}) collective-permute-start(bf16[16,16,384]{2,1,0:T(8,128)(2,1)S(1)} %all-to-all-done.4.refs_0_), channel_id=1, source_target_pairs={{0,4},{2,6},{4,0},{6,2},{1,5},{3,7},{5,1},{7,3},{8,12},{10,14},{12... | collective-permute-start | bytes 589832 | tf_op jit(solution)/shard_map/ppermute | solution.py:585
  141.2 10.8 %collective-permute-start.16 = (bf16[16,16,384]{2,1,0:T(8,128)(2,1)S(1)}, bf16[16,16,384]{2,1,0:T(8,128)(2,1)S(1)}, u32[]{:S(2)}, u32[]{:S(2)}) collective-permute-start(bf16[16,16,384]{2,1,0:T(8,128)(2,1)S(1)} %all-to-all-done.4.refs_0_), channel_id=1, source_target_pairs={{0,6},{2,0},{4,2},{6,4},{1,7},{3,1},{5,3},{7,5},{8,14},{10,8},{12,... | collective-permute-start | bytes 589832 | tf_op jit(solution)/shard_map/ppermute | solution.py:585
  143.3 9.2 %collective-permute-start.17 = (bf16[16,16,384]{2,1,0:T(8,128)(2,1)S(1)}, bf16[16,16,384]{2,1,0:T(8,128)(2,1)S(1)}, u32[]{:S(2)}, u32[]{:S(2)}) collective-permute-start(bf16[16,16,384]{2,1,0:T(8,128)(2,1)S(1)} %all-to-all-done.4.refs_0_), channel_id=1, source_target_pairs={{0,1},{1,0},{2,3},{3,2},{4,5},{5,4},{6,7},{7,6},{8,9},{9,8},{10,11... | collective-permute-start | bytes 589832 | tf_op jit(solution)/shard_map/ppermute | solution.py:581
  145.6 7.4 %collective-permute-start.18 = (bf16[16,16,384]{2,1,0:T(8,128)(2,1)S(1)}, bf16[16,16,384]{2,1,0:T(8,128)(2,1)S(1)}, u32[]{:S(2)}, u32[]{:S(2)}) collective-permute-start(bf16[16,16,384]{2,1,0:T(8,128)(2,1)S(1)} %collective-permute-done.14.refs_1_), channel_id=1, source_target_pairs={{0,1},{1,0},{2,3},{3,2},{4,5},{5,4},{6,7},{7,6},{8,9},{9,8},{10,11... | collective-permute-start | bytes 589832 | tf_op jit(solution)/shard_map/ppermute | solution.py:581
  (2 other events, 3.2 us)
Sparse Core Ops, SparseCore 0:
  76.6 49.0 all-gather.2

commit v3 on v2

--- a/solution.py
+++ b/solution.py
@@ -30,6 +30,10 @@
     return lax.dot_general(a, b, (((1,), (1,)), ((), ())), preferred_element_type=F32)
 
 
+def dot_tt(a, b):
+    return lax.dot_general(a, b, (((0,), (1,)), ((), ())), preferred_element_type=F32)
+
+
 def dot_tn(a, b):
     return lax.dot_general(a, b, (((0,), (0,)), ((), ())), preferred_element_type=F32)
 
@@ -66,17 +70,32 @@
     return total
 
 
-def conv_backward(d_pre, v, cols, masks):
-    d_v = cols[0] * d_pre
-    taps = [jnp.sum(d_pre * v, axis=1, keepdims=True)]
-    for k in range(1, KERNEL):
-        back = pltpu.roll(d_pre * masks[k - 1], T - k, 1)
-        d_v = d_v + cols[k] * back
-        taps.append(jnp.sum(back * v, axis=1, keepdims=True))
-    return d_v, taps, jnp.sum(d_pre, axis=1, keepdims=True)
-
-
-def scan_logs(step, rate, rows_ref, segf):
+def conv_backward(dp_scr, v_ref, taps_ref, mark_scr, out_ref):
+    width = v_ref.shape[1]
+    rows = 32
+    taps = [jnp.zeros((8, width), F32) for _ in range(KERNEL + 1)]
+
+    def fold(v):
+        return jnp.sum(v.reshape(rows // 8, 8, width), axis=0)
+
+    for first in range(0, T, rows):
+        here = slice(first, first + rows)
+        v = v_ref[here, :].astype(F32)
+        d_pre = dp_scr[here, :]
+        total = taps_ref[0:1, :] * d_pre
+        taps[0] = taps[0] + fold(d_pre * v)
+        taps[KERNEL] = taps[KERNEL] + fold(d_pre)
+        for k in range(1, KERNEL):
+            mark = jnp.concatenate([mark_scr[k - 1, here, :]] * (width // 128), axis=1)
+            back = dp_scr[first + k : first + k + rows, :] * mark
+            total = total + taps_ref[k : k + 1, :] * back
+            taps[k] = taps[k] + fold(back * v)
+        out_ref[here, :] = total.astype(BF)
+    sums = [jnp.sum(tap, axis=0, keepdims=True) for tap in taps]
+    return jnp.concatenate([*sums, jnp.zeros((3, width), F32)], axis=0)
+
+
+def scan_logs(step, rate, rows_ref, segf, more=()):
     upper = (row_ids(GROUP, GROUP) <= lane_ids(GROUP, GROUP)).astype(F32)
     a = step * rate
     logs = jnp.concatenate(
@@ -85,6 +104,8 @@
     rows_ref[...] = jnp.zeros_like(rows_ref)
     rows_ref[0:8, :] = logs
     rows_ref[8:9, :] = segf
+    for k, row in enumerate(more):
+        rows_ref[9 + k : 10 + k, :] = row
     return logs, rows_ref[...].T
 
 
@@ -112,25 +133,35 @@
 
 class Source:
     def __init__(self, hbm, vmem, sem):
-        self.copy, self.ref = pltpu.make_async_copy(hbm, vmem, sem), vmem
-        self.copy.start()
-        self.waits = True
+        self.ref, self.waits = vmem, True
+        if isinstance(sem, list):
+            rows = vmem.shape[0] // len(sem)
+            parts = [slice(k * rows, (k + 1) * rows) for k in range(len(sem))]
+            self.copies = [
+                pltpu.make_async_copy(hbm.at[part], vmem.at[part], one)
+                for part, one in zip(parts, sem)
+            ]
+        else:
+            self.copies = [pltpu.make_async_copy(hbm, vmem, sem)]
+        for copy in self.copies:
+            copy.start()
 
     def __call__(self):
         if self.waits:
-            self.copy.wait()
+            for copy in self.copies:
+                copy.wait()
             self.waits = False
         return self.ref
 
 
 class Target:
     def __init__(self, hbm, vmem, sem):
-        self.copy, self.ref = pltpu.make_async_copy(vmem, hbm, sem), vmem
-        self.sent = False
+        self.hbm, self.ref, self.sem = hbm, vmem, sem
+        self.copies = []
 
     def put(self):
-        self.copy.start()
-        self.sent = True
+        self.copies.append(pltpu.make_async_copy(self.ref, self.hbm, self.sem))
+        self.copies[-1].start()
 
 
 def sds(shape, dtype):
@@ -157,8 +188,9 @@
 
 def call(
     body, outs, args, scratch=(), name=None, near=(), free=(), near_out=(), free_out=(), us=0.0,
-    vmem=40,
+    vmem=40, into=None, twin=None, split=None,
 ):
+    into, twin = into or {}, twin or {}
     n, m = len(args) - 1, len(outs)
     where = [NEAR if k in near else FREE if k in free else FAR for k in range(n)]
     where_out = [NEAR if k in near_out else FREE if k in free_out else FAR for k in range(m)]
@@ -167,30 +199,38 @@
 
     def kernel(idx_ref, *refs):
         ins, results, rest = refs[:n], refs[n : n + m], refs[n + m :]
-        buffers, rest = rest[: len(far)], rest[len(far) :]
-        out_buffers, rest = rest[: len(far_out)], rest[len(far_out) :]
-        in_sems, out_sems, *own = rest
+        *buffers, in_sems, out_sems = rest[: count + 2]
+        own = rest[count + 2 :]
         sources, targets = [Here(ref) for ref in ins], [Here(ref) for ref in results]
         for j, k in enumerate(far):
-            sources[k] = Source(ins[k], buffers[j], in_sems.at[j])
+            buffer = results[into[k]] if k in into else buffers.pop(0)
+            sem = in_sems.at[j]
+            if k == split:
+                sem = [sem, *[in_sems.at[len(far) + i] for i in range(3)]]
+            sources[k] = Source(ins[k], buffer, sem)
         for j, k in enumerate(far_out):
-            targets[k] = Target(results[k], out_buffers[j], out_sems.at[j])
+            buffer = results[twin[k]] if k in twin else buffers.pop(0)
+            targets[k] = Target(results[k], buffer, out_sems.at[j])
         body(idx_ref, sources, targets, *own)
         for source in sources:
             source()
         for k in far_out:
-            if not targets[k].sent:
+            if not targets[k].copies:
                 targets[k].put()
         for k in far_out:
-            targets[k].copy.wait()
-
-    buffers = [pltpu.VMEM(args[1 + k].shape, args[1 + k].dtype) for k in far]
-    buffers += [pltpu.VMEM(outs[k].shape, outs[k].dtype) for k in far_out]
-    sems = [pltpu.SemaphoreType.DMA((max(len(v), 1),)) for v in (far, far_out)]
+            for copy in targets[k].copies:
+                copy.wait()
+
+    buffers = [pltpu.VMEM(args[1 + k].shape, args[1 + k].dtype) for k in far if k not in into]
+    buffers += [pltpu.VMEM(outs[k].shape, outs[k].dtype) for k in far_out if k not in twin]
+    count = len(buffers)
+    sems = [pltpu.SemaphoreType.DMA((len(v) + 4,)) for v in (far, far_out)]
     return launch(kernel, outs, args, [*buffers, *sems, *scratch], name, where, where_out, us, vmem)
 
 
-def launch(kernel, outs, args, scratch, name, where, where_out, us=0.0, vmem=40):
+def launch(
+    kernel, outs, args, scratch, name, where, where_out, us=0.0, vmem=40, aliases=None
+):
     return pl.pallas_call(
         kernel,
         out_shape=[v if w is FREE else w(v.shape, v.dtype) for v, w in zip(outs, where_out)],
@@ -198,6 +238,7 @@
         + [pl.BlockSpec(memory_space=w) for w in where],
         out_specs=[pl.BlockSpec(memory_space=w) for w in where_out],
         scratch_shapes=scratch,
+        input_output_aliases=aliases or {},
         compiler_params=pltpu.CompilerParams(vmem_limit_bytes=vmem << 20),
         cost_estimate=pl.CostEstimate(
             flops=int(us * 1e9) + 1000, bytes_accessed=1000, transcendentals=0
@@ -206,7 +247,7 @@
     )(args[0], *[pinned(v, w) for v, w in zip(args[1:], where)])
 
 
-SPREAD_US, WIDEN_US, REDUCE_US, INPUT_US = 0.0, 20.0, 0.0, 20.0
+SPREAD_US, WIDEN_US, FINISH_US, INPUT_US = 0.0, 0.0, 20.0, 10.0
 
 
 def fwd_kernel(idx_ref, sources, targets, rows_scr, par_scr, u_scr, inner_scr):
@@ -216,19 +257,21 @@
     ) = sources
     (
         normed_ref, gate_ref, inner_ref, pre_ref, mixed_ref, dno_ref, states_ref, spre_ref,
-        raw_ref, cols_ref, scols_ref, head_ref, sums_ref, x_part_ref, cot_part_ref,
+        raw_ref, cols_ref, scols_ref, head_ref, sums_ref, x_part_ref, cot_part_ref, _, _,
     ) = [target.ref for target in targets]
     par_scr[...] = jnp.zeros_like(par_scr)
-    nw_ref, x_ref = nw_in(), x_in()
-
-    def norm_block(r, _):
-        sl = pl.ds(r * 64, 64)
+    nw_ref, x_ref = nw_in(), x_in.ref
+
+    def norm_block(r):
+        sl = slice(r * 128, (r + 1) * 128)
+        x_in.copies[r].wait()
         v = x_ref[sl, :].astype(F32)
         scale = lax.rsqrt(jnp.mean(v * v, axis=1, keepdims=True) + EPS)
         normed_ref[sl, :] = (v * scale * nw_ref[...].reshape(1, D)).astype(BF)
-        return 0
-
-    lax.fori_loop(0, T // 64, norm_block, 0)
+
+    for r in range(T // 128):
+        norm_block(r)
+    x_in.waits = False
     own = pl.ds(pl.multiple_of(idx_ref[0] * GROUP + idx_ref[1] * 64, 64), 64)
     x_part_ref[...] = x_ref[own, :]
     targets[0].put()
@@ -251,11 +294,11 @@
     )
     segf = seg_in()[...].astype(F32)
     raw_ref[8:16, :] = jnp.broadcast_to(segf, (8, T))
-    inner_scr[...] = dot(normed, ip_in()[...]).T
-    inner_ref[...] = inner_scr[...].astype(BF)
-    states = dot(normed, sp_in()[...]).T
-    states_ref[...] = states.astype(BF)
-    gate_ref[...] = dot(normed, gp_in()[...]).T
+    inner_scr[...] = dot_tt(ip_in()[...], normed)
+    inner_ref[...] = inner_scr[...].astype(BF).T
+    states = dot_tt(sp_in()[...], normed)
+    states_ref[...] = states.astype(BF).T
+    gate_ref[...] = dot_tt(gp_in()[...], normed)
     for k in (1, 2, 6, 8, 9, 10, 11):
         targets[k].put()
     cot_ref = cot_in()
@@ -320,21 +363,25 @@
 
 def forward(*args):
     outs = [
-        sds((T, D), BF), sds((C, T), F32), sds((C, T), BF), sds((C, T), F32), sds((C, T), F32),
-        sds((C, T), F32), sds((256, T), BF), sds((256, T), F32), sds((16, T), F32),
+        sds((T, D), BF), sds((C, T), F32), sds((T, C), BF), sds((C, T), F32), sds((C, T), F32),
+        sds((C, T), F32), sds((T, 256), BF), sds((256, T), F32), sds((16, T), F32),
         sds((C, 8), F32), sds((256, 8), F32), sds((8, 128), F32), sds((8, 2, T), F32),
-        sds((64, D), BF), sds((64, D), BF),
+        sds((64, D), BF), sds((64, D), BF), sds((T, D), BF), sds((T, D), BF),
     ]
     scratch = [
         pltpu.VMEM((128, T), F32), pltpu.VMEM((128, 640), F32), pltpu.VMEM((C, T), F32),
         pltpu.VMEM((C, T), F32),
     ]
-    return call(fwd_kernel, outs, args, scratch, "forward", near_out=(1, 4, 5))
-
-
-def mid_kernel(idx_ref, sources, targets, no_scr, low_scr):
+    return call(
+        fwd_kernel, outs, args, scratch, "forward", near_out=(1, 4, 5, 15, 16), into={16: 16},
+        twin={0: 15}, split=0,
+    )
+
+
+def mid_kernel(idx_ref, sources, targets, no_scr, low_scr, out_scr, gate_scr, sems):
     sums_in, gate_in, mixed_in, dno_in, cols_in, cot_in, normed_in = sources
-    grads_ref, no_ref, gate_low_ref, dy_ref, gain_ref = [t.ref for t in targets]
+    _, no_ref, gate_low_ref, dy_ref, gain_ref = [t.ref for t in targets]
+    grads = targets[0]
     total = jnp.sum(sums_in()[...], axis=0)
     scale = lax.rsqrt(total[0:1, :] / INNER + EPS)
     slope = scale * scale * scale * (total[1:2, :] / INNER)
@@ -355,44 +402,59 @@
         low_scr[hs, :] = (d_gated * mixed * (s * (1.0 + g * (1.0 - s)))).astype(BF)
         dy_ref[hs, :] = (d_gated * silu).astype(BF)
     targets[3].put()
-    out_grad = dot(no_scr[...], cot_in()[...]).astype(BF)
-    for k in range(16):
-        rows, columns = slice(k % 4 * 96, (k % 4 + 1) * 96), slice(k // 4 * C, (k // 4 + 1) * C)
-        grads_ref[k, 96:192, :] = out_grad[rows, columns]
-    gate_grad = dot(low_scr[...], normed_in()[...]).T.astype(BF)
-    for k in range(16):
-        grads_ref[k, 0:96, :] = gate_grad[k * 96 : (k + 1) * 96, :]
-    targets[0].put()
+    out_scr[...] = dot(no_scr[...], cot_in()[...]).astype(BF).reshape(4, 96, D)
+    for k in range(4):
+        source = out_scr.at[:, :, k * C : (k + 1) * C]
+        grads.copies.append(
+            pltpu.make_async_copy(source, grads.hbm.at[4 * k : 4 * k + 4, 96:192], sems.at[k])
+        )
+        grads.copies[-1].start()
     no_ref[...] = no_scr[...].T
     gate_low_ref[...] = low_scr[...].T
+    targets[1].put()
+    targets[2].put()
+    gate_scr[...] = dot(low_scr[...], normed_in()[...]).T.astype(BF).reshape(16, 96, C)
+    grads.copies.append(pltpu.make_async_copy(gate_scr, grads.hbm.at[:, 0:96], sems.at[4]))
+    grads.copies[-1].start()
 
 
 def middle(*args):
     outs = [
         sds((16, 192, C), BF), sds((T, C), BF), sds((T, C), BF), sds((C, T), BF), sds((C, 8), F32),
     ]
-    scratch = [pltpu.VMEM((C, T), BF), pltpu.VMEM((C, T), BF)]
-    return call(mid_kernel, outs, args, scratch, "middle", near=(1, 2, 3), free=(0,))
+    scratch = [
+        pltpu.VMEM((C, T), BF), pltpu.VMEM((C, T), BF), pltpu.VMEM((4, 96, D), BF),
+        pltpu.VMEM((16, 96, C), BF), pltpu.SemaphoreType.DMA((5,)),
+    ]
+    return call(mid_kernel, outs, args, scratch, "middle", near=(1, 2, 3, 5, 6), free=(0,))
 
 
 def bwd_kernel(
-    idx_ref, sources, targets, rows_scr, u_scr, di_scr, low_scr, cs_scr, slow_scr, tpad, pad_scr,
-    grad_scr, tok_scr, low_tok, step_tok, give_scr,
+    idx_ref, sources, targets, rows_scr, u_scr, di_scr, mark_scr, cs_scr, dp_scr, tpad, dps_scr,
+    grad_scr, tok_scr, low_tok, step_tok, give_scr, inner_scr,
 ):
     (
-        raw_in, head_in, spre_in, pre_in, dy_in, cols_in, inner_in, normed_in, scols_in,
+        raw_in, head_in, spre_in, pre_in, dy_in, ic_in, inner_in, normed_in, sc_in,
         states_in, gate_low_in, sp_in, tp_in, gp_in, ip_in, no_in, op_in,
     ) = sources
-    inner_grad_ref, keep_ref, extra_ref, *gives = [t.ref for t in targets]
+    _, keep_ref, keep_state_ref, extra_ref, give_state_ref, *gives = [
+        t.ref for t in targets
+    ]
     core = idx_ref[0]
     raw_ref, head_ref, spre_ref = raw_in(), head_in(), spre_in()
     segf = raw_ref[8:9, :]
-    masks = conv_masks(segf)
+    later = [
+        ((pltpu.roll(segf, T - k, 1) == segf) & (lane_ids(1, T) < T - k)).astype(F32)
+        for k in range(1, KERNEL)
+    ]
     head = head_ref[...]
     raw = raw_ref[0:8, :] + head[:, 8:9]
     step = softplus(raw)
     rate = -jnp.exp(head[:, 9:10])
-    logs, lcols = scan_logs(step, rate, rows_scr, segf)
+    logs, lcols = scan_logs(step, rate, rows_scr, segf, later)
+    marks = [jnp.broadcast_to(lcols[:, 9 + k : 10 + k], (T, 128)) for k in range(3)]
+    for k in range(3):
+        mark_scr[k] = marks[k]
     spre = spre_ref[...]
     cs = spre * sigmoid(spre)
     b_low = cs[0:N, :].astype(BF)
@@ -450,7 +512,7 @@
             d_c = d_c + d_c_second
         cs_scr[0:N, sl] = d_b
         cs_scr[N:, sl] = d_c
-    cols_ref, inner_ref, normed_ref = cols_in(), inner_in(), normed_in()
+    ic_ref, inner_ref, normed_ref = ic_in(), inner_in(), normed_in()
     zero = jnp.zeros((1, GROUP), F32)
     q_rows, e_rows = [], []
     for h in range(NH):
@@ -465,7 +527,6 @@
     da1 = jnp.concatenate([da_rows[h][1] for h in range(NH)] + [zero, zero], axis=0)
     da = jnp.concatenate([da0 + dot(q8, upto, EXACT), da1 + dot(e8, since, EXACT)], axis=1)
     d_steps = []
-    pad_scr[...] = jnp.zeros_like(pad_scr)
     for h in range(NH):
         hs = slice(h * HD, (h + 1) * HD)
         pre = pre_ref[hs, :]
@@ -477,58 +538,48 @@
         out_skip.append(jnp.sum(dy * u, axis=0, keepdims=True))
         d_u = di * step[h : h + 1, :] + head[h : h + 1, 10:11] * dy
         d_pre = d_u * (s * (1.0 + pre * (1.0 - s)))
-        d_v, taps, bias = conv_backward(
-            d_pre, inner_ref[hs, :].astype(F32),
-            [cols_ref[hs, k : k + 1] for k in range(KERNEL)], masks,
-        )
-        low_scr[hs, :] = d_v.astype(BF)
-        for k in range(KERNEL):
-            pad_scr[hs, k : k + 1] = taps[k]
-        pad_scr[hs, 4:5] = bias
+        di_scr[hs, :] = d_pre
     zero = jnp.zeros((2, T), F32)
     d_step = jnp.concatenate(d_steps + [zero], axis=0) + da * rate
     skips = jnp.concatenate(out_skip + [zero], axis=0)
     d_raw = d_step * sigmoid(raw)
-    inner_grad_ref[...] = dot(low_scr[...], normed_ref[...]).T.astype(BF)
-    targets[0].put()
+    dp_scr[0:T, :] = di_scr[...].T
+    dp_scr[T:, :] = jnp.zeros((8, C), F32)
+    rows = conv_backward(dp_scr, inner_ref, ic_ref, mark_scr, low_tok)
+    inner_grad = dot_tn(normed_ref[...], low_tok[...]).astype(BF)
+    inner_scr[...] = inner_grad.reshape(16, 96, C)
+    buffer = targets[0]
+    buffer.copies.append(pltpu.make_async_copy(inner_scr, buffer.hbm.at[:, 0:96], buffer.sem))
+    buffer.copies[-1].start()
     rows_scr[...] = jnp.zeros_like(rows_scr)
     rows_scr[0:8, :] = d_raw
     step_tok[...] = rows_scr[...].T.astype(BF)
     extra_ref[0:8, :] = dot(d_raw.astype(BF), normed_ref[...])
-    scols_ref, states_ref = scols_in(), states_in()
+    sc_ref, states_ref = sc_in(), states_in()
     for part in range(4):
         rs = slice(part * 64, (part + 1) * 64)
-        ps = slice(C + part * 64, C + (part + 1) * 64)
         pre = spre_ref[rs, :]
         s = sigmoid(pre)
-        d_pre = cs_scr[rs, :] * (s * (1.0 + pre * (1.0 - s)))
-        d_v, taps, bias = conv_backward(
-            d_pre, states_ref[rs, :].astype(F32),
-            [scols_ref[rs, k : k + 1] for k in range(KERNEL)], masks,
-        )
-        slow_scr[rs, :] = d_v.astype(BF)
-        for k in range(KERNEL):
-            pad_scr[ps, k : k + 1] = taps[k]
-        pad_scr[ps, 4:5] = bias
-    rows = pad_scr[...].T[0:8, :]
+        cs_scr[rs, :] = cs_scr[rs, :] * (s * (1.0 + pre * (1.0 - s)))
+    dps_scr[0:T, :] = cs_scr[...].T
+    dps_scr[T:, :] = jnp.zeros((8, 256), F32)
+    state_rows_ = conv_backward(dps_scr, states_ref, sc_ref, mark_scr, tok_scr)
     columns = [
         jnp.sum(d_raw, axis=1, keepdims=True), jnp.sum(da * step, axis=1, keepdims=True) * rate,
         jnp.sum(skips, axis=1, keepdims=True), jnp.zeros((8, 125), F32),
     ]
     extra_ref[8:16, :] = jnp.concatenate(
-        [rows[:, 0:C], *columns, jnp.zeros((8, D - C - 128), F32)], axis=1
-    )
-    targets[2].put()
+        [rows, *columns, jnp.zeros((8, D - C - 128), F32)], axis=1
+    )
+    targets[3].put()
     taps = jnp.concatenate(
         [
-            jnp.concatenate([rows[:, C:], jnp.zeros((8, D - 256), F32)], axis=1),
+            jnp.concatenate([state_rows_, jnp.zeros((8, D - 256), F32)], axis=1),
             jnp.zeros((8, D), F32),
         ],
         axis=0,
     ).astype(BF)
-    tok_scr[...] = slow_scr[...].T
-    low_tok[...] = low_scr[...].T
-    grad_scr[...] = dot(slow_scr[...], normed_ref[...]).astype(BF)
+    grad_scr[...] = dot_tn(tok_scr[...], normed_ref[...]).astype(BF)
     tpad[...] = jnp.zeros_like(tpad)
     tpad[0:NH, :] = tp_in()[...]
     gate_low_ref, no_ref = gate_low_in(), no_in()
@@ -543,38 +594,51 @@
         for k in range(4):
             slot = lax.rem(k + 4 - idx_ref[1], 4)
             rows = pl.ds(pl.multiple_of(half * 128 + k * 32, 32), 32)
-            ref = give_scr if give else keep_ref
+            ref, state_ref = (give_scr, give_state_ref) if give else (keep_ref, keep_state_ref)
             ref[slot, 0:64, :] = total[k * 64 : (k + 1) * 64, :]
-            ref[slot, 64:96, :] = grad_scr[rows, :]
-            ref[slot, 96:112, :] = taps
-            ref[slot, 112:176, :] = out[k * 64 : (k + 1) * 64, :]
+            ref[slot, 64:128, :] = out[k * 64 : (k + 1) * 64, :]
+            state_ref[slot, 0:32, :] = grad_scr[rows, :]
+            state_ref[slot, 32:48, :] = taps
         if give:
             for k in range(4):
                 gives[k][...] = give_scr[k]
 
 
 def backward(*args):
-    outs = [sds((D, C), BF), sds((4, 176, D), BF), sds((16, D), F32), *[sds((176, D), BF)] * 4]
+    outs = [
+        sds((16, 112, C), BF), sds((4, 128, D), BF), sds((4, 48, D), BF), sds((16, D), F32),
+        sds((4, 48, D), BF), *[sds((128, D), BF)] * 4,
+    ]
     scratch = [
         pltpu.VMEM((128, T), F32), pltpu.VMEM((C, T), F32), pltpu.VMEM((C, T), F32),
-        pltpu.VMEM((C, T), BF), pltpu.VMEM((256, T), F32), pltpu.VMEM((256, T), BF),
-        pltpu.VMEM((128, D), BF), pltpu.VMEM((C + 256, 128), F32), pltpu.VMEM((256, D), BF),
+        pltpu.VMEM((3, T, 128), F32), pltpu.VMEM((256, T), F32), pltpu.VMEM((T + 8, C), F32),
+        pltpu.VMEM((128, D), BF), pltpu.VMEM((T + 8, 256), F32), pltpu.VMEM((256, D), BF),
         pltpu.VMEM((T, 256), BF), pltpu.VMEM((T, C), BF), pltpu.VMEM((T, 128), BF),
-        pltpu.VMEM((4, 176, D), BF),
-    ]
-    return call(bwd_kernel, outs, args, scratch, "backward", near_out=(1, 3, 4, 5, 6))
-
-
-def fold_kernel(idx_ref, keep, g0, g1, g2, g3, own_hbm, s1, s2, s3, own, sem):
-    for k in (0, 1, 2, 3):
-        total = keep[k].astype(F32) + (g0, g1, g2, g3)[k][...].astype(F32)
-        if k == 0:
-            own[...] = total
-            store = pltpu.make_async_copy(own, own_hbm, sem)
-            store.start()
-        else:
-            (s1, s2, s3)[k - 1][...] = total.astype(BF)
-    store.wait()
+        pltpu.VMEM((4, 128, D), BF), pltpu.VMEM((16, 96, C), BF),
+    ]
+    return call(
+        bwd_kernel, outs, args, scratch, "backward",
+        near_out=(1, 2, 4, 5, 6, 7, 8),
+    )
+
+
+def fold_kernel(idx_ref, *refs):
+    keep, keep_state, got_state, *got = refs[:7]
+    own_hbm, own_state_hbm, *sends = refs[7:15]
+    own, own_state, sems = refs[15:]
+    stores = [
+        pltpu.make_async_copy(own_state, own_state_hbm, sems.at[0]),
+        pltpu.make_async_copy(own, own_hbm, sems.at[1]),
+    ]
+    own[...] = keep[0].astype(F32) + got[0][...].astype(F32)
+    stores[1].start()
+    own_state[...] = keep_state[0].astype(F32) + got_state[0].astype(F32)
+    stores[0].start()
+    for k in range(1, 4):
+        sends[k - 1][...] = (keep_state[k].astype(F32) + got_state[k].astype(F32)).astype(BF)
+        sends[k + 2][...] = (keep[k].astype(F32) + got[k][...].astype(F32)).astype(BF)
+    for store in stores:
+        store.wait()
 
 
 def swap(v):
@@ -585,19 +649,25 @@
     return lax.ppermute(v, axis, [(i, (i + by) % 4) for i in range(4)])
 
 
-def scatter(idx, gives, keep):
-    _, rows, width = keep.shape
-    outs = [sds((rows, width), F32)] + [sds((rows, width), BF)] * 3
-    scratch = [pltpu.VMEM((rows, width), F32), pltpu.SemaphoreType.DMA(())]
-    own, *sends = launch(
-        fold_kernel, outs, (idx, keep, *map(swap, gives)), scratch, "fold", [NEAR] * 5,
-        [FAR, NEAR, NEAR, NEAR], vmem=16,
-    )
-    return [own] + [turn(send, "y", k + 1) for k, send in enumerate(sends)]
-
-
-def gather(chunk, *earlier):
-    pieces = [chunk] + [turn(chunk, "y", k) for k in range(1, 4)]
+def scatter(idx, keep, keep_state, give_state, gives):
+    rows, state_rows = sds((128, D), BF), sds((48, D), BF)
+    outs = [sds((128, D), F32), sds((48, D), F32), *[state_rows] * 3, *[rows] * 3]
+    scratch = [
+        pltpu.VMEM((128, D), F32), pltpu.VMEM((48, D), F32), pltpu.SemaphoreType.DMA((2,)),
+    ]
+    own, own_state, *sends = launch(
+        fold_kernel, outs, (idx, keep, keep_state, swap(give_state), *map(swap, gives)), scratch,
+        "fold", [NEAR] * 7, [FAR] * 2 + [NEAR] * 6, vmem=16,
+    )
+    sends = [turn(send, "y", k % 3 + 1) for k, send in enumerate(sends)]
+    return [own_state, *sends[:3]], [own, *sends[3:]]
+
+
+def spread_out(chunk):
+    return [chunk] + [turn(chunk, "y", k) for k in range(1, 4)]
+
+
+def gather(pieces, *earlier):
     return pieces + [swap(after(piece, *earlier)) for piece in pieces]
 
 
@@ -665,10 +735,42 @@
     sk_ref[...] = heads[2:3, 0:NH].reshape(NH)
 
 
-def input_kernel(idx_ref, sources, targets, pad_scr):
-    x_ref, cot_ref, nw_ref, extra_ref, gain_ref = [source() for source in sources[:5]]
-    chunk_ref, pack_ref = [t.ref for t in targets]
-    p0, p1, p2, p3 = [source() for source in sources[5:]]
+def pack_kernel(idx_ref, *refs):
+    buf_hbm, own_any, p1_any, p2_any, p3_any, extra_hbm, gain_hbm, out_hbm = refs[:8]
+    own, parts, extra, gain, pad, blocks, sems = refs[8:]
+    loads = [
+        pltpu.make_async_copy(source, target, sems.at[k])
+        for k, (source, target) in enumerate(
+            (
+                (own_any, own), (p1_any, parts.at[0]), (p2_any, parts.at[1]),
+                (p3_any, parts.at[2]), (extra_hbm, extra), (gain_hbm, gain),
+            )
+        )
+    ]
+    for load in loads:
+        load.start()
+    for load in loads:
+        load.wait()
+    total = (own[...] + parts[0].astype(F32)) + (parts[1].astype(F32) + parts[2].astype(F32))
+    pad[...] = jnp.zeros_like(pad)
+    pad[:, 5:6] = gain[:, 0:1]
+    gain_row = jnp.concatenate([pad[...].T[0:8, :], jnp.zeros((8, D - C), F32)], axis=1)
+    rows = [
+        total[0:16, :], total[16:32, :],
+        jnp.concatenate([total[32:40, :], jnp.zeros((8, D), F32)], axis=0),
+        jnp.concatenate([extra[0:8, :], extra[8:16, :] + gain_row], axis=0),
+    ]
+    for k in range(16):
+        blocks[k] = rows[k % 4][:, k // 4 * C : (k // 4 + 1) * C].astype(BF)
+    store = pltpu.make_async_copy(blocks, out_hbm.at[:, 96:112], sems.at[6])
+    store.start()
+    store.wait()
+
+
+def input_kernel(idx_ref, sources, targets):
+    x_ref, cot_ref, nw_ref = [source() for source in sources[:3]]
+    chunk_ref, norm_ref = [t.ref for t in targets]
+    p0, p1, p2, p3 = [source() for source in sources[3:]]
     total = (p0[...] + p1[...].astype(F32)) + (p2[...].astype(F32) + p3[...].astype(F32))
     d_normed = total[0:64, :]
     v = x_ref[...].astype(F32)
@@ -678,24 +780,27 @@
         scale * scale * scale * jnp.mean(weighted * v, axis=1, keepdims=True)
     )
     chunk_ref[0:64, :] = (cot_ref[...].astype(F32) + grad).astype(BF)
-    chunk_ref[64:128, :] = (v + total[112:176, :]).astype(BF)
+    chunk_ref[64:128, :] = (v + total[64:128, :]).astype(BF)
     targets[0].put()
-    norm = jnp.broadcast_to(jnp.sum(d_normed * v * scale, axis=0, keepdims=True), (8, D))
-    pad_scr[...] = jnp.zeros_like(pad_scr)
-    pad_scr[:, 5:6] = gain_ref[:, 0:1]
-    gain = jnp.concatenate([pad_scr[...].T[0:8, :], jnp.zeros((8, D - C), F32)], axis=1)
-    rows = [
-        total[64:80, :], total[80:96, :], jnp.concatenate([total[96:104, :], norm], axis=0),
-        jnp.concatenate([extra_ref[0:8, :], extra_ref[8:16, :] + gain], axis=0),
-    ]
+    norm = jnp.sum(d_normed * v * scale, axis=0, keepdims=True)
+    rows = [norm[:, k * C : (k + 1) * C] for k in range(4)]
+    norm_ref[...] = jnp.concatenate([*rows, jnp.zeros((12, C), F32)], axis=0).astype(BF)
+
+
+def share_kernel(idx_ref, sources, targets):
+    parts_ref, out_ref = sources[0](), targets[0].ref
+    norm = parts_ref[0, 16:32, :].astype(F32)
+    for k in range(1, 16):
+        norm = norm + parts_ref[k, 16:32, :].astype(F32)
     for k in range(16):
-        pack_ref[k] = rows[k % 4][:, k // 4 * C : (k // 4 + 1) * C].astype(BF)
-
-
-def share_kernel(idx_ref, sources, targets):
-    total = total_of(sources[0]())
-    for k in range(16):
-        targets[0].ref[k] = total
+        if k % 4 == 2:
+            row = jnp.concatenate(
+                [jnp.zeros((8, C), F32), norm[k // 4 : k // 4 + 1, :], jnp.zeros((7, C), F32)],
+                axis=0,
+            )
+            out_ref[k] = (parts_ref[k, 0:16, :].astype(F32) + row).astype(BF)
+        else:
+            out_ref[k] = parts_ref[k, 0:16, :]
 
 
 def total_of(parts_ref):
@@ -709,33 +814,60 @@
     targets[0].ref[...] = total_of(sources[0]())
 
 
-def spread_kernel(idx_ref, parts_hbm, out_hbm, parts, own, sem, sems):
-    load = pltpu.make_async_copy(parts_hbm, parts, sem)
+def spread_kernel(
+    idx_ref, terms_any, first_any, norm_any, small_hbm, wide_hbm, terms, first, norm, own, small,
+    load_sems, sems,
+):
+    pairs = [(terms_any.at[4 * k : 4 * k + 4], terms.at[4 * k : 4 * k + 4]) for k in range(4)]
+    pairs += [(first_any, first), (norm_any, norm)]
+    loads = [
+        pltpu.make_async_copy(source, target, load_sems.at[k])
+        for k, (source, target) in enumerate(pairs)
+    ]
+    for load in loads:
+        load.start()
+    total = jnp.zeros((112, C), F32)
+    for k in range(4):
+        loads[k].wait()
+        part = terms[4 * k].astype(F32)
+        for j in range(1, 4):
+            part = part + terms[4 * k + j].astype(F32)
+        total = total + part
+    own[...] = total.astype(BF)
+    loads[4].wait()
+    stores = [
+        pltpu.make_async_copy(own.at[0:96], wide_hbm.at[k, 192:288], sems.at[k])
+        for k in range(4)
+    ]
+    stores += [
+        pltpu.make_async_copy(first, wide_hbm.at[k, 0:192], sems.at[4 + k]) for k in range(4)
+    ]
+    for store in stores:
+        store.start()
+    loads[5].wait()
+    both = jnp.concatenate([own[96:112, :], norm[...]], axis=0)
+    for k in range(16):
+        small[k] = both
+    stores.append(pltpu.make_async_copy(small, small_hbm, sems.at[8]))
+    stores[-1].start()
+    for store in stores:
+        store.wait()
+
+
+def again_kernel(idx_ref, blocks_any, out_hbm, blocks, load_sem, sems):
+    load = pltpu.make_async_copy(blocks_any, blocks, load_sem)
     load.start()
     load.wait()
-    own[...] = total_of(parts)
-    stores = [pltpu.make_async_copy(own, out_hbm.at[k], sems.at[k]) for k in range(16)]
+    stores = [pltpu.make_async_copy(blocks, out_hbm.at[k], sems.at[k]) for k in range(4)]
     for store in stores:
         store.start()
     for store in stores:
         store.wait()
 
 
-def widen_kernel(idx_ref, hbm, wide_hbm, buf, wide, in_sems, out_sems):
-    loads = [pltpu.make_async_copy(hbm.at[k], buf.at[k], in_sems.at[k]) for k in range(4)]
-    for load in loads:
-        load.start()
-    stores = []
-    for k in range(4):
-        loads[k].wait()
-        wide[k] = buf[k].astype(F32)
-        stores.append(pltpu.make_async_copy(wide.at[k], wide_hbm.at[k], out_sems.at[k]))
-        stores[-1].start()
-    for store in stores:
-        store.wait()
-
-
-def widen_two_kernel(idx_ref, hbm, out_hbm, gate_hbm, buf, out, gate, in_sems, out_sems):
+def widen_kernel(
+    idx_ref, hbm, gate_hbm, out_hbm, inner_hbm, buf, gate, out, inner, in_sems, out_sems
+):
     loads = [pltpu.make_async_copy(hbm.at[k], buf.at[k], in_sems.at[k]) for k in range(4)]
     for load in loads:
         load.start()
@@ -745,15 +877,45 @@
         for j in range(4):
             gate[k, j] = buf[k, j, 0:96, :].astype(F32)
             out[k, j * 96 : (j + 1) * 96, :] = buf[k, j, 96:192, :].astype(F32)
+            inner[k, j] = buf[k, j, 192:288, :].astype(F32)
         columns = slice(k * C, (k + 1) * C)
-        stores.append(pltpu.make_async_copy(gate.at[k], gate_hbm.at[k], out_sems.at[0, k]))
-        stores.append(
-            pltpu.make_async_copy(out.at[k], out_hbm.at[:, columns], out_sems.at[1, k])
-        )
-        stores[-2].start()
-        stores[-1].start()
+        for j, (source, target) in enumerate(
+            (
+                (gate.at[k], gate_hbm.at[k]), (out.at[k], out_hbm.at[:, columns]),
+                (inner.at[k], inner_hbm.at[k]),
+            )
+        ):
+            stores.append(pltpu.make_async_copy(source, target, out_sems.at[j, k]))
+            stores[-1].start()
     for store in stores:
         store.wait()
+
+
+def flat(z, x, y, core):
+    return ((z * 4 + x) * 4 + y) * 2 + core
+
+
+def teams(kind):
+    out = []
+    for core in range(2):
+        for y in range(4):
+            grid = [
+                [flat(b, a, y, 0) if core == 0 else flat(a, b, y, 1) for b in range(4)]
+                for a in range(4)
+            ]
+            if kind == "both":
+                out.append([place for row in grid for place in row])
+            elif kind == "second":
+                out.extend(grid)
+            else:
+                out.extend([list(column) for column in zip(*grid)])
+    return out
+
+
+def exchange(v, kind):
+    return lax.all_to_all(
+        v, ("z", "x", "y", "core"), 0, 0, axis_index_groups=teams(kind), tiled=True
+    )
 
 
 def after(idx, *values):
@@ -770,58 +932,71 @@
     idx = jnp.stack([lax.axis_index(a) for a in ("core", "y", "x", "z")]).astype(jnp.int32)
     (
         normed, gate, inner, pre, mixed, dno, states, spre, raw, cols, scols, head, sums, x_part,
-        cot_part,
+        cot_part, normed_here, cot_here,
     ) = forward(
         idx, x, norm_weight, inner_conv, inner_conv_bias, state_conv, state_conv_bias, step_bias,
         decay_log, skip_weight, gated_norm_weight, segments, step_rows, inner_proj, state_proj,
         gate_proj, out_proj, cot,
     )
     sums = lax.all_to_all(sums, ("y", "core"), 0, 0, tiled=True)
-    grads, no, gate_low, dy, gain = middle(idx, sums, gate, mixed, dno, cols, cot, normed)
-
-    def dp_terms(v):
-        return lax.all_to_all(v, ("x", "z"), 0, 0, tiled=True)
-
-    first_terms = dp_terms(grads)
-    inner_grad, keep, extra, *gives = backward(
-        idx, raw, head, spre, pre, dy, cols, inner, normed, scols, states, gate_low, state_proj,
+    grads, no, gate_low, dy, gain = middle(
+        idx, sums, gate, mixed, dno, cols, cot_here, normed_here
+    )
+
+    first_terms = exchange(grads, "both")
+    inner_grad, keep, keep_state, extra, give_state, *gives = backward(
+        idx, raw, head, spre, pre, dy, inner_conv, inner, normed, state_conv, states, gate_low, state_proj,
         step_rows, gate_proj, inner_proj, no, out_proj,
     )
-    pieces = scatter(idx, gives, keep)
+    state_pieces, pieces = scatter(idx, keep, keep_state, give_state, gives)
+    (terms,) = launch(
+        pack_kernel, [sds((16, 112, C), BF)], (idx, inner_grad, *state_pieces, extra, gain),
+        [
+            pltpu.VMEM((48, D), F32), pltpu.VMEM((3, 48, D), BF), pltpu.VMEM((16, D), F32),
+            pltpu.VMEM((C, 8), F32), pltpu.VMEM((C, 128), F32), pltpu.VMEM((16, 16, C), BF),
+            dma((7,)),
+        ],
+        "pack", [FAR, FAR, FREE, FREE, FREE, FAR, FAR], [FAR], aliases={1: 0},
+    )
+    second_terms = exchange(terms, "both")
     (first,) = call(
-        reduce_kernel, [sds((192, C), BF)], (after(idx, pieces[0]), first_terms), name="reduce",
-        free=(0,), us=REDUCE_US,
-    )
-    inner_grad = after(inner_grad.reshape(16, D // 16, C), first)
-    inner_terms = dp_terms(inner_grad)
-    first = lax.all_gather(first, ("x", "z"))
-    chunk, pack = call(
-        input_kernel, [sds((128, D), BF), sds((16, 16, C), BF)],
-        (idx, x_part, cot_part, norm_weight, extra, gain, *pieces),
-        [pltpu.VMEM((C, 128), F32)], "input_part", free=(6, 7, 8), free_out=(0, 1),
-        us=INPUT_US,
-    )
-    (spread,) = launch(
-        spread_kernel, [sds((16, D // 16, C), BF)], (after(idx, chunk), inner_terms),
+        reduce_kernel, [sds((192, C), BF)], (idx, first_terms), name="reduce", free=(0,),
+    )
+    chunk, norm = call(
+        input_kernel, [sds((128, D), BF), sds((16, C), BF)],
+        (idx, x_part, cot_part, norm_weight, *pieces), (), "input_part", free=(4, 5, 6),
+        free_out=(0,), us=INPUT_US,
+    )
+    small, wide = launch(
+        spread_kernel, [sds((16, 32, C), BF), sds((4, 288, C), BF)],
+        (idx, second_terms, first, norm),
         [
-            pltpu.VMEM((16, D // 16, C), BF), pltpu.VMEM((D // 16, C), BF), dma(()), dma((16,)),
+            pltpu.VMEM((16, 112, C), BF), pltpu.VMEM((192, C), BF), pltpu.VMEM((16, C), BF),
+            pltpu.VMEM((112, C), BF), pltpu.VMEM((16, 32, C), BF), dma((6,)), dma((9,)),
         ],
-        "spread", [FREE], [FAR], SPREAD_US,
-    )
+        "spread", [FREE, FAR, FAR], [FAR] * 2, SPREAD_US,
+    )
+    small = exchange(small, "both")
+    chunks = spread_out(chunk)
+    wide = exchange(after(wide, small, *chunks[1:]), "second")
     (pack,) = call(
-        share_kernel, [sds((16, 16, C), BF)], (idx, dp_terms(after(pack, spread))), name="share",
-        free=(0,), free_out=(0,),
-    )
-    parts = gather(chunk, pack)
+        share_kernel, [sds((16, 16, C), BF)], (idx, small), name="share", free=(0,),
+        free_out=(0,),
+    )
+    (wide,) = launch(
+        again_kernel, [sds((4, 4, 288, C), BF)], (idx, wide),
+        [pltpu.VMEM((4, 288, C), BF), dma(()), dma((4,))], "again", [FREE], [FAR],
+    )
+    parts = gather(chunks, wide)
+    ends = gather(spread_out(pack), wide)
     outputs, input_grad = launch(
         finish_kernel, [sds((T, D), BF), sds((T, D), F32)], (idx, *parts),
         [
             pltpu.VMEM((8, 128, D), BF), pltpu.VMEM((8, 64, D), F32), dma((8,)), dma((2, 8)),
         ],
-        "finish", [FREE] * 8, [FAR] * 2,
-    )
-    pack = dp_terms(pack)
-    whole = dp_terms(after(spread, pack, input_grad))
+        "finish", [FREE] * 8, [FAR] * 2, FINISH_US,
+    )
+    wide = exchange(wide, "first")
     (
         state_grad, norm_grad, sconv, sbias, step_grad, taps, bias, tb, dl, sk, gnw,
     ) = call(
@@ -831,22 +1006,17 @@
             sds((NH, D), F32), sds((KERNEL, C), F32), sds((C,), F32), sds((NH,), F32),
             sds((NH,), F32), sds((NH,), F32), sds((C,), F32),
         ],
-        (idx, *gather(pack)), [pltpu.VMEM((256, D), F32), pltpu.VMEM((8, 16, D), F32)], "ends",
+        (idx, *ends), [pltpu.VMEM((256, D), F32), pltpu.VMEM((8, 16, D), F32)], "ends",
         free=range(8),
     )
-    (inner_grad,) = launch(
-        widen_kernel, [sds((4, 384, C), F32)], (idx, whole.reshape(4, 384, C)),
-        [pltpu.VMEM((4, 384, C), BF), pltpu.VMEM((4, 384, C), F32), dma((4,)), dma((4,))],
-        "widen", [FREE], [FAR], WIDEN_US,
-    )
-    out_grad, gate_grad = launch(
-        widen_two_kernel, [sds((C, D), F32), sds((4, 4, 96, C), F32)],
-        (idx, first.reshape(4, 4, 192, C)),
+    gate_grad, out_grad, inner_grad = launch(
+        widen_kernel,
+        [sds((4, 4, 96, C), F32), sds((C, D), F32), sds((4, 4, 96, C), F32)], (idx, wide),
         [
-            pltpu.VMEM((4, 4, 192, C), BF), pltpu.VMEM((4, C, C), F32),
-            pltpu.VMEM((4, 4, 96, C), F32), dma((4,)), dma((2, 4)),
+            pltpu.VMEM((4, 4, 288, C), BF), pltpu.VMEM((4, 4, 96, C), F32),
+            pltpu.VMEM((4, C, C), F32), pltpu.VMEM((4, 4, 96, C), F32), dma((4,)), dma((3, 4)),
         ],
-        "widen_two", [FAR], [FAR] * 2,
+        "widen", [FREE], [FAR] * 3, WIDEN_US,
     )
     return (
         outputs[None], input_grad[None], norm_grad, gate_grad.reshape(D, C),

time: 172 us -> 164 us (0.953); the launches traced: 171 us -> 161 us
  blocking collectives: 26.1 us -> 10.6 us
  between operations: 14.3 us -> 1.07 us
  starting transfers between devices: 45.4 us -> 57.4 us
  waiting for transfers between devices: 26 us -> 30.4 us
  local copies, waits for them, and re-layouts: 0 us -> 1.75 us
    all_to_all x1 -> x0, blocking collectives: 15.4 us -> none  [dp_terms(): return lax.all_to_all(v, ('x', 'z'), 0, 0, tiled=True)]
    all_to_all x4 -> x5, starting transfers between devices: 19.3 us -> 29.2 us  [exchange(): lax.all_to_all(v, ('z', 'x', 'y', 'core'), 0, 0, axis_index_groups=teams(...]
    ppermute x9 -> x12, waiting for transfers between devices: 13.4 us -> 18.8 us  [turn(): return lax.ppermute(v, axis, [(i, (i + by) % 4) for i in range(4)])]
    ppermute x9 -> x12, starting transfers between devices: 11.8 us -> 14.4 us  [turn(): return lax.ppermute(v, axis, [(i, (i + by) % 4) for i in range(4)])]
    unnamed x0 -> x12, local copies, waits for them, and re-layouts: none -> 1.75 us
    all_to_all x4 -> x5, waiting for transfers between devices: 8.18 us -> 6.87 us  [exchange(): lax.all_to_all(v, ('z', 'x', 'y', 'core'), 0, 0, axis_index_groups=teams(...]
    ppermute x12 -> x13, waiting for transfers between devices: 4.43 us -> 4.74 us  [swap(): return lax.ppermute(v, 'core', [(0, 1), (1, 0)])]
    ppermute x12 -> x13, starting transfers between devices: 14 us -> 13.9 us  [swap(): return lax.ppermute(v, 'core', [(0, 1), (1, 0)])]
  transfers between devices with their start and end apart: 26 -> 30, of which waited for: 13 -> 15; matrix products, arithmetic and copies ran while one was open for 0% -> 0% of each run, Pallas kernels for 22% -> 25%
where the time goes in v3:
time: 164 us; the launch traced here: 161 us
  Pallas kernels  59.8 us (36%)
  starting transfers between devices  57.4 us (35%)
  waiting for transfers between devices  30.4 us (19%)
  blocking collectives  10.6 us (6%)
  local copies, waits for them, and re-layouts  1.75 us (1%)
    pallas_call x13, Pallas kernels, launch(): pl.pallas_call(kernel, out_shape=[v if w is FREE else w(v.shape, v.dtype)...  59.8 us
    all_to_all x5, starting transfers between devices, exchange(): lax.all_to_all(v, ('z', 'x', 'y', 'core'), 0, 0, axis_index_groups=teams(...  29.2 us
    ppermute x12, waiting for transfers between devices, turn(): return lax.ppermute(v, axis, [(i, (i + by) % 4) for i in range(4)])  18.8 us
    ppermute x12, starting transfers between devices, turn(): return lax.ppermute(v, axis, [(i, (i + by) % 4) for i in range(4)])  14.4 us
    ppermute x13, starting transfers between devices, swap(): return lax.ppermute(v, 'core', [(0, 1), (1, 0)])  13.9 us
    all_to_all x1, blocking collectives, per_device(): sums = lax.all_to_all(sums, ('y', 'core'), 0, 0, tiled=True)  10.6 us
    all_to_all x5, waiting for transfers between devices, exchange(): lax.all_to_all(v, ('z', 'x', 'y', 'core'), 0, 0, axis_index_groups=teams(...  6.87 us
    ppermute x13, waiting for transfers between devices, swap(): return lax.ppermute(v, 'core', [(0, 1), (1, 0)])  4.74 us
  transfers between devices with their start and end apart: 30, of which 15 were waited for; matrix products, arithmetic and copies ran while one was open for 0% of the time, Pallas kernels for 25%

profile of v3, /device:TPU:1, one launch (start us, length us, event | category | flops | bytes accessed | tf_op | source)
XLA Modules:
  0.0 161.1 jit_solution(14375632929175865544)
XLA Ops:
  0.7 10.9 %forward.1 = (bf16[512,1536]{1,0:T(8,128)(2,1)}, f32[384,512]{1,0:T(8,128)S(1)}, bf16[512,384]{1,0:T(8,128)(2,1)}, f32[384,512]{1,0:T(8,128)}, f32[384,512]{1,0:...) custom-call(s32[4]{0:T(128)S(1)} %pad_add_fusion.idx_ref, ...), custom_call_target="tpu_custom_call" | custom-call | flops 1000 | bytes 1000 | tf_op jit(solution)/shard_map/forward/pallas_call | solution.py:234
  11.6 10.6 %all_to_all.30.refs_0_ = f32[8,2,512]{2,1,0:T(2,128)S(1)} all-to-all(f32[8,2,512]{2,1,0:T(2,128)} %get-tuple-element.89), channel_id=1, replica_groups=mesh['z'=4,'x'=4,'y'=4,'core'=2] {'y','core'}, dimensions={0} | all-to-all | bytes 65536 | tf_op jit(solution)/shard_map/all_to_all | solution.py:941
  22.2 4.9 %middle.1 = (bf16[16,192,384]{2,1,0:T(8,128)(2,1)}, bf16[512,384]{1,0:T(8,128)(2,1)}, bf16[512,384]{1,0:T(8,128)(2,1)}, bf16[384,512]{1,0:T(8,128)(2,1)}, f32[384,8]{1,0:T(8,128)}) custom-call(s32[4]{0:T(128)S(1)} %pad_add_fusion.idx_ref, f32[8,2,512]{2,1,0:T(2,128)S(1)} %all_to_all.30.refs_0_, f32[384,512]{1,0:T(8,128)S(1)} %get-tuple-element.90.refs_1_, ...), custom_call_target="tpu_custom_call" | custom-call | flops 1000 | bytes 1000 | tf_op jit(solution)/shard_map/middle/pallas_call | solution.py:234
  27.2 7.6 %all-to-all-start.2 = ((bf16[16,192,384]{2,1,0:T(8,128)(2,1)}), bf16[16,192,384]{2,1,0:T(8,128)(2,1)S(1)}, u32[]{:S(2)}, u32[]{:S(2)}) async-start(bf16[16,192,384]{2,1,0:T(8,128)(2,1)} %get-tuple-element.121), calls=%async_computation.2 | async-start | bytes 4718592 | tf_op jit(solution)/shard_map/all_to_all | solution.py:916
  34.8 13.4 %backward.1 = (bf16[16,112,384]{2,1,0:T(8,128)(2,1)}, bf16[4,128,1536]{2,1,0:T(8,128)(2,1)S(1)}, bf16[4,48,1536]{2,1,0:T(8,128)(2,1)S(1)}, f32[16,1536]{1,0:T(8,...) custom-call(s32[4]{0:T(128)S(1)} %pad_add_fusion.idx_ref, ...), custom_call_target="tpu_custom_call" | custom-call | flops 1000 | bytes 1000 | tf_op jit(solution)/shard_map/backward/pallas_call | solution.py:234
  53.2 2.6 %fold.1 = (f32[128,1536]{1,0:T(8,128)}, f32[48,1536]{1,0:T(8,128)}, bf16[48,1536]{1,0:T(8,128)(2,1)S(1)}, bf16[48,1536]{1,0:T(8,128)(2,1)S(1)}, bf16[48,1536]{1,...) custom-call(s32[4]{0:T(128)S(1)} %pad_add_fusion.idx_ref, ...), custom_call_target="tpu_custom_call" | custom-call | flops 1000 | bytes 1000 | tf_op jit(solution)/shard_map/fold/pallas_call | solution.py:234
  65.8 3.1 %pack.1 = bf16[16,112,384]{2,1,0:T(8,128)(2,1)} custom-call(s32[4]{0:T(128)S(1)} %pad_add_fusion.idx_ref, bf16[16,112,384]{2,1,0:T(8,128)(2,1)} %get-tuple-element.114.refs_0_, f32[48,1536]{1,0:T(8,128)} %get-tuple-element.115.refs_1_, bf16[48,1536]{1,0:T(8,128)(2,1)S(1)} %collective-permute-done.11.refs_2_, ...), custom_call_target="tpu_custom_call", output_to_operand_aliasing={{}: (1, {})} | custom-call | flops 1000 | bytes 1000 | tf_op jit(solution)/shard_map/pack/pallas_call | solution.py:234
  68.9 7.0 %all-to-all-start.1 = ((bf16[16,112,384]{2,1,0:T(8,128)(2,1)}), bf16[16,112,384]{2,1,0:T(8,128)(2,1)}, u32[]{:S(2)}, u32[]{:S(2)}) async-start(bf16[16,112,384]{2,1,0:T(8,128)(2,1)} %pack.1), calls=%async_computation.1 | async-start | bytes 2752512 | tf_op jit(solution)/shard_map/all_to_all | solution.py:916
  76.7 5.3 %collective-permute-done.6.refs_5_ = bf16[128,1536]{1,0:T(8,128)(2,1)} collective-permute-done((bf16[128,1536]{1,0:T(8,128)(2,1)}, bf16[128,1536]{1,0:T(8,128)(2,1)}, u32[]{:S(2)}, u32[]{:S(2)}) %collective-permute-start.6) | collective-permute-done | bytes 393248 | tf_op jit(solution)/shard_map/ppermute | solution.py:649
  83.8 3.5 %input_part.1 = (bf16[128,1536]{1,0:T(8,128)(2,1)}, bf16[16,384]{1,0:T(8,128)(2,1)}) custom-call(s32[4]{0:T(128)S(1)} %pad_add_fusion.idx_ref, bf16[64,1536]{1,0:T(8,128)(2,1)} %get-tuple-element.83.refs_0_, bf16[64,1536]{1,0:T(8,128)(2,1)} %get-tuple-element.84.refs_1_, f32[1536]{0:T(1024)} %refs_2_.3, f32[128,1536]{1,0:T(8,128)} %get-tuple-element.109.refs_3_, ...), custom_call_target="tpu_custom_call" | custom-call | flops 10000001024 | bytes 1000 | tf_op jit(solution)/shard_map/input_part/pallas_call | solution.py:234
  87.3 3.1 %collective-permute-start.10 = (bf16[128,1536]{1,0:T(8,128)(2,1)}, bf16[128,1536]{1,0:T(8,128)(2,1)S(1)}, u32[]{:S(2)}, u32[]{:S(2)}) collective-permute-start(bf16[128,1536]{1,0:T(8,128)(2,1)} %get-tuple-element.126.refs_0_), channel_id=1, source_target_pairs={{0,6},{2,0},{4,2},{6,4},{1,7},{3,1},{5,3},{7,5},{8,14},{10,8},{12,... | collective-permute-start | bytes 1179656 | tf_op jit(solution)/shard_map/ppermute | solution.py:649
  93.6 3.1 %spread.1 = (bf16[16,32,384]{2,1,0:T(8,128)(2,1)}, bf16[4,288,384]{2,1,0:T(8,128)(2,1)}) custom-call(s32[4]{0:T(128)S(1)} %pad_add_fusion.idx_ref, bf16[16,112,384]{2,1,0:T(8,128)(2,1)} %all-to-all-done.1.terms_any, bf16[192,384]{1,0:T(8,128)(2,1)} %reduce.1.first_any, bf16[16,384]{1,0:T(8,128)(2,1)} %get-tuple-element.122.norm_any), custom_call_target="tpu_custom_call" | custom-call | flops 1000 | bytes 1000 | tf_op jit(solution)/shard_map/spread/pallas_call | solution.py:234
  96.6 6.3 %all-to-all-start.3 = ((bf16[16,32,384]{2,1,0:T(8,128)(2,1)}), bf16[16,32,384]{2,1,0:T(8,128)(2,1)S(1)}, u32[]{:S(2)}, u32[]{:S(2)}) async-start(bf16[16,32,384]{2,1,0:T(8,128)(2,1)} %get-tuple-element.124), calls=%async_computation.3 | async-start | bytes 786432 | tf_op jit(solution)/shard_map/all_to_all | solution.py:916
  102.9 4.0 %collective-permute-done.10.refs_3_ = bf16[128,1536]{1,0:T(8,128)(2,1)S(1)} collective-permute-done((bf16[128,1536]{1,0:T(8,128)(2,1)}, bf16[128,1536]{1,0:T(8,128)(2,1)S(1)}, u32[]{:S(2)}, u32[]{:S(2)}) %collective-permute-start.10) | collective-permute-done | bytes 393248 | tf_op jit(solution)/shard_map/ppermute | solution.py:649
  106.9 4.2 %collective-permute-done.8.refs_1_ = bf16[128,1536]{1,0:T(8,128)(2,1)} collective-permute-done((bf16[128,1536]{1,0:T(8,128)(2,1)}, bf16[128,1536]{1,0:T(8,128)(2,1)}, u32[]{:S(2)}, u32[]{:S(2)}) %collective-permute-start.8) | collective-permute-done | bytes 393248 | tf_op jit(solution)/shard_map/ppermute | solution.py:649
  111.2 4.4 %all-to-all-start.4 = ((bf16[4,288,384]{2,1,0:T(8,128)(2,1)}), bf16[4,288,384]{2,1,0:T(8,128)(2,1)S(1)}, u32[]{:S(2)}, u32[]{:S(2)}) async-start(bf16[4,288,384]{2,1,0:T(8,128)(2,1)} %get-tuple-element.125), calls=%async_computation.4 | async-start | bytes 1769472 | tf_op jit(solution)/shard_map/all_to_all | solution.py:916
  118.3 6.1 %all-to-all-done.4.blocks_any = bf16[4,288,384]{2,1,0:T(8,128)(2,1)S(1)} async-done(((bf16[4,288,384]{2,1,0:T(8,128)(2,1)}), bf16[4,288,384]{2,1,0:T(8,128)(2,1)S(1)}, u32[]{:S(2)}, u32[]{:S(2)}) %all-to-all-start.4) | async-done | bytes 884768 | tf_op jit(solution)/shard_map/all_to_all | solution.py:916
  124.4 2.5 %again.1 = bf16[4,4,288,384]{3,2,1,0:T(8,128)(2,1)} custom-call(s32[4]{0:T(128)S(1)} %pad_add_fusion.idx_ref, bf16[4,288,384]{2,1,0:T(8,128)(2,1)S(1)} %all-to-all-done.4.blocks_any), custom_call_target="tpu_custom_call" | custom-call | flops 1000 | bytes 1000 | tf_op jit(solution)/shard_map/again/pallas_call | solution.py:234
  126.9 4.0 %all-to-all-start.5 = ((bf16[4,4,288,384]{3,2,1,0:T(8,128)(2,1)}), bf16[4,4,288,384]{3,2,1,0:T(8,128)(2,1)S(1)}, u32[]{:S(2)}, u32[]{:S(2)}) async-start(bf16[4,4,288,384]{3,2,1,0:T(8,128)(2,1)} %again.1), calls=%async_computation.5 | async-start | bytes 7077888 | tf_op jit(solution)/shard_map/all_to_all | solution.py:916
  134.7 4.6 %collective-permute-start.21 = (bf16[16,16,384]{2,1,0:T(8,128)(2,1)}, bf16[16,16,384]{2,1,0:T(8,128)(2,1)S(1)}, u32[]{:S(2)}, u32[]{:S(2)}) collective-permute-start(bf16[16,16,384]{2,1,0:T(8,128)(2,1)} %share.1.refs_0_), channel_id=1, source_target_pairs={{0,1},{1,0},{2,3},{3,2},{4,5},{5,4},{6,7},{7,6},{8,9},{9,8},{10,11... | collective-permute-start | bytes 589832 | tf_op jit(solution)/shard_map/ppermute | solution.py:645
  141.8 4.0 %collective-permute-start.15 = (bf16[128,1536]{1,0:T(8,128)(2,1)}, bf16[128,1536]{1,0:T(8,128)(2,1)S(1)}, u32[]{:S(2)}, u32[]{:S(2)}) collective-permute-start(bf16[128,1536]{1,0:T(8,128)(2,1)} %collective-permute-done.8.refs_1_), channel_id=1, source_target_pairs={{0,1},{1,0},{2,3},{3,2},{4,5},{5,4},{6,7},{7,6},{8,9},{9,8},{10,11... | collective-permute-start | bytes 1179656 | tf_op jit(solution)/shard_map/ppermute | solution.py:645
  148.3 4.2 %ends.1 = (f32[1536,256]{1,0:T(8,128)}, f32[1536]{0:T(1024)}, f32[4,256]{1,0:T(4,128)}, f32[256]{0:T(256)}, f32[6,1536]{1,0:T(8,128)}, /*index=5*/f32[4,384]{1,0...) custom-call(s32[4]{0:T(128)S(1)} %pad_add_fusion.idx_ref, ...), custom_call_target="tpu_custom_call" | custom-call | flops 1000 | bytes 1000 | tf_op jit(solution)/shard_map/ends/pallas_call | solution.py:234
  152.6 4.0 %finish.1 = (bf16[512,1536]{1,0:T(8,128)(2,1)}, f32[512,1536]{1,0:T(8,128)}) custom-call(s32[4]{0:T(128)S(1)} %pad_add_fusion.idx_ref, bf16[128,1536]{1,0:T(8,128)(2,1)} %get-tuple-element.126.refs_0_, bf16[128,1536]{1,0:T(8,128)(2,1)} %collective-permute-done.8.refs_1_, bf16[128,1536]{1,0:T(8,128)(2,1)S(1)} %copy-done.3, bf16[128,1536]{1,0:T(8,128)(2,1)S(1)} %copy-done.1, ...), custom_call_target="tpu_custom_call" | custom-call | flops 20000000000 | bytes 1000 | tf_op jit(solution)/shard_map/finish/pallas_call | solution.py:234
  156.6 4.3 %widen.1 = (f32[4,4,96,384]{3,2,1,0:T(8,128)}, f32[384,1536]{1,0:T(8,128)}, f32[4,4,96,384]{3,2,1,0:T(8,128)}) custom-call(s32[4]{0:T(128)S(1)} %pad_add_fusion.idx_ref, bf16[4,4,288,384]{3,2,1,0:T(8,128)(2,1)S(1)} %all-to-all-done.5.hbm), custom_call_target="tpu_custom_call" | custom-call | flops 1000 | bytes 1000 | tf_op jit(solution)/shard_map/widen/pallas_call | solution.py:234
  (63 shorter events, 32.4 us)
Async XLA Ops:
  27.2 41.7 %all-to-all-start.2 = ((bf16[16,192,384]{2,1,0:T(8,128)(2,1)}), bf16[16,192,384]{2,1,0:T(8,128)(2,1)S(1)}, u32[]{:S(2)}, u32[]{:S(2)}) async-start(bf16[16,192,384]{2,1,0:T(8,128)(2,1)} %get-tuple-element.121), calls=%async_computation.2 | async-start | bytes 4718592 | tf_op jit(solution)/shard_map/all_to_all | solution.py:916
  55.8 7.2 %collective-permute-start.11 = (bf16[48,1536]{1,0:T(8,128)(2,1)S(1)}, bf16[48,1536]{1,0:T(8,128)(2,1)S(1)}, u32[]{:S(2)}, u32[]{:S(2)}) collective-permute-start(bf16[48,1536]{1,0:T(8,128)(2,1)S(1)} %get-tuple-element.116), channel_id=1, source_target_pairs={{0,2},{2,4},{4,6},{6,0},{1,3},{3,5},{5,7},{7,1},{8,10},{10,12},{12... | collective-permute-start | bytes 442376 | tf_op jit(solution)/shard_map/ppermute | solution.py:649
  56.3 8.6 %collective-permute-start.12 = (bf16[48,1536]{1,0:T(8,128)(2,1)S(1)}, bf16[48,1536]{1,0:T(8,128)(2,1)S(1)}, u32[]{:S(2)}, u32[]{:S(2)}) collective-permute-start(bf16[48,1536]{1,0:T(8,128)(2,1)S(1)} %get-tuple-element.117), channel_id=1, source_target_pairs={{0,4},{2,6},{4,0},{6,2},{1,5},{3,7},{5,1},{7,3},{8,12},{10,14},{12... | collective-permute-start | bytes 442376 | tf_op jit(solution)/shard_map/ppermute | solution.py:649
  58.1 7.7 %collective-permute-start.13 = (bf16[48,1536]{1,0:T(8,128)(2,1)S(1)}, bf16[48,1536]{1,0:T(8,128)(2,1)S(1)}, u32[]{:S(2)}, u32[]{:S(2)}) collective-permute-start(bf16[48,1536]{1,0:T(8,128)(2,1)S(1)} %get-tuple-element.118), channel_id=1, source_target_pairs={{0,6},{2,0},{4,2},{6,4},{1,7},{3,1},{5,3},{7,5},{8,14},{10,8},{12,... | collective-permute-start | bytes 442376 | tf_op jit(solution)/shard_map/ppermute | solution.py:649
  58.9 17.0 %collective-permute-start.5 = (bf16[128,1536]{1,0:T(8,128)(2,1)}, bf16[128,1536]{1,0:T(8,128)(2,1)S(1)}, u32[]{:S(2)}, u32[]{:S(2)}) collective-permute-start(bf16[128,1536]{1,0:T(8,128)(2,1)} %get-tuple-element.110), channel_id=1, source_target_pairs={{0,2},{2,4},{4,6},{6,0},{1,3},{3,5},{5,7},{7,1},{8,10},{10,12},{12... | collective-permute-start | bytes 1179656 | tf_op jit(solution)/shard_map/ppermute | solution.py:649
  59.6 22.3 %collective-permute-start.6 = (bf16[128,1536]{1,0:T(8,128)(2,1)}, bf16[128,1536]{1,0:T(8,128)(2,1)}, u32[]{:S(2)}, u32[]{:S(2)}) collective-permute-start(bf16[128,1536]{1,0:T(8,128)(2,1)} %get-tuple-element.111), channel_id=1, source_target_pairs={{0,4},{2,6},{4,0},{6,2},{1,5},{3,7},{5,1},{7,3},{8,12},{10,14},{12... | collective-permute-start | bytes 1179656 | tf_op jit(solution)/shard_map/ppermute | solution.py:649
  62.9 19.9 %collective-permute-start.7 = (bf16[128,1536]{1,0:T(8,128)(2,1)}, bf16[128,1536]{1,0:T(8,128)(2,1)}, u32[]{:S(2)}, u32[]{:S(2)}) collective-permute-start(bf16[128,1536]{1,0:T(8,128)(2,1)} %get-tuple-element.112), channel_id=1, source_target_pairs={{0,6},{2,0},{4,2},{6,4},{1,7},{3,1},{5,3},{7,5},{8,14},{10,8},{12,... | collective-permute-start | bytes 1179656 | tf_op jit(solution)/shard_map/ppermute | solution.py:649
  68.9 24.7 %all-to-all-start.1 = ((bf16[16,112,384]{2,1,0:T(8,128)(2,1)}), bf16[16,112,384]{2,1,0:T(8,128)(2,1)}, u32[]{:S(2)}, u32[]{:S(2)}) async-start(bf16[16,112,384]{2,1,0:T(8,128)(2,1)} %pack.1), calls=%async_computation.1 | async-start | bytes 2752512 | tf_op jit(solution)/shard_map/all_to_all | solution.py:916
  87.3 19.6 %collective-permute-start.10 = (bf16[128,1536]{1,0:T(8,128)(2,1)}, bf16[128,1536]{1,0:T(8,128)(2,1)S(1)}, u32[]{:S(2)}, u32[]{:S(2)}) collective-permute-start(bf16[128,1536]{1,0:T(8,128)(2,1)} %get-tuple-element.126.refs_0_), channel_id=1, source_target_pairs={{0,6},{2,0},{4,2},{6,4},{1,7},{3,1},{5,3},{7,5},{8,14},{10,8},{12,... | collective-permute-start | bytes 1179656 | tf_op jit(solution)/shard_map/ppermute | solution.py:649
  90.5 16.4 %collective-permute-start.9 = (bf16[128,1536]{1,0:T(8,128)(2,1)}, bf16[128,1536]{1,0:T(8,128)(2,1)S(1)}, u32[]{:S(2)}, u32[]{:S(2)}) collective-permute-start(bf16[128,1536]{1,0:T(8,128)(2,1)} %get-tuple-element.126.refs_0_), channel_id=1, source_target_pairs={{0,4},{2,6},{4,0},{6,2},{1,5},{3,7},{5,1},{7,3},{8,12},{10,14},{12... | collective-permute-start | bytes 1179656 | tf_op jit(solution)/shard_map/ppermute | solution.py:649
  90.5 20.6 %collective-permute-start.8 = (bf16[128,1536]{1,0:T(8,128)(2,1)}, bf16[128,1536]{1,0:T(8,128)(2,1)}, u32[]{:S(2)}, u32[]{:S(2)}) collective-permute-start(bf16[128,1536]{1,0:T(8,128)(2,1)} %get-tuple-element.126.refs_0_), channel_id=1, source_target_pairs={{0,2},{2,4},{4,6},{6,0},{1,3},{3,5},{5,7},{7,1},{8,10},{10,12},{12... | collective-permute-start | bytes 1179656 | tf_op jit(solution)/shard_map/ppermute | solution.py:649
  96.6 14.5 %all-to-all-start.3 = ((bf16[16,32,384]{2,1,0:T(8,128)(2,1)}), bf16[16,32,384]{2,1,0:T(8,128)(2,1)S(1)}, u32[]{:S(2)}, u32[]{:S(2)}) async-start(bf16[16,32,384]{2,1,0:T(8,128)(2,1)} %get-tuple-element.124), calls=%async_computation.3 | async-start | bytes 786432 | tf_op jit(solution)/shard_map/all_to_all | solution.py:916
  111.2 13.2 %all-to-all-start.4 = ((bf16[4,288,384]{2,1,0:T(8,128)(2,1)}), bf16[4,288,384]{2,1,0:T(8,128)(2,1)S(1)}, u32[]{:S(2)}, u32[]{:S(2)}) async-start(bf16[4,288,384]{2,1,0:T(8,128)(2,1)} %get-tuple-element.125), calls=%async_computation.4 | async-start | bytes 1769472 | tf_op jit(solution)/shard_map/all_to_all | solution.py:916
  117.1 22.3 %collective-permute-start.18 = (bf16[16,16,384]{2,1,0:T(8,128)(2,1)}, bf16[16,16,384]{2,1,0:T(8,128)(2,1)}, u32[]{:S(2)}, u32[]{:S(2)}) collective-permute-start(bf16[16,16,384]{2,1,0:T(8,128)(2,1)} %share.1.refs_0_), channel_id=1, source_target_pairs={{0,2},{2,4},{4,6},{6,0},{1,3},{3,5},{5,7},{7,1},{8,10},{10,12},{12... | collective-permute-start | bytes 589832 | tf_op jit(solution)/shard_map/ppermute | solution.py:649
  126.9 29.7 %all-to-all-start.5 = ((bf16[4,4,288,384]{3,2,1,0:T(8,128)(2,1)}), bf16[4,4,288,384]{3,2,1,0:T(8,128)(2,1)S(1)}, u32[]{:S(2)}, u32[]{:S(2)}) async-start(bf16[4,4,288,384]{3,2,1,0:T(8,128)(2,1)} %again.1), calls=%async_computation.5 | async-start | bytes 7077888 | tf_op jit(solution)/shard_map/all_to_all | solution.py:916
  130.9 8.4 %collective-permute-start.19 = (bf16[16,16,384]{2,1,0:T(8,128)(2,1)}, bf16[16,16,384]{2,1,0:T(8,128)(2,1)S(1)}, u32[]{:S(2)}, u32[]{:S(2)}) collective-permute-start(bf16[16,16,384]{2,1,0:T(8,128)(2,1)} %share.1.refs_0_), channel_id=1, source_target_pairs={{0,4},{2,6},{4,0},{6,2},{1,5},{3,7},{5,1},{7,3},{8,12},{10,14},{12... | collective-permute-start | bytes 589832 | tf_op jit(solution)/shard_map/ppermute | solution.py:649
  132.5 9.4 %collective-permute-start.20 = (bf16[16,16,384]{2,1,0:T(8,128)(2,1)}, bf16[16,16,384]{2,1,0:T(8,128)(2,1)S(1)}, u32[]{:S(2)}, u32[]{:S(2)}) collective-permute-start(bf16[16,16,384]{2,1,0:T(8,128)(2,1)} %share.1.refs_0_), channel_id=1, source_target_pairs={{0,6},{2,0},{4,2},{6,4},{1,7},{3,1},{5,3},{7,5},{8,14},{10,8},{12,... | collective-permute-start | bytes 589832 | tf_op jit(solution)/shard_map/ppermute | solution.py:649
  134.7 11.2 %collective-permute-start.21 = (bf16[16,16,384]{2,1,0:T(8,128)(2,1)}, bf16[16,16,384]{2,1,0:T(8,128)(2,1)S(1)}, u32[]{:S(2)}, u32[]{:S(2)}) collective-permute-start(bf16[16,16,384]{2,1,0:T(8,128)(2,1)} %share.1.refs_0_), channel_id=1, source_target_pairs={{0,1},{1,0},{2,3},{3,2},{4,5},{5,4},{6,7},{7,6},{8,9},{9,8},{10,11... | collective-permute-start | bytes 589832 | tf_op jit(solution)/shard_map/ppermute | solution.py:645
  139.3 6.5 %collective-permute-start.22 = (bf16[16,16,384]{2,1,0:T(8,128)(2,1)}, bf16[16,16,384]{2,1,0:T(8,128)(2,1)S(1)}, u32[]{:S(2)}, u32[]{:S(2)}) collective-permute-start(bf16[16,16,384]{2,1,0:T(8,128)(2,1)} %collective-permute-done.18.refs_1_), channel_id=1, source_target_pairs={{0,1},{1,0},{2,3},{3,2},{4,5},{5,4},{6,7},{7,6},{8,9},{9,8},{10,11... | collective-permute-start | bytes 589832 | tf_op jit(solution)/shard_map/ppermute | solution.py:645
  139.3 7.0 %collective-permute-start.23 = (bf16[16,16,384]{2,1,0:T(8,128)(2,1)S(1)}, bf16[16,16,384]{2,1,0:T(8,128)(2,1)S(1)}, u32[]{:S(2)}, u32[]{:S(2)}) collective-permute-start(bf16[16,16,384]{2,1,0:T(8,128)(2,1)S(1)} %collective-permute-done.19.refs_2_), channel_id=1, source_target_pairs={{0,1},{1,0},{2,3},{3,2},{4,5},{5,4},{6,7},{7,6},{8,9},{9,8},{10,11... | collective-permute-start | bytes 589832 | tf_op jit(solution)/shard_map/ppermute | solution.py:645
  141.8 10.7 %collective-permute-start.14 = (bf16[128,1536]{1,0:T(8,128)(2,1)}, bf16[128,1536]{1,0:T(8,128)(2,1)S(1)}, u32[]{:S(2)}, u32[]{:S(2)}) collective-permute-start(bf16[128,1536]{1,0:T(8,128)(2,1)} %get-tuple-element.126.refs_0_), channel_id=1, source_target_pairs={{0,1},{1,0},{2,3},{3,2},{4,5},{5,4},{6,7},{7,6},{8,9},{9,8},{10,11... | collective-permute-start | bytes 1179656 | tf_op jit(solution)/shard_map/ppermute | solution.py:645
  141.8 10.7 %collective-permute-start.15 = (bf16[128,1536]{1,0:T(8,128)(2,1)}, bf16[128,1536]{1,0:T(8,128)(2,1)S(1)}, u32[]{:S(2)}, u32[]{:S(2)}) collective-permute-start(bf16[128,1536]{1,0:T(8,128)(2,1)} %collective-permute-done.8.refs_1_), channel_id=1, source_target_pairs={{0,1},{1,0},{2,3},{3,2},{4,5},{5,4},{6,7},{7,6},{8,9},{9,8},{10,11... | collective-permute-start | bytes 1179656 | tf_op jit(solution)/shard_map/ppermute | solution.py:645
  145.9 6.7 %collective-permute-start.16 = (bf16[128,1536]{1,0:T(8,128)(2,1)}, bf16[128,1536]{1,0:T(8,128)(2,1)S(1)}, u32[]{:S(2)}, u32[]{:S(2)}) collective-permute-start(bf16[128,1536]{1,0:T(8,128)(2,1)} %copy-done.2), channel_id=1, source_target_pairs={{0,1},{1,0},{2,3},{3,2},{4,5},{5,4},{6,7},{7,6},{8,9},{9,8},{10,11... | collective-permute-start | bytes 1179656 | tf_op jit(solution)/shard_map/ppermute | solution.py:645
  145.9 6.7 %collective-permute-start.17 = (bf16[128,1536]{1,0:T(8,128)(2,1)}, bf16[128,1536]{1,0:T(8,128)(2,1)S(1)}, u32[]{:S(2)}, u32[]{:S(2)}) collective-permute-start(bf16[128,1536]{1,0:T(8,128)(2,1)} %copy-done), channel_id=1, source_target_pairs={{0,1},{1,0},{2,3},{3,2},{4,5},{5,4},{6,7},{7,6},{8,9},{9,8},{10,11... | collective-permute-start | bytes 1179656 | tf_op jit(solution)/shard_map/ppermute | solution.py:645
  (12 other events, 87.2 us)

commit v4 on v3

--- a/solution.py
+++ b/solution.py
@@ -622,23 +622,19 @@
     )
 
 
-def fold_kernel(idx_ref, *refs):
-    keep, keep_state, got_state, *got = refs[:7]
-    own_hbm, own_state_hbm, *sends = refs[7:15]
-    own, own_state, sems = refs[15:]
-    stores = [
-        pltpu.make_async_copy(own_state, own_state_hbm, sems.at[0]),
-        pltpu.make_async_copy(own, own_hbm, sems.at[1]),
-    ]
-    own[...] = keep[0].astype(F32) + got[0][...].astype(F32)
-    stores[1].start()
-    own_state[...] = keep_state[0].astype(F32) + got_state[0].astype(F32)
-    stores[0].start()
-    for k in range(1, 4):
-        sends[k - 1][...] = (keep_state[k].astype(F32) + got_state[k].astype(F32)).astype(BF)
-        sends[k + 2][...] = (keep[k].astype(F32) + got[k][...].astype(F32)).astype(BF)
-    for store in stores:
-        store.wait()
+def fold_kernel(idx_ref, keep, *refs):
+    *got, own_hbm, s1, s2, s3, own, sem = refs
+
+    def both(k):
+        other = got[k][...] if len(got) == 4 else got[0][k]
+        return keep[k].astype(F32) + other.astype(F32)
+
+    own[...] = both(0)
+    store = pltpu.make_async_copy(own, own_hbm, sem)
+    store.start()
+    for k, send in enumerate((s1, s2, s3)):
+        send[...] = both(k + 1).astype(BF)
+    store.wait()
 
 
 def swap(v):
@@ -649,18 +645,19 @@
     return lax.ppermute(v, axis, [(i, (i + by) % 4) for i in range(4)])
 
 
+def fold(idx, keep, got, name):
+    rows = keep.shape[1]
+    own, *sends = launch(
+        fold_kernel, [sds((rows, D), F32), *[sds((rows, D), BF)] * 3], (idx, keep, *got),
+        [pltpu.VMEM((rows, D), F32), pltpu.SemaphoreType.DMA(())], name, [NEAR] * (1 + len(got)),
+        [FAR] + [NEAR] * 3, vmem=16,
+    )
+    return [own, *[turn(send, "y", k + 1) for k, send in enumerate(sends)]]
+
+
 def scatter(idx, keep, keep_state, give_state, gives):
-    rows, state_rows = sds((128, D), BF), sds((48, D), BF)
-    outs = [sds((128, D), F32), sds((48, D), F32), *[state_rows] * 3, *[rows] * 3]
-    scratch = [
-        pltpu.VMEM((128, D), F32), pltpu.VMEM((48, D), F32), pltpu.SemaphoreType.DMA((2,)),
-    ]
-    own, own_state, *sends = launch(
-        fold_kernel, outs, (idx, keep, keep_state, swap(give_state), *map(swap, gives)), scratch,
-        "fold", [NEAR] * 7, [FAR] * 2 + [NEAR] * 6, vmem=16,
-    )
-    sends = [turn(send, "y", k % 3 + 1) for k, send in enumerate(sends)]
-    return [own_state, *sends[:3]], [own, *sends[3:]]
+    state = fold(idx, keep_state, [swap(give_state)], "fold_state")
+    return state, fold(after(idx, state[0]), keep, [swap(give) for give in gives], "fold")
 
 
 def spread_out(chunk):

time: 164 us -> 160 us (0.976)
  waiting for transfers between devices: 30.4 us -> 25.4 us
    ppermute x12, waiting for transfers between devices: 18.8 us -> 13.2 us  [turn(): return lax.ppermute(v, axis, [(i, (i + by) % 4) for i in range(4)])]
    all_to_all x5, waiting for transfers between devices: 6.87 us -> 9.69 us  [exchange(): lax.all_to_all(v, ('z', 'x', 'y', 'core'), 0, 0, axis_index_groups=teams(...]
    ppermute x12, starting transfers between devices: 14.4 us -> 16.7 us  [turn(): return lax.ppermute(v, axis, [(i, (i + by) % 4) for i in range(4)])]
    ppermute x13, waiting for transfers between devices: 4.74 us -> 2.5 us  [swap(): return lax.ppermute(v, 'core', [(0, 1), (1, 0)])]
    all_to_all x5, starting transfers between devices: 29.2 us -> 27.1 us  [exchange(): lax.all_to_all(v, ('z', 'x', 'y', 'core'), 0, 0, axis_index_groups=teams(...]
    pallas_call x13 -> x14, Pallas kernels: 59.8 us -> 61.1 us  [launch(): pl.pallas_call(kernel, out_shape=[v if w is FREE else w(v.shape, v.dtype)...]
  transfers between devices with their start and end apart: 30 -> 30, of which waited for: 15 -> 11; matrix products, arithmetic and copies ran while one was open for 0% -> 0% of each run, Pallas kernels for 25% -> 26%
where the time goes in v4:
time: 160 us; the launch traced here: 158 us
  Pallas kernels  61.1 us (38%)
  starting transfers between devices  57.8 us (36%)
  waiting for transfers between devices  25.4 us (16%)
  blocking collectives  10.6 us (7%)
  local copies, waits for them, and re-layouts  1.77 us (1%)
    pallas_call x14, Pallas kernels, launch(): pl.pallas_call(kernel, out_shape=[v if w is FREE else w(v.shape, v.dtype)...  61.1 us
    all_to_all x5, starting transfers between devices, exchange(): lax.all_to_all(v, ('z', 'x', 'y', 'core'), 0, 0, axis_index_groups=teams(...  27.1 us
    ppermute x12, starting transfers between devices, turn(): return lax.ppermute(v, axis, [(i, (i + by) % 4) for i in range(4)])  16.7 us
    ppermute x13, starting transfers between devices, swap(): return lax.ppermute(v, 'core', [(0, 1), (1, 0)])  13.9 us
    ppermute x12, waiting for transfers between devices, turn(): return lax.ppermute(v, axis, [(i, (i + by) % 4) for i in range(4)])  13.2 us
    all_to_all x1, blocking collectives, per_device(): sums = lax.all_to_all(sums, ('y', 'core'), 0, 0, tiled=True)  10.6 us
    all_to_all x5, waiting for transfers between devices, exchange(): lax.all_to_all(v, ('z', 'x', 'y', 'core'), 0, 0, axis_index_groups=teams(...  9.69 us
  transfers between devices with their start and end apart: 30, of which 11 were waited for; matrix products, arithmetic and copies ran while one was open for 0% of the time, Pallas kernels for 26%

profile of v4, /device:TPU:1, one launch (start us, length us, event | category | flops | bytes accessed | tf_op | source)
XLA Modules:
  0.0 157.8 jit_solution(8742698205600504805)
XLA Ops:
  0.7 10.9 %forward.1 = (bf16[512,1536]{1,0:T(8,128)(2,1)}, f32[384,512]{1,0:T(8,128)S(1)}, bf16[512,384]{1,0:T(8,128)(2,1)}, f32[384,512]{1,0:T(8,128)}, f32[384,512]{1,0:...) custom-call(s32[4]{0:T(128)S(1)} %pad_add_fusion.idx_ref, ...), custom_call_target="tpu_custom_call" | custom-call | flops 1000 | bytes 1000 | tf_op jit(solution)/shard_map/forward/pallas_call | solution.py:234
  11.6 10.6 %all_to_all.30.refs_0_ = f32[8,2,512]{2,1,0:T(2,128)S(1)} all-to-all(f32[8,2,512]{2,1,0:T(2,128)} %get-tuple-element.90), channel_id=1, replica_groups=mesh['z'=4,'x'=4,'y'=4,'core'=2] {'y','core'}, dimensions={0} | all-to-all | bytes 65536 | tf_op jit(solution)/shard_map/all_to_all | solution.py:938
  22.2 4.9 %middle.1 = (bf16[16,192,384]{2,1,0:T(8,128)(2,1)}, bf16[512,384]{1,0:T(8,128)(2,1)}, bf16[512,384]{1,0:T(8,128)(2,1)}, bf16[384,512]{1,0:T(8,128)(2,1)}, f32[384,8]{1,0:T(8,128)}) custom-call(s32[4]{0:T(128)S(1)} %pad_add_fusion.idx_ref, f32[8,2,512]{2,1,0:T(2,128)S(1)} %all_to_all.30.refs_0_, f32[384,512]{1,0:T(8,128)S(1)} %get-tuple-element.91.refs_1_, ...), custom_call_target="tpu_custom_call" | custom-call | flops 1000 | bytes 1000 | tf_op jit(solution)/shard_map/middle/pallas_call | solution.py:234
  27.2 7.6 %all-to-all-start.2 = ((bf16[16,192,384]{2,1,0:T(8,128)(2,1)}), bf16[16,192,384]{2,1,0:T(8,128)(2,1)S(1)}, u32[]{:S(2)}, u32[]{:S(2)}) async-start(bf16[16,192,384]{2,1,0:T(8,128)(2,1)} %get-tuple-element.123), calls=%async_computation.2 | async-start | bytes 4718592 | tf_op jit(solution)/shard_map/all_to_all | solution.py:913
  34.8 13.4 %backward.1 = (bf16[16,112,384]{2,1,0:T(8,128)(2,1)}, bf16[4,128,1536]{2,1,0:T(8,128)(2,1)S(1)}, bf16[4,48,1536]{2,1,0:T(8,128)(2,1)S(1)}, f32[16,1536]{1,0:T(8,...) custom-call(s32[4]{0:T(128)S(1)} %pad_add_fusion.idx_ref, ...), custom_call_target="tpu_custom_call" | custom-call | flops 1000 | bytes 1000 | tf_op jit(solution)/shard_map/backward/pallas_call | solution.py:234
  62.0 3.1 %pack.1 = bf16[16,112,384]{2,1,0:T(8,128)(2,1)} custom-call(s32[4]{0:T(128)S(1)} %pad_add_fusion.idx_ref, bf16[16,112,384]{2,1,0:T(8,128)(2,1)} %get-tuple-element.117.refs_0_, f32[48,1536]{1,0:T(8,128)} %get-tuple-element.105.refs_1_, bf16[48,1536]{1,0:T(8,128)(2,1)S(1)} %collective-permute-done.11.refs_2_, ...), custom_call_target="tpu_custom_call", output_to_operand_aliasing={{}: (1, {})} | custom-call | flops 1000 | bytes 1000 | tf_op jit(solution)/shard_map/pack/pallas_call | solution.py:234
  65.1 2.8 %all-to-all-done.2.refs_0_ = bf16[16,192,384]{2,1,0:T(8,128)(2,1)S(1)} async-done(((bf16[16,192,384]{2,1,0:T(8,128)(2,1)}), bf16[16,192,384]{2,1,0:T(8,128)(2,1)S(1)}, u32[]{:S(2)}, u32[]{:S(2)}) %all-to-all-start.2) | async-done | bytes 2359328 | tf_op jit(solution)/shard_map/all_to_all | solution.py:913
  67.9 5.1 %all-to-all-start.1 = ((bf16[16,112,384]{2,1,0:T(8,128)(2,1)}), bf16[16,112,384]{2,1,0:T(8,128)(2,1)}, u32[]{:S(2)}, u32[]{:S(2)}) async-start(bf16[16,112,384]{2,1,0:T(8,128)(2,1)} %pack.1), calls=%async_computation.1 | async-start | bytes 2752512 | tf_op jit(solution)/shard_map/all_to_all | solution.py:913
  73.0 5.0 %collective-permute-done.6.refs_5_ = bf16[128,1536]{1,0:T(8,128)(2,1)S(1)} collective-permute-done((bf16[128,1536]{1,0:T(8,128)(2,1)}, bf16[128,1536]{1,0:T(8,128)(2,1)S(1)}, u32[]{:S(2)}, u32[]{:S(2)}) %collective-permute-start.6) | collective-permute-done | bytes 393248 | tf_op jit(solution)/shard_map/ppermute | solution.py:645
  79.9 3.6 %input_part.1 = (bf16[128,1536]{1,0:T(8,128)(2,1)S(1)}, bf16[16,384]{1,0:T(8,128)(2,1)}) custom-call(s32[4]{0:T(128)S(1)} %pad_add_fusion.idx_ref, bf16[64,1536]{1,0:T(8,128)(2,1)} %get-tuple-element.84.refs_0_, bf16[64,1536]{1,0:T(8,128)(2,1)} %get-tuple-element.85.refs_1_, f32[1536]{0:T(1024)} %refs_2_.3, f32[128,1536]{1,0:T(8,128)} %get-tuple-element.112.refs_3_, ...), custom_call_target="tpu_custom_call" | custom-call | flops 10000001024 | bytes 1000 | tf_op jit(solution)/shard_map/input_part/pallas_call | solution.py:234
  83.5 3.4 %collective-permute-start.10 = (bf16[128,1536]{1,0:T(8,128)(2,1)S(1)}, bf16[128,1536]{1,0:T(8,128)(2,1)S(1)}, u32[]{:S(2)}, u32[]{:S(2)}) collective-permute-start(bf16[128,1536]{1,0:T(8,128)(2,1)S(1)} %get-tuple-element.128.refs_0_), channel_id=1, source_target_pairs={{0,6},{2,0},{4,2},{6,4},{1,7},{3,1},{5,3},{7,5},{8,14},{10,8},{12,... | collective-permute-start | bytes 1179656 | tf_op jit(solution)/shard_map/ppermute | solution.py:645
  90.0 3.1 %spread.1 = (bf16[16,32,384]{2,1,0:T(8,128)(2,1)}, bf16[4,288,384]{2,1,0:T(8,128)(2,1)}) custom-call(s32[4]{0:T(128)S(1)} %pad_add_fusion.idx_ref, bf16[16,112,384]{2,1,0:T(8,128)(2,1)} %all-to-all-done.1.terms_any, bf16[192,384]{1,0:T(8,128)(2,1)} %reduce.1.first_any, bf16[16,384]{1,0:T(8,128)(2,1)} %get-tuple-element.124.norm_any), custom_call_target="tpu_custom_call" | custom-call | flops 1000 | bytes 1000 | tf_op jit(solution)/shard_map/spread/pallas_call | solution.py:234
  93.1 6.3 %all-to-all-start.3 = ((bf16[16,32,384]{2,1,0:T(8,128)(2,1)}), bf16[16,32,384]{2,1,0:T(8,128)(2,1)S(1)}, u32[]{:S(2)}, u32[]{:S(2)}) async-start(bf16[16,32,384]{2,1,0:T(8,128)(2,1)} %get-tuple-element.126), calls=%async_computation.3 | async-start | bytes 786432 | tf_op jit(solution)/shard_map/all_to_all | solution.py:913
  99.3 3.7 %collective-permute-done.10.refs_3_ = bf16[128,1536]{1,0:T(8,128)(2,1)S(1)} collective-permute-done((bf16[128,1536]{1,0:T(8,128)(2,1)S(1)}, bf16[128,1536]{1,0:T(8,128)(2,1)S(1)}, u32[]{:S(2)}, u32[]{:S(2)}) %collective-permute-start.10) | collective-permute-done | bytes 393248 | tf_op jit(solution)/shard_map/ppermute | solution.py:645
  103.0 4.3 %collective-permute-done.8.refs_1_ = bf16[128,1536]{1,0:T(8,128)(2,1)} collective-permute-done((bf16[128,1536]{1,0:T(8,128)(2,1)S(1)}, bf16[128,1536]{1,0:T(8,128)(2,1)}, u32[]{:S(2)}, u32[]{:S(2)}) %collective-permute-start.8) | collective-permute-done | bytes 393248 | tf_op jit(solution)/shard_map/ppermute | solution.py:645
  107.6 4.1 %all-to-all-start.4 = ((bf16[4,288,384]{2,1,0:T(8,128)(2,1)}), bf16[4,288,384]{2,1,0:T(8,128)(2,1)S(1)}, u32[]{:S(2)}, u32[]{:S(2)}) async-start(bf16[4,288,384]{2,1,0:T(8,128)(2,1)} %get-tuple-element.127), calls=%async_computation.4 | async-start | bytes 1769472 | tf_op jit(solution)/shard_map/all_to_all | solution.py:913
  114.7 5.9 %all-to-all-done.4.blocks_any = bf16[4,288,384]{2,1,0:T(8,128)(2,1)S(1)} async-done(((bf16[4,288,384]{2,1,0:T(8,128)(2,1)}), bf16[4,288,384]{2,1,0:T(8,128)(2,1)S(1)}, u32[]{:S(2)}, u32[]{:S(2)}) %all-to-all-start.4) | async-done | bytes 884768 | tf_op jit(solution)/shard_map/all_to_all | solution.py:913
  123.1 4.0 %all-to-all-start.5 = ((bf16[4,4,288,384]{3,2,1,0:T(8,128)(2,1)}), bf16[4,4,288,384]{3,2,1,0:T(8,128)(2,1)S(1)}, u32[]{:S(2)}, u32[]{:S(2)}) async-start(bf16[4,4,288,384]{3,2,1,0:T(8,128)(2,1)} %again.1), calls=%async_computation.5 | async-start | bytes 7077888 | tf_op jit(solution)/shard_map/all_to_all | solution.py:913
  131.1 4.4 %collective-permute-start.21 = (bf16[16,16,384]{2,1,0:T(8,128)(2,1)}, bf16[16,16,384]{2,1,0:T(8,128)(2,1)S(1)}, u32[]{:S(2)}, u32[]{:S(2)}) collective-permute-start(bf16[16,16,384]{2,1,0:T(8,128)(2,1)} %share.1.refs_0_), channel_id=1, source_target_pairs={{0,1},{1,0},{2,3},{3,2},{4,5},{5,4},{6,7},{7,6},{8,9},{9,8},{10,11... | collective-permute-start | bytes 589832 | tf_op jit(solution)/shard_map/ppermute | solution.py:641
  135.5 3.4 %collective-permute-start.23 = (bf16[16,16,384]{2,1,0:T(8,128)(2,1)S(1)}, bf16[16,16,384]{2,1,0:T(8,128)(2,1)S(1)}, u32[]{:S(2)}, u32[]{:S(2)}) collective-permute-start(bf16[16,16,384]{2,1,0:T(8,128)(2,1)S(1)} %collective-permute-done.19.refs_2_), channel_id=1, source_target_pairs={{0,1},{1,0},{2,3},{3,2},{4,5},{5,4},{6,7},{7,6},{8,9},{9,8},{10,11... | collective-permute-start | bytes 589832 | tf_op jit(solution)/shard_map/ppermute | solution.py:641
  139.0 3.3 %collective-permute-start.15 = (bf16[128,1536]{1,0:T(8,128)(2,1)}, bf16[128,1536]{1,0:T(8,128)(2,1)S(1)}, u32[]{:S(2)}, u32[]{:S(2)}) collective-permute-start(bf16[128,1536]{1,0:T(8,128)(2,1)} %collective-permute-done.8.refs_1_), channel_id=1, source_target_pairs={{0,1},{1,0},{2,3},{3,2},{4,5},{5,4},{6,7},{7,6},{8,9},{9,8},{10,11... | collective-permute-start | bytes 1179656 | tf_op jit(solution)/shard_map/ppermute | solution.py:641
  144.8 4.2 %ends.1 = (f32[1536,256]{1,0:T(8,128)}, f32[1536]{0:T(1024)}, f32[4,256]{1,0:T(4,128)}, f32[256]{0:T(256)}, f32[6,1536]{1,0:T(8,128)}, /*index=5*/f32[4,384]{1,0...) custom-call(s32[4]{0:T(128)S(1)} %pad_add_fusion.idx_ref, ...), custom_call_target="tpu_custom_call" | custom-call | flops 1000 | bytes 1000 | tf_op jit(solution)/shard_map/ends/pallas_call | solution.py:234
  149.0 4.2 %finish.1 = (bf16[512,1536]{1,0:T(8,128)(2,1)}, f32[512,1536]{1,0:T(8,128)}) custom-call(s32[4]{0:T(128)S(1)} %pad_add_fusion.idx_ref, bf16[128,1536]{1,0:T(8,128)(2,1)S(1)} %copy-done.1, bf16[128,1536]{1,0:T(8,128)(2,1)} %collective-permute-done.8.refs_1_, bf16[128,1536]{1,0:T(8,128)(2,1)S(1)} %copy-done.5, bf16[128,1536]{1,0:T(8,128)(2,1)S(1)} %copy-done.3, ...), custom_call_target="tpu_custom_call" | custom-call | flops 20000000000 | bytes 1000 | tf_op jit(solution)/shard_map/finish/pallas_call | solution.py:234
  153.3 4.3 %widen.1 = (f32[4,4,96,384]{3,2,1,0:T(8,128)}, f32[384,1536]{1,0:T(8,128)}, f32[4,4,96,384]{3,2,1,0:T(8,128)}) custom-call(s32[4]{0:T(128)S(1)} %pad_add_fusion.idx_ref, bf16[4,4,288,384]{3,2,1,0:T(8,128)(2,1)S(1)} %all-to-all-done.5.hbm), custom_call_target="tpu_custom_call" | custom-call | flops 1000 | bytes 1000 | tf_op jit(solution)/shard_map/widen/pallas_call | solution.py:234
  (68 shorter events, 31.1 us)
Async XLA Ops:
  27.2 40.7 %all-to-all-start.2 = ((bf16[16,192,384]{2,1,0:T(8,128)(2,1)}), bf16[16,192,384]{2,1,0:T(8,128)(2,1)S(1)}, u32[]{:S(2)}, u32[]{:S(2)}) async-start(bf16[16,192,384]{2,1,0:T(8,128)(2,1)} %get-tuple-element.123), calls=%async_computation.2 | async-start | bytes 4718592 | tf_op jit(solution)/shard_map/all_to_all | solution.py:913
  52.2 7.7 %collective-permute-start.11 = (bf16[48,1536]{1,0:T(8,128)(2,1)S(1)}, bf16[48,1536]{1,0:T(8,128)(2,1)S(1)}, u32[]{:S(2)}, u32[]{:S(2)}) collective-permute-start(bf16[48,1536]{1,0:T(8,128)(2,1)S(1)} %get-tuple-element.118), channel_id=1, source_target_pairs={{0,2},{2,4},{4,6},{6,0},{1,3},{3,5},{5,7},{7,1},{8,10},{10,12},{12... | collective-permute-start | bytes 442376 | tf_op jit(solution)/shard_map/ppermute | solution.py:645
  52.6 9.3 %collective-permute-start.12 = (bf16[48,1536]{1,0:T(8,128)(2,1)S(1)}, bf16[48,1536]{1,0:T(8,128)(2,1)S(1)}, u32[]{:S(2)}, u32[]{:S(2)}) collective-permute-start(bf16[48,1536]{1,0:T(8,128)(2,1)S(1)} %get-tuple-element.119), channel_id=1, source_target_pairs={{0,4},{2,6},{4,0},{6,2},{1,5},{3,7},{5,1},{7,3},{8,12},{10,14},{12... | collective-permute-start | bytes 442376 | tf_op jit(solution)/shard_map/ppermute | solution.py:645
  54.3 7.7 %collective-permute-start.13 = (bf16[48,1536]{1,0:T(8,128)(2,1)S(1)}, bf16[48,1536]{1,0:T(8,128)(2,1)S(1)}, u32[]{:S(2)}, u32[]{:S(2)}) collective-permute-start(bf16[48,1536]{1,0:T(8,128)(2,1)S(1)} %get-tuple-element.120), channel_id=1, source_target_pairs={{0,6},{2,0},{4,2},{6,4},{1,7},{3,1},{5,3},{7,5},{8,14},{10,8},{12,... | collective-permute-start | bytes 442376 | tf_op jit(solution)/shard_map/ppermute | solution.py:645
  57.7 15.3 %collective-permute-start.5 = (bf16[128,1536]{1,0:T(8,128)(2,1)}, bf16[128,1536]{1,0:T(8,128)(2,1)S(1)}, u32[]{:S(2)}, u32[]{:S(2)}) collective-permute-start(bf16[128,1536]{1,0:T(8,128)(2,1)} %get-tuple-element.113), channel_id=1, source_target_pairs={{0,2},{2,4},{4,6},{6,0},{1,3},{3,5},{5,7},{7,1},{8,10},{10,12},{12... | collective-permute-start | bytes 1179656 | tf_op jit(solution)/shard_map/ppermute | solution.py:645
  58.3 19.8 %collective-permute-start.6 = (bf16[128,1536]{1,0:T(8,128)(2,1)}, bf16[128,1536]{1,0:T(8,128)(2,1)S(1)}, u32[]{:S(2)}, u32[]{:S(2)}) collective-permute-start(bf16[128,1536]{1,0:T(8,128)(2,1)} %get-tuple-element.114), channel_id=1, source_target_pairs={{0,4},{2,6},{4,0},{6,2},{1,5},{3,7},{5,1},{7,3},{8,12},{10,14},{12... | collective-permute-start | bytes 1179656 | tf_op jit(solution)/shard_map/ppermute | solution.py:645
  59.9 19.0 %collective-permute-start.7 = (bf16[128,1536]{1,0:T(8,128)(2,1)S(1)}, bf16[128,1536]{1,0:T(8,128)(2,1)}, u32[]{:S(2)}, u32[]{:S(2)}) collective-permute-start(bf16[128,1536]{1,0:T(8,128)(2,1)S(1)} %get-tuple-element.115), channel_id=1, source_target_pairs={{0,6},{2,0},{4,2},{6,4},{1,7},{3,1},{5,3},{7,5},{8,14},{10,8},{12,... | collective-permute-start | bytes 1179656 | tf_op jit(solution)/shard_map/ppermute | solution.py:645
  67.9 22.1 %all-to-all-start.1 = ((bf16[16,112,384]{2,1,0:T(8,128)(2,1)}), bf16[16,112,384]{2,1,0:T(8,128)(2,1)}, u32[]{:S(2)}, u32[]{:S(2)}) async-start(bf16[16,112,384]{2,1,0:T(8,128)(2,1)} %pack.1), calls=%async_computation.1 | async-start | bytes 2752512 | tf_op jit(solution)/shard_map/all_to_all | solution.py:913
  83.5 19.5 %collective-permute-start.10 = (bf16[128,1536]{1,0:T(8,128)(2,1)S(1)}, bf16[128,1536]{1,0:T(8,128)(2,1)S(1)}, u32[]{:S(2)}, u32[]{:S(2)}) collective-permute-start(bf16[128,1536]{1,0:T(8,128)(2,1)S(1)} %get-tuple-element.128.refs_0_), channel_id=1, source_target_pairs={{0,6},{2,0},{4,2},{6,4},{1,7},{3,1},{5,3},{7,5},{8,14},{10,8},{12,... | collective-permute-start | bytes 1179656 | tf_op jit(solution)/shard_map/ppermute | solution.py:645
  86.9 16.2 %collective-permute-start.9 = (bf16[128,1536]{1,0:T(8,128)(2,1)S(1)}, bf16[128,1536]{1,0:T(8,128)(2,1)S(1)}, u32[]{:S(2)}, u32[]{:S(2)}) collective-permute-start(bf16[128,1536]{1,0:T(8,128)(2,1)S(1)} %get-tuple-element.128.refs_0_), channel_id=1, source_target_pairs={{0,4},{2,6},{4,0},{6,2},{1,5},{3,7},{5,1},{7,3},{8,12},{10,14},{12... | collective-permute-start | bytes 1179656 | tf_op jit(solution)/shard_map/ppermute | solution.py:645
  86.9 20.4 %collective-permute-start.8 = (bf16[128,1536]{1,0:T(8,128)(2,1)S(1)}, bf16[128,1536]{1,0:T(8,128)(2,1)}, u32[]{:S(2)}, u32[]{:S(2)}) collective-permute-start(bf16[128,1536]{1,0:T(8,128)(2,1)S(1)} %get-tuple-element.128.refs_0_), channel_id=1, source_target_pairs={{0,2},{2,4},{4,6},{6,0},{1,3},{3,5},{5,7},{7,1},{8,10},{10,12},{12... | collective-permute-start | bytes 1179656 | tf_op jit(solution)/shard_map/ppermute | solution.py:645
  93.1 14.5 %all-to-all-start.3 = ((bf16[16,32,384]{2,1,0:T(8,128)(2,1)}), bf16[16,32,384]{2,1,0:T(8,128)(2,1)S(1)}, u32[]{:S(2)}, u32[]{:S(2)}) async-start(bf16[16,32,384]{2,1,0:T(8,128)(2,1)} %get-tuple-element.126), calls=%async_computation.3 | async-start | bytes 786432 | tf_op jit(solution)/shard_map/all_to_all | solution.py:913
  107.6 13.0 %all-to-all-start.4 = ((bf16[4,288,384]{2,1,0:T(8,128)(2,1)}), bf16[4,288,384]{2,1,0:T(8,128)(2,1)S(1)}, u32[]{:S(2)}, u32[]{:S(2)}) async-start(bf16[4,288,384]{2,1,0:T(8,128)(2,1)} %get-tuple-element.127), calls=%async_computation.4 | async-start | bytes 1769472 | tf_op jit(solution)/shard_map/all_to_all | solution.py:913
  113.2 22.3 %collective-permute-start.18 = (bf16[16,16,384]{2,1,0:T(8,128)(2,1)}, bf16[16,16,384]{2,1,0:T(8,128)(2,1)}, u32[]{:S(2)}, u32[]{:S(2)}) collective-permute-start(bf16[16,16,384]{2,1,0:T(8,128)(2,1)} %share.1.refs_0_), channel_id=1, source_target_pairs={{0,2},{2,4},{4,6},{6,0},{1,3},{3,5},{5,7},{7,1},{8,10},{10,12},{12... | collective-permute-start | bytes 589832 | tf_op jit(solution)/shard_map/ppermute | solution.py:645
  123.1 30.1 %all-to-all-start.5 = ((bf16[4,4,288,384]{3,2,1,0:T(8,128)(2,1)}), bf16[4,4,288,384]{3,2,1,0:T(8,128)(2,1)S(1)}, u32[]{:S(2)}, u32[]{:S(2)}) async-start(bf16[4,4,288,384]{3,2,1,0:T(8,128)(2,1)} %again.1), calls=%async_computation.5 | async-start | bytes 7077888 | tf_op jit(solution)/shard_map/all_to_all | solution.py:913
  127.1 8.4 %collective-permute-start.19 = (bf16[16,16,384]{2,1,0:T(8,128)(2,1)}, bf16[16,16,384]{2,1,0:T(8,128)(2,1)S(1)}, u32[]{:S(2)}, u32[]{:S(2)}) collective-permute-start(bf16[16,16,384]{2,1,0:T(8,128)(2,1)} %share.1.refs_0_), channel_id=1, source_target_pairs={{0,4},{2,6},{4,0},{6,2},{1,5},{3,7},{5,1},{7,3},{8,12},{10,14},{12... | collective-permute-start | bytes 589832 | tf_op jit(solution)/shard_map/ppermute | solution.py:645
  128.7 10.3 %collective-permute-start.20 = (bf16[16,16,384]{2,1,0:T(8,128)(2,1)}, bf16[16,16,384]{2,1,0:T(8,128)(2,1)S(1)}, u32[]{:S(2)}, u32[]{:S(2)}) collective-permute-start(bf16[16,16,384]{2,1,0:T(8,128)(2,1)} %share.1.refs_0_), channel_id=1, source_target_pairs={{0,6},{2,0},{4,2},{6,4},{1,7},{3,1},{5,3},{7,5},{8,14},{10,8},{12,... | collective-permute-start | bytes 589832 | tf_op jit(solution)/shard_map/ppermute | solution.py:645
  131.1 11.2 %collective-permute-start.21 = (bf16[16,16,384]{2,1,0:T(8,128)(2,1)}, bf16[16,16,384]{2,1,0:T(8,128)(2,1)S(1)}, u32[]{:S(2)}, u32[]{:S(2)}) collective-permute-start(bf16[16,16,384]{2,1,0:T(8,128)(2,1)} %share.1.refs_0_), channel_id=1, source_target_pairs={{0,1},{1,0},{2,3},{3,2},{4,5},{5,4},{6,7},{7,6},{8,9},{9,8},{10,11... | collective-permute-start | bytes 589832 | tf_op jit(solution)/shard_map/ppermute | solution.py:641
  135.5 6.8 %collective-permute-start.22 = (bf16[16,16,384]{2,1,0:T(8,128)(2,1)}, bf16[16,16,384]{2,1,0:T(8,128)(2,1)S(1)}, u32[]{:S(2)}, u32[]{:S(2)}) collective-permute-start(bf16[16,16,384]{2,1,0:T(8,128)(2,1)} %collective-permute-done.18.refs_1_), channel_id=1, source_target_pairs={{0,1},{1,0},{2,3},{3,2},{4,5},{5,4},{6,7},{7,6},{8,9},{9,8},{10,11... | collective-permute-start | bytes 589832 | tf_op jit(solution)/shard_map/ppermute | solution.py:641
  135.5 7.3 %collective-permute-start.23 = (bf16[16,16,384]{2,1,0:T(8,128)(2,1)S(1)}, bf16[16,16,384]{2,1,0:T(8,128)(2,1)S(1)}, u32[]{:S(2)}, u32[]{:S(2)}) collective-permute-start(bf16[16,16,384]{2,1,0:T(8,128)(2,1)S(1)} %collective-permute-done.19.refs_2_), channel_id=1, source_target_pairs={{0,1},{1,0},{2,3},{3,2},{4,5},{5,4},{6,7},{7,6},{8,9},{9,8},{10,11... | collective-permute-start | bytes 589832 | tf_op jit(solution)/shard_map/ppermute | solution.py:641
  139.0 10.0 %collective-permute-start.14 = (bf16[128,1536]{1,0:T(8,128)(2,1)}, bf16[128,1536]{1,0:T(8,128)(2,1)S(1)}, u32[]{:S(2)}, u32[]{:S(2)}) collective-permute-start(bf16[128,1536]{1,0:T(8,128)(2,1)} %copy-done), channel_id=1, source_target_pairs={{0,1},{1,0},{2,3},{3,2},{4,5},{5,4},{6,7},{7,6},{8,9},{9,8},{10,11... | collective-permute-start | bytes 1179656 | tf_op jit(solution)/shard_map/ppermute | solution.py:641
  139.0 10.0 %collective-permute-start.15 = (bf16[128,1536]{1,0:T(8,128)(2,1)}, bf16[128,1536]{1,0:T(8,128)(2,1)S(1)}, u32[]{:S(2)}, u32[]{:S(2)}) collective-permute-start(bf16[128,1536]{1,0:T(8,128)(2,1)} %collective-permute-done.8.refs_1_), channel_id=1, source_target_pairs={{0,1},{1,0},{2,3},{3,2},{4,5},{5,4},{6,7},{7,6},{8,9},{9,8},{10,11... | collective-permute-start | bytes 1179656 | tf_op jit(solution)/shard_map/ppermute | solution.py:641
  142.3 6.7 %collective-permute-start.16 = (bf16[128,1536]{1,0:T(8,128)(2,1)}, bf16[128,1536]{1,0:T(8,128)(2,1)S(1)}, u32[]{:S(2)}, u32[]{:S(2)}) collective-permute-start(bf16[128,1536]{1,0:T(8,128)(2,1)} %copy-done.4), channel_id=1, source_target_pairs={{0,1},{1,0},{2,3},{3,2},{4,5},{5,4},{6,7},{7,6},{8,9},{9,8},{10,11... | collective-permute-start | bytes 1179656 | tf_op jit(solution)/shard_map/ppermute | solution.py:641
  142.3 6.7 %collective-permute-start.17 = (bf16[128,1536]{1,0:T(8,128)(2,1)}, bf16[128,1536]{1,0:T(8,128)(2,1)S(1)}, u32[]{:S(2)}, u32[]{:S(2)}) collective-permute-start(bf16[128,1536]{1,0:T(8,128)(2,1)} %copy-done.2), channel_id=1, source_target_pairs={{0,1},{1,0},{2,3},{3,2},{4,5},{5,4},{6,7},{7,6},{8,9},{9,8},{10,11... | collective-permute-start | bytes 1179656 | tf_op jit(solution)/shard_map/ppermute | solution.py:641
  (14 other events, 141.1 us)
